TPU v7x, 32 devices: a whole 2x2x4 slice. The times are simulated.
32 devices in a mesh: seg: 4 (over z), sec: 8 (over y, x, core).
Axes of the slice: x: 2, y: 2, z: 4, core: 2. Of those that a mesh axis runs over, the one named last changes fastest.
Arguments:
- boundary_env: bfloat16 [4, 8, 13, 256, 256], P('seg', 'sec'), may hold values from -6 to 6
- site_block_tensors: bfloat16 [8, 8, 4, 256, 256], P('seg', 'sec'), may hold values from -0.375 to 0.375
- mpo_tensors: bfloat16 [8, 4, 13, 13], P('seg'), may hold values from -1.75 to 1.75
- block_mask: int32 [8, 8, 4], P('seg', 'sec'), may hold values 0 or 1
- sector_dims: int32 [8], replicated, may hold values from 128 to 256, as said below
Outputs:
- handed_env: bfloat16 [4, 8, 13, 256, 256], P('seg', 'sec')
Inputs may be any that keep to these rules, and one draw needn't show every extreme that they name: `sector_dims`: each entry is 128 or 256, and both occur in every draw.
All inputs are finite; a program needn't handle non-finite values. No bound on the sum of `block_mask` on one device may be relied on, other than what follows from the above.
Results may differ from a plain program's by a relative error of at most 0.02.
Values may be sent and summed in bfloat16 or wider, within the bound.
No kernel may reach another device: no remote copies, remote signals or barrier semaphores. Data moves between devices by JAX's collectives and lax.ppermute only.
A program may use at most 64 MiB of HBM per device.

v0:
```python
import jax
import jax.numpy as jnp
from jax import lax
from jax.sharding import PartitionSpec as P

ND = 4


def from_behind(shard, axis, by):
    count = lax.axis_size(axis)
    pairs = [(i, i + by) for i in range(count) if 0 <= i + by < count]
    return lax.ppermute(shard, axis, pairs)


def contract(left_environ_tensor, block_list, weight_factors):
    merged_mixture = jnp.einsum(
        "umi,ue->emi", left_environ_tensor, weight_factors, preferred_element_type=jnp.float32
    ).astype(jnp.bfloat16)
    combined_mixture = jnp.einsum(
        "gip,pq->giq", merged_mixture, block_list, preferred_element_type=jnp.float32
    ).astype(jnp.bfloat16)
    return jnp.einsum(
        "ba,vbc->vac", block_list, combined_mixture, preferred_element_type=jnp.float32
    ).astype(jnp.bfloat16)


def body(boundary_env, site_block_tensors, mpo_tensors, block_mask, sector_dims):
    capacity = site_block_tensors.shape[-1]
    site_count = site_block_tensors.shape[0]
    sector_total = lax.axis_size("sec")
    sector_id = lax.axis_index("sec")
    offsets = jnp.array([0, ND, 1, ND + 1])
    down_step = jnp.array([0, 0, 1, 1])
    targets = sector_id + offsets
    allowed = (targets < sector_total) & ((down_step == 0) | (sector_id % ND < ND - 1))
    sectors = jnp.arange(sector_total)
    own_dims = jnp.sum(jnp.where(sectors == sector_id, sector_dims, 0))
    target_dims = jnp.sum(
        jnp.where(sectors[None, :] == targets[:, None], sector_dims[None, :], 0), axis=1
    )
    target_dims = jnp.where(allowed, target_dims, 0)
    line = jnp.arange(capacity)
    row_live = (line < own_dims).astype(jnp.int32)
    col_live = (line[None, :] < target_dims[:, None]).astype(jnp.int32)
    left_environ_tensor = (
        boundary_env[0, 0] * (row_live[:, None] * row_live[None, :]).astype(jnp.bfloat16)[None]
    )
    for site_pos in range(site_count):
        present = block_mask[site_pos, 0] * allowed.astype(jnp.int32)
        factor = present[:, None, None] * row_live[None, :, None] * col_live[:, None, :]
        block_list = site_block_tensors[site_pos, 0] * factor.astype(jnp.bfloat16)
        partials = []
        for carry_state in range(4):
            weight_factors = mpo_tensors[site_pos, carry_state]
            block = block_list[carry_state]
            result = contract(left_environ_tensor, block, weight_factors)
            partials.append(result)
        from_up = from_behind(partials[1], "sec", ND)
        from_down = from_behind(partials[2], "sec", 1)
        from_pair = from_behind(partials[3], "sec", ND + 1)
        total = partials[0].astype(jnp.float32) + from_up.astype(jnp.float32)
        total = total + from_down.astype(jnp.float32) + from_pair.astype(jnp.float32)
        left_environ_tensor = total.astype(jnp.bfloat16)
    handed = from_behind(left_environ_tensor, "seg", 1)
    return handed[None, None]


def solution(mesh):
    in_specs = (
        P("seg", "sec", None, None, None),
        P("seg", "sec", None, None, None),
        P("seg", None, None, None),
        P("seg", "sec", None),
        P(),
    )
    out_specs = P("seg", "sec", None, None, None)
    return jax.shard_map(body, mesh=mesh, in_specs=in_specs, out_specs=out_specs, check_vma=False)
```

profile of v0, /device:TPU:0, one launch (start us, length us, event | category | flops | bytes accessed | tf_op | source)
XLA Modules:
  0.0 218.2 jit_solution(10418955041243928973)
XLA Ops:
  7.0 2.5 %convert_bitcast_fusion.6 = bf16[13,256,256]{2,0,1:T(8,128)(2,1)} fusion(bf16[13,256,256]{2,1,0:T(8,128)(2,1)S(1)} %multiply_bitcast_fusion, bf16[1,1,13,13]{3,1,2,0:T(2,128)(2,1)S(1)} %get-tuple-element.14), kind=kOutput, calls=%fused_computation.14 | convolution fusion | flops 23003136 | bytes 3408210 | tf_op jit(solution)/shard_map/umi,ue->emi/dot_general | solution.py:16
  10.1 4.7 %fusion.30 = bf16[13,256,256]{1,2,0:T(8,128)(2,1)} fusion(bf16[13,256,256]{2,0,1:T(8,128)(2,1)} %convert_bitcast_fusion.6, bf16[4,256,256]{2,1,0:T(8,128)(2,1)S(1)} %get-tuple-element.8), kind=kOutput, calls=%fused_computation.49 | convolution fusion | flops 874119168 | bytes 3670016 | tf_op jit(solution)/shard_map/ba,vbc->vac/dot_general | solution.py:22
  14.8 6.1 %collective-permute-start = (bf16[13,256,256]{1,2,0:T(8,128)(2,1)}, bf16[13,256,256]{1,2,0:T(8,128)(2,1)}, u32[]{:S(2)}, u32[]{:S(2)}) collective-permute-start(bf16[13,256,256]{1,2,0:T(8,128)(2,1)} %fusion.30), channel_id=1, source_target_pairs={{0,4},{1,5},{2,6},{3,7},{8,12},{9,13},{10,14},{11,15},{16,20},{17,... | collective-permute-start | bytes 5111816 | tf_op jit(solution)/shard_map/ppermute | solution.py:12
  20.8 2.5 %convert_bitcast_fusion.5 = bf16[13,256,256]{2,0,1:T(8,128)(2,1)} fusion(bf16[13,256,256]{2,1,0:T(8,128)(2,1)S(1)} %multiply_bitcast_fusion, bf16[1,1,13,13]{3,1,2,0:T(2,128)(2,1)S(1)} %get-tuple-element.13), kind=kOutput, calls=%fused_computation.13 | convolution fusion | flops 23003136 | bytes 3408210 | tf_op jit(solution)/shard_map/umi,ue->emi/dot_general | solution.py:16
  23.4 4.7 %fusion.31 = bf16[13,256,256]{1,2,0:T(8,128)(2,1)} fusion(bf16[13,256,256]{2,0,1:T(8,128)(2,1)} %convert_bitcast_fusion.5, bf16[4,256,256]{2,1,0:T(8,128)(2,1)S(1)} %get-tuple-element.8), kind=kOutput, calls=%fused_computation.50 | convolution fusion | flops 874119168 | bytes 3670016 | tf_op jit(solution)/shard_map/ba,vbc->vac/dot_general | solution.py:22
  28.1 2.7 %collective-permute-start.1 = (bf16[13,256,256]{1,2,0:T(8,128)(2,1)}, bf16[13,256,256]{1,2,0:T(8,128)(2,1)}, u32[]{:S(2)}, u32[]{:S(2)}) collective-permute-start(bf16[13,256,256]{1,2,0:T(8,128)(2,1)} %fusion.31), channel_id=1, source_target_pairs={{0,1},{1,2},{2,3},{3,4},{4,5},{5,6},{6,7},{8,9},{9,10},{10,11},{11... | collective-permute-start | bytes 5111816 | tf_op jit(solution)/shard_map/ppermute | solution.py:12
  30.8 2.5 %convert_bitcast_fusion.4 = bf16[13,256,256]{2,0,1:T(8,128)(2,1)} fusion(bf16[13,256,256]{2,1,0:T(8,128)(2,1)S(1)} %multiply_bitcast_fusion, bf16[1,1,13,13]{3,1,2,0:T(2,128)(2,1)S(1)} %get-tuple-element.12), kind=kOutput, calls=%fused_computation.12 | convolution fusion | flops 23003136 | bytes 3408210 | tf_op jit(solution)/shard_map/umi,ue->emi/dot_general | solution.py:16
  33.4 4.7 %fusion.32 = bf16[13,256,256]{1,2,0:T(8,128)(2,1)} fusion(bf16[13,256,256]{2,0,1:T(8,128)(2,1)} %convert_bitcast_fusion.4, bf16[4,256,256]{2,1,0:T(8,128)(2,1)S(1)} %get-tuple-element.8), kind=kOutput, calls=%fused_computation.51 | convolution fusion | flops 874119168 | bytes 3670016 | tf_op jit(solution)/shard_map/ba,vbc->vac/dot_general | solution.py:22
  38.1 2.5 %collective-permute-start.2 = (bf16[13,256,256]{1,2,0:T(8,128)(2,1)}, bf16[13,256,256]{1,2,0:T(8,128)(2,1)}, u32[]{:S(2)}, u32[]{:S(2)}) collective-permute-start(bf16[13,256,256]{1,2,0:T(8,128)(2,1)} %fusion.32), channel_id=1, source_target_pairs={{0,5},{1,6},{2,7},{8,13},{9,14},{10,15},{16,21},{17,22},{18,23},{2... | collective-permute-start | bytes 5111816 | tf_op jit(solution)/shard_map/ppermute | solution.py:12
  40.6 2.5 %convert_bitcast_fusion.7 = bf16[13,256,256]{2,0,1:T(8,128)(2,1)} fusion(bf16[13,256,256]{2,1,0:T(8,128)(2,1)S(1)} %multiply_bitcast_fusion, bf16[1,1,13,13]{3,1,2,0:T(2,128)(2,1)S(1)} %get-tuple-element.15), kind=kOutput, calls=%fused_computation.15 | convolution fusion | flops 23003136 | bytes 3408210 | tf_op jit(solution)/shard_map/umi,ue->emi/dot_general | solution.py:16
  43.1 31.5 %collective-permute-done = bf16[13,256,256]{1,2,0:T(8,128)(2,1)} collective-permute-done((bf16[13,256,256]{1,2,0:T(8,128)(2,1)}, bf16[13,256,256]{1,2,0:T(8,128)(2,1)}, u32[]{:S(2)}, u32[]{:S(2)}) %collective-permute-start) | collective-permute-done | bytes 1703968 | tf_op jit(solution)/shard_map/ppermute | solution.py:12
  74.6 18.3 %collective-permute-done.2 = bf16[13,256,256]{1,2,0:T(8,128)(2,1)} collective-permute-done((bf16[13,256,256]{1,2,0:T(8,128)(2,1)}, bf16[13,256,256]{1,2,0:T(8,128)(2,1)}, u32[]{:S(2)}, u32[]{:S(2)}) %collective-permute-start.2) | collective-permute-done | bytes 1703968 | tf_op jit(solution)/shard_map/ppermute | solution.py:12
  92.9 6.2 %fusion.5 = bf16[13,256,256]{1,2,0:T(8,128)(2,1)} fusion(bf16[13,256,256]{1,2,0:T(8,128)(2,1)} %collective-permute-done.2, bf16[13,256,256]{1,2,0:T(8,128)(2,1)} %collective-permute-done.1, bf16[13,256,256]{1,2,0:T(8,128)(2,1)} %collective-permute-done, bf16[13,256,256]{2,0,1:T(8,128)(2,1)} %convert_bitcast_fusion.7, ...), kind=kOutput, calls=%fused_computation.7 | convolution fusion | flops 880934912 | bytes 8781824 | tf_op jit(solution)/shard_map/ba,vbc->vac/dot_general | solution.py:22
  99.1 3.5 %copy.39 = bf16[13,256,256]{2,0,1:T(8,128)(2,1)S(1)} copy(bf16[13,256,256]{1,2,0:T(8,128)(2,1)} %fusion.5) | data formatting | bytes 3407872 | tf_op jit(solution)/shard_map/convert_element_type | solution.py:63
  104.8 4.7 %fusion.33 = bf16[13,256,256]{1,2,0:T(8,128)(2,1)} fusion(bf16[13,256,256]{2,0,1:T(8,128)(2,1)} %convert_bitcast_fusion.2, bf16[4,256,256]{2,1,0:T(8,128)(2,1)S(1)} %get-tuple-element.7), kind=kOutput, calls=%fused_computation.52 | convolution fusion | flops 874119168 | bytes 3670016 | tf_op jit(solution)/shard_map/ba,vbc->vac/dot_general | solution.py:22
  109.5 2.5 %collective-permute-start.3 = (bf16[13,256,256]{1,2,0:T(8,128)(2,1)}, bf16[13,256,256]{1,2,0:T(8,128)(2,1)}, u32[]{:S(2)}, u32[]{:S(2)}) collective-permute-start(bf16[13,256,256]{1,2,0:T(8,128)(2,1)} %fusion.33), channel_id=1, source_target_pairs={{0,4},{1,5},{2,6},{3,7},{8,12},{9,13},{10,14},{11,15},{16,20},{17,... | collective-permute-start | bytes 5111816 | tf_op jit(solution)/shard_map/ppermute | solution.py:12
  114.1 4.7 %fusion.34 = bf16[13,256,256]{1,2,0:T(8,128)(2,1)} fusion(bf16[13,256,256]{2,0,1:T(8,128)(2,1)} %convert_bitcast_fusion.1, bf16[4,256,256]{2,1,0:T(8,128)(2,1)S(1)} %get-tuple-element.7), kind=kOutput, calls=%fused_computation.53 | convolution fusion | flops 874119168 | bytes 3670016 | tf_op jit(solution)/shard_map/ba,vbc->vac/dot_general | solution.py:22
  118.8 5.8 %collective-permute-start.4 = (bf16[13,256,256]{1,2,0:T(8,128)(2,1)}, bf16[13,256,256]{1,2,0:T(8,128)(2,1)}, u32[]{:S(2)}, u32[]{:S(2)}) collective-permute-start(bf16[13,256,256]{1,2,0:T(8,128)(2,1)} %fusion.34), channel_id=1, source_target_pairs={{0,1},{1,2},{2,3},{3,4},{4,5},{5,6},{6,7},{8,9},{9,10},{10,11},{11... | collective-permute-start | bytes 5111816 | tf_op jit(solution)/shard_map/ppermute | solution.py:12
  126.7 4.7 %fusion.35 = bf16[13,256,256]{1,2,0:T(8,128)(2,1)} fusion(bf16[13,256,256]{2,0,1:T(8,128)(2,1)} %convert_bitcast_fusion, bf16[4,256,256]{2,1,0:T(8,128)(2,1)S(1)} %get-tuple-element.7), kind=kOutput, calls=%fused_computation.54 | convolution fusion | flops 874119168 | bytes 3670016 | tf_op jit(solution)/shard_map/ba,vbc->vac/dot_general | solution.py:22
  136.0 28.9 %collective-permute-done.3 = bf16[13,256,256]{1,2,0:T(8,128)(2,1)} collective-permute-done((bf16[13,256,256]{1,2,0:T(8,128)(2,1)}, bf16[13,256,256]{1,2,0:T(8,128)(2,1)}, u32[]{:S(2)}, u32[]{:S(2)}) %collective-permute-start.3) | collective-permute-done | bytes 1703968 | tf_op jit(solution)/shard_map/ppermute | solution.py:12
  164.9 20.3 %collective-permute-done.5 = bf16[13,256,256]{1,2,0:T(8,128)(2,1)} collective-permute-done((bf16[13,256,256]{1,2,0:T(8,128)(2,1)}, bf16[13,256,256]{1,2,0:T(8,128)(2,1)}, u32[]{:S(2)}, u32[]{:S(2)}) %collective-permute-start.5) | collective-permute-done | bytes 1703968 | tf_op jit(solution)/shard_map/ppermute | solution.py:12
  185.2 6.2 %fusion.2 = bf16[13,256,256]{1,2,0:T(8,128)(2,1)} fusion(bf16[13,256,256]{1,2,0:T(8,128)(2,1)} %collective-permute-done.5, bf16[13,256,256]{1,2,0:T(8,128)(2,1)} %collective-permute-done.4, bf16[13,256,256]{1,2,0:T(8,128)(2,1)} %collective-permute-done.3, bf16[13,256,256]{2,0,1:T(8,128)(2,1)} %convert_bitcast_fusion.3, ...), kind=kOutput, calls=%fused_computation.3 | convolution fusion | flops 880934912 | bytes 8781824 | tf_op jit(solution)/shard_map/ba,vbc->vac/dot_general | solution.py:22
  191.4 3.6 %collective-permute-start.6 = (bf16[13,256,256]{1,2,0:T(8,128)(2,1)}, bf16[13,256,256]{1,2,0:T(8,128)(2,1)S(1)}, u32[]{:S(2)}, u32[]{:S(2)}) collective-permute-start(bf16[13,256,256]{1,2,0:T(8,128)(2,1)} %fusion.2), channel_id=1, source_target_pairs={{0,8},{8,16},{16,24},{1,9},{9,17},{17,25},{2,10},{10,18},{18,26},{... | collective-permute-start | bytes 5111816 | tf_op jit(solution)/shard_map/ppermute | solution.py:12
  195.0 20.7 %collective-permute-done.6 = bf16[13,256,256]{1,2,0:T(8,128)(2,1)S(1)} collective-permute-done((bf16[13,256,256]{1,2,0:T(8,128)(2,1)}, bf16[13,256,256]{1,2,0:T(8,128)(2,1)S(1)}, u32[]{:S(2)}, u32[]{:S(2)}) %collective-permute-start.6) | collective-permute-done | bytes 1703968 | tf_op jit(solution)/shard_map/ppermute | solution.py:12
  (21 shorter events, 20.9 us)
Async XLA Ops:
  7.0 2.6 %copy-start = (bf16[2,1,4,256,256]{4,3,2,1,0:T(8,128)(2,1)S(1)}, bf16[2,1,4,256,256]{4,3,2,1,0:T(8,128)(2,1)}, u32[]{:S(2)}) copy-start(bf16[2,1,4,256,256]{4,3,2,1,0:T(8,128)(2,1)} %param.8) | copy-start | bytes 3145732
  14.8 59.9 %collective-permute-start = (bf16[13,256,256]{1,2,0:T(8,128)(2,1)}, bf16[13,256,256]{1,2,0:T(8,128)(2,1)}, u32[]{:S(2)}, u32[]{:S(2)}) collective-permute-start(bf16[13,256,256]{1,2,0:T(8,128)(2,1)} %fusion.30), channel_id=1, source_target_pairs={{0,4},{1,5},{2,6},{3,7},{8,12},{9,13},{10,14},{11,15},{16,20},{17,... | collective-permute-start | bytes 5111816 | tf_op jit(solution)/shard_map/ppermute | solution.py:12
  28.1 46.5 %collective-permute-start.1 = (bf16[13,256,256]{1,2,0:T(8,128)(2,1)}, bf16[13,256,256]{1,2,0:T(8,128)(2,1)}, u32[]{:S(2)}, u32[]{:S(2)}) collective-permute-start(bf16[13,256,256]{1,2,0:T(8,128)(2,1)} %fusion.31), channel_id=1, source_target_pairs={{0,1},{1,2},{2,3},{3,4},{4,5},{5,6},{6,7},{8,9},{9,10},{10,11},{11... | collective-permute-start | bytes 5111816 | tf_op jit(solution)/shard_map/ppermute | solution.py:12
  38.1 54.8 %collective-permute-start.2 = (bf16[13,256,256]{1,2,0:T(8,128)(2,1)}, bf16[13,256,256]{1,2,0:T(8,128)(2,1)}, u32[]{:S(2)}, u32[]{:S(2)}) collective-permute-start(bf16[13,256,256]{1,2,0:T(8,128)(2,1)} %fusion.32), channel_id=1, source_target_pairs={{0,5},{1,6},{2,7},{8,13},{9,14},{10,15},{16,21},{17,22},{18,23},{2... | collective-permute-start | bytes 5111816 | tf_op jit(solution)/shard_map/ppermute | solution.py:12
  109.5 55.4 %collective-permute-start.3 = (bf16[13,256,256]{1,2,0:T(8,128)(2,1)}, bf16[13,256,256]{1,2,0:T(8,128)(2,1)}, u32[]{:S(2)}, u32[]{:S(2)}) collective-permute-start(bf16[13,256,256]{1,2,0:T(8,128)(2,1)} %fusion.33), channel_id=1, source_target_pairs={{0,4},{1,5},{2,6},{3,7},{8,12},{9,13},{10,14},{11,15},{16,20},{17,... | collective-permute-start | bytes 5111816 | tf_op jit(solution)/shard_map/ppermute | solution.py:12
  118.8 46.1 %collective-permute-start.4 = (bf16[13,256,256]{1,2,0:T(8,128)(2,1)}, bf16[13,256,256]{1,2,0:T(8,128)(2,1)}, u32[]{:S(2)}, u32[]{:S(2)}) collective-permute-start(bf16[13,256,256]{1,2,0:T(8,128)(2,1)} %fusion.34), channel_id=1, source_target_pairs={{0,1},{1,2},{2,3},{3,4},{4,5},{5,6},{6,7},{8,9},{9,10},{10,11},{11... | collective-permute-start | bytes 5111816 | tf_op jit(solution)/shard_map/ppermute | solution.py:12
  131.4 53.8 %collective-permute-start.5 = (bf16[13,256,256]{1,2,0:T(8,128)(2,1)}, bf16[13,256,256]{1,2,0:T(8,128)(2,1)}, u32[]{:S(2)}, u32[]{:S(2)}) collective-permute-start(bf16[13,256,256]{1,2,0:T(8,128)(2,1)} %fusion.35), channel_id=1, source_target_pairs={{0,5},{1,6},{2,7},{8,13},{9,14},{10,15},{16,21},{17,22},{18,23},{2... | collective-permute-start | bytes 5111816 | tf_op jit(solution)/shard_map/ppermute | solution.py:12
  191.4 24.3 %collective-permute-start.6 = (bf16[13,256,256]{1,2,0:T(8,128)(2,1)}, bf16[13,256,256]{1,2,0:T(8,128)(2,1)S(1)}, u32[]{:S(2)}, u32[]{:S(2)}) collective-permute-start(bf16[13,256,256]{1,2,0:T(8,128)(2,1)} %fusion.2), channel_id=1, source_target_pairs={{0,8},{8,16},{16,24},{1,9},{9,17},{17,25},{2,10},{10,18},{18,26},{... | collective-permute-start | bytes 5111816 | tf_op jit(solution)/shard_map/ppermute | solution.py:12
where the time goes:
time: 219 us; the launch traced here: 218 us
  waiting for transfers between devices  120 us (55%)
  matrix products  59.2 us (27%)
  starting transfers between devices  25.7 us (12%)
  local copies, waits for them, and re-layouts  6.99 us (3%)
  other arithmetic  6.52 us (3%)
    ppermute x7, waiting for transfers between devices, from_behind(): return lax.ppermute(shard, axis, pairs)  120 us
    dot_general x8, matrix products, contract(): jnp.einsum('ba,vbc->vac', block_list, combined_mixture, preferred_element...  40.6 us
    ppermute x7, starting transfers between devices, from_behind(): return lax.ppermute(shard, axis, pairs)  25.7 us
    dot_general x8, matrix products, contract(): jnp.einsum('umi,ue->emi', left_environ_tensor, weight_factors, preferred_...  18.6 us
  transfers between devices with their start and end apart: 7, of which 5 were waited for; matrix products, arithmetic and copies ran while one was open for 15% of the time, Pallas kernels for 0%

commit v1 on v0

v1 whole, which is shorter than its diff:
```python
import jax
import jax.numpy as jnp
from jax import lax
from jax.experimental import pallas as pl
from jax.experimental.pallas import tpu as pltpu
from jax.sharding import PartitionSpec as P

ND = 4
ROWS = 16
VMEM_BYTES = 56 * 2**20


def from_behind(shard, axis, by):
    count = lax.axis_size(axis)
    pairs = [(i, i + by) for i in range(count) if 0 <= i + by < count]
    return lax.ppermute(shard, axis, pairs)


def shift_column(shard):
    count = lax.axis_size("sec")
    return lax.ppermute(shard, "sec", [(q, q + 1) for q in range(count - 1) if q % ND < ND - 1])


def widen(weights):
    eye = jnp.eye(ROWS, dtype=weights.dtype)
    return weights.transpose(0, 2, 1)[:, :, None, :, None] * eye[None, None, :, None, :]


def product_kernel(plan, out_sizes, sources, *refs):
    env_refs = refs[:sources]
    mix_refs = refs[sources:2 * sources]
    block_ref = refs[2 * sources]
    out_refs = refs[2 * sources + 1:2 * sources + 1 + len(out_sizes)]
    scratch = refs[2 * sources + 1 + len(out_sizes):]
    mixed_refs, flipped_ref = scratch[:-1], scratch[-1]
    channels, cap, _ = env_refs[0].shape
    for k in range(block_ref.shape[0]):
        flipped_ref[k] = block_ref[k].T
    for env_ref, mix_ref, mixed_ref in zip(env_refs, mix_refs, mixed_refs):
        count = mixed_ref.shape[0]

        def mix(g, _):
            rows = pl.ds(pl.multiple_of(g * ROWS, ROWS), ROWS)
            piece = env_ref[:, rows, :].reshape(channels * ROWS, cap)
            mixed = jnp.dot(mix_ref[...], piece, preferred_element_type=jnp.float32)
            mixed_ref[:, rows, :] = mixed.astype(jnp.bfloat16).reshape(count, ROWS, cap)
            return 0

        lax.fori_loop(0, cap // ROWS, mix, 0, unroll=2)
    width = out_refs[0].shape[1]

    def channel(v, _):
        totals = {}
        for source, states in enumerate(plan):
            for place, (block, out, slot) in enumerate(states):
                blended = jnp.dot(
                    mixed_refs[source][place * width + v], block_ref[block], preferred_element_type=jnp.float32
                ).astype(jnp.bfloat16)
                part = jnp.dot(flipped_ref[block], blended, preferred_element_type=jnp.float32)
                key = (out, slot)
                totals[key] = part if key not in totals else totals[key] + part
        for (out, slot), total in totals.items():
            out_refs[out][slot, v] = total.astype(jnp.bfloat16)
        return 0

    lax.fori_loop(0, width, channel, 0)


def products(plan, out_sizes, envs, mixers, blocks, width):
    cap = envs[0].shape[-1]
    work = sum(len(states) for states in plan)
    kernel = lambda *refs: product_kernel(plan, out_sizes, len(envs), *refs)
    return pl.pallas_call(
        kernel,
        out_shape=[jax.ShapeDtypeStruct((n, width, cap, cap), jnp.bfloat16) for n in out_sizes],
        in_specs=[pl.BlockSpec(memory_space=pltpu.VMEM)] * (2 * len(envs) + 1),
        out_specs=[pl.BlockSpec(memory_space=pltpu.VMEM)] * len(out_sizes),
        scratch_shapes=[pltpu.VMEM((len(states) * width, cap, cap), jnp.bfloat16) for states in plan]
        + [pltpu.VMEM(blocks.shape, jnp.bfloat16)],
        compiler_params=pltpu.CompilerParams(vmem_limit_bytes=VMEM_BYTES),
        cost_estimate=pl.CostEstimate(
            flops=6 * work * width * cap**3, bytes_accessed=4 * 2**20, transcendentals=0
        ),
    )(*envs, *mixers, blocks)


def masked_blocks(site_block_tensors, block_mask, sector_dims):
    capacity = site_block_tensors.shape[-1]
    sector_total = lax.axis_size("sec")
    sector_id = lax.axis_index("sec")
    offsets = jnp.array([0, ND, 1, ND + 1])
    down_step = jnp.array([0, 0, 1, 1])
    targets = sector_id + offsets
    allowed = (targets < sector_total) & ((down_step == 0) | (sector_id % ND < ND - 1))
    sectors = jnp.arange(sector_total)
    own_dims = jnp.sum(jnp.where(sectors == sector_id, sector_dims, 0))
    target_dims = jnp.sum(
        jnp.where(sectors[None, :] == targets[:, None], sector_dims[None, :], 0), axis=1
    )
    target_dims = jnp.where(allowed, target_dims, 0)
    line = jnp.arange(capacity)
    row_live = line < own_dims
    col_live = line[None, :] < target_dims[:, None]
    present = (block_mask[:, 0] * allowed.astype(jnp.int32)).astype(jnp.bfloat16)
    live = row_live[None, :, None] & col_live[:, None, :]
    return jnp.where(live[None], site_block_tensors[:, 0] * present[:, :, None, None], 0)


def two_rows(boundary_env, site_block_tensors, mpo_tensors, block_mask, sector_dims):
    env = boundary_env[0, 0]
    channels = env.shape[0]
    near_env = shift_column(env)
    blocks = masked_blocks(site_block_tensors, block_mask, sector_dims)
    near_blocks = shift_column(blocks[0, 2:4])
    below = lax.ppermute(blocks[1, 0::2], "sec", [(ND + j, j) for j in range(ND)])
    wide = [widen(mpo_tensors[n]) for n in range(2)]
    span = channels * ROWS

    def mixer(n, states, low, high):
        return jnp.concatenate([wide[n][s, low:high] for s in states]).reshape(-1, span)

    (middle,) = products(
        (((0, 0, 0), (1, 0, 1)), ((2, 0, 0), (3, 0, 1))), (2,),
        (env, near_env), (mixer(0, (0, 1), 0, channels), mixer(0, (2, 3), 0, channels)),
        jnp.concatenate([blocks[0, 0:2], near_blocks]), channels,
    )
    last_blocks = jnp.concatenate([blocks[1], below])
    handed = []
    cuts = [0, 4, 7, 10, channels]
    for low, high in zip(cuts[:-1], cuts[1:]):
        stay, up = products(
            (((0, 0, 0), (1, 0, 1), (2, 1, 0), (3, 1, 1)), ((4, 0, 1), (5, 1, 1))), (2, 2),
            (middle[0], middle[1]), (mixer(1, (0, 1, 2, 3), low, high), mixer(1, (0, 2), low, high)),
            last_blocks, high - low,
        )
        arrived = shift_column(up)
        both = stay.astype(jnp.float32) + arrived.astype(jnp.float32)
        from_up = from_behind(both[1].astype(jnp.bfloat16), "sec", ND)
        total = (both[0] + from_up.astype(jnp.float32)).astype(jnp.bfloat16)
        handed.append(from_behind(total, "seg", 1))
    return jnp.concatenate(handed)[None, None]


def contract(left_environ_tensor, block_list, weight_factors):
    merged_mixture = jnp.einsum(
        "umi,ue->emi", left_environ_tensor, weight_factors, preferred_element_type=jnp.float32
    ).astype(jnp.bfloat16)
    combined_mixture = jnp.einsum(
        "gip,pq->giq", merged_mixture, block_list, preferred_element_type=jnp.float32
    ).astype(jnp.bfloat16)
    return jnp.einsum(
        "ba,vbc->vac", block_list, combined_mixture, preferred_element_type=jnp.float32
    ).astype(jnp.bfloat16)


def any_rows(boundary_env, site_block_tensors, mpo_tensors, block_mask, sector_dims):
    blocks = masked_blocks(site_block_tensors, block_mask, sector_dims)
    env = boundary_env[0, 0]
    for n in range(blocks.shape[0]):
        parts = [contract(env, blocks[n, s], mpo_tensors[n, s]) for s in range(4)]
        total = parts[0].astype(jnp.float32) + from_behind(parts[1], "sec", ND).astype(jnp.float32)
        total = total + from_behind(parts[2], "sec", 1).astype(jnp.float32)
        total = total + from_behind(parts[3], "sec", ND + 1).astype(jnp.float32)
        env = total.astype(jnp.bfloat16)
    return from_behind(env, "seg", 1)[None, None]


def solution(mesh):
    in_specs = (
        P("seg", "sec", None, None, None),
        P("seg", "sec", None, None, None),
        P("seg", None, None, None),
        P("seg", "sec", None),
        P(),
    )
    out_specs = P("seg", "sec", None, None, None)
    body = two_rows if mesh.shape["sec"] == 2 * ND else any_rows
    return jax.shard_map(body, mesh=mesh, in_specs=in_specs, out_specs=out_specs, check_vma=False)
```

time: 219 us -> 182 us (0.83)
  the two profiles are of different devices: /device:TPU:0 before, /device:TPU:1 now
where the time goes in v1:
time: 182 us; the launch traced here: 179 us
  Pallas kernels  57.4 us (32%)
  starting transfers between devices  41.1 us (23%)
  waiting for transfers between devices  35.6 us (20%)
  local copies, waits for them, and re-layouts  24.1 us (13%)
  other arithmetic  19.9 us (11%)
    pallas_call x5, Pallas kernels, products(): pl.pallas_call(kernel, out_shape=[jax.ShapeDtypeStruct((n, width, cap, ca...  57.4 us
    ppermute x8, waiting for transfers between devices, from_behind(): return lax.ppermute(shard, axis, pairs)  33.2 us
    ppermute x8, starting transfers between devices, from_behind(): return lax.ppermute(shard, axis, pairs)  25.6 us
    reshape x10, local copies, waits for them, and re-layouts, mixer(): jnp.concatenate([wide[n][s, low:high] for s in states]).reshape(-1, span)  15.3 us
    ppermute x6, starting transfers between devices, shift_column(): lax.ppermute(shard, 'sec', [(q, q + 1) for q in range(count - 1) if q % N...  14.2 us
    concatenate x7, other arithmetic, mixer(): jnp.concatenate([wide[n][s, low:high] for s in states]).reshape(-1, span)  5.88 us
    squeeze x1, local copies, waits for them, and re-layouts, two_rows(): middle[1]  4.08 us
  transfers between devices with their start and end apart: 15, of which 4 were waited for; matrix products, arithmetic and copies ran while one was open for 16% of the time, Pallas kernels for 18%

profile of v1, /device:TPU:1, one launch (start us, length us, event | category | flops | bytes accessed | tf_op | source)
XLA Modules:
  0.0 178.6 jit_solution(17453441552622415168)
XLA Ops:
  9.1 4.5 %collective-permute-start.1 = (bf16[2,256,256]{2,1,0:T(8,128)(2,1)}, bf16[2,256,256]{2,1,0:T(8,128)(2,1)}, u32[]{:S(2)}, u32[]{:S(2)}) collective-permute-start(bf16[2,256,256]{2,1,0:T(8,128)(2,1)} %get-tuple-element.44), channel_id=1, source_target_pairs={{0,1},{1,2},{2,3},{4,5},{5,6},{6,7},{8,9},{9,10},{10,11},{12,13},{... | collective-permute-start | bytes 786440 | tf_op jit(solution)/shard_map/ppermute | solution.py:21
  13.6 1.9 %collective-permute-start = (bf16[13,256,256]{2,1,0:T(8,128)(2,1)}, bf16[13,256,256]{2,1,0:T(8,128)(2,1)}, u32[]{:S(2)}, u32[]{:S(2)}) collective-permute-start(bf16[13,256,256]{2,1,0:T(8,128)(2,1)} %bitcast.refs_0_), channel_id=1, source_target_pairs={{0,1},{1,2},{2,3},{4,5},{5,6},{6,7},{8,9},{9,10},{10,11},{12,13},{... | collective-permute-start | bytes 5111816 | tf_op jit(solution)/shard_map/ppermute | solution.py:21
  25.6 2.0 %reshape.85.refs_2_ = bf16[416,208]{1,0:T(8,128)(2,1)} reshape(bf16[26,16,13,16]{3,2,1,0:T(8,128)(2,1)S(1)} %get-tuple-element.50) | data formatting | bytes 346112 | tf_op jit(solution)/shard_map/reshape | solution.py:120
  27.7 2.1 %reshape.86.refs_3_ = bf16[416,208]{1,0:T(8,128)(2,1)} reshape(bf16[26,16,13,16]{3,2,1,0:T(8,128)(2,1)S(1)} %get-tuple-element.51) | data formatting | bytes 346112 | tf_op jit(solution)/shard_map/reshape | solution.py:120
  32.3 2.4 %reshape.89.refs_2_ = bf16[192,208]{1,0:T(8,128)(2,1)} reshape(bf16[12,16,13,16]{3,2,1,0:T(8,128)(2,1)} %get-tuple-element.52) | data formatting | bytes 159744 | tf_op jit(solution)/shard_map/reshape | solution.py:120
  34.8 1.9 %reshape.90.refs_3_ = bf16[96,208]{1,0:T(8,128)(2,1)} reshape(bf16[6,16,13,16]{3,2,1,0:T(8,128)(2,1)} %get-tuple-element.54) | data formatting | bytes 79872 | tf_op jit(solution)/shard_map/reshape | solution.py:120
  42.6 16.1 %shard_map.73 = bf16[2,13,256,256]{3,2,1,0:T(8,128)(2,1)} custom-call(bf16[13,256,256]{2,1,0:T(8,128)(2,1)} %bitcast.refs_0_, bf16[13,256,256]{2,1,0:T(8,128)(2,1)} %collective-permute-done.refs_1_, bf16[416,208]{1,0:T(8,128)(2,1)} %reshape.85.refs_2_, bf16[416,208]{1,0:T(8,128)(2,1)} %reshape.86.refs_3_, bf16[4,256,256]{2,1,0:T(8,128)(2,1)} %pad_maximum_fusion.7.refs_4_), custom_call_target="tpu_custom_call" | custom-call | flops 5234491392 | bytes 4194304 | tf_op jit(solution)/shard_map/pallas_call | solution.py:73
  58.7 4.1 %slice_bitcast_fusion = (bf16[13,256,256]{2,1,0:T(8,128)(2,1)}, bf16[13,256,256]{2,1,0:T(8,128)(2,1)}) fusion(bf16[2,13,256,256]{3,2,1,0:T(8,128)(2,1)} %shard_map.73), kind=kLoop, calls=%fused_computation.1 | loop fusion | bytes 6815744 | tf_op jit(solution)/shard_map/squeeze | solution.py:133
  62.8 10.0 %shard_map.75 = (bf16[2,3,256,256]{3,2,1,0:T(8,128)(2,1)}, bf16[2,3,256,256]{3,2,1,0:T(8,128)(2,1)}) custom-call(bf16[13,256,256]{2,1,0:T(8,128)(2,1)} %get-tuple-element.38.refs_0_, bf16[13,256,256]{2,1,0:T(8,128)(2,1)} %get-tuple-element.37.refs_1_, bf16[192,208]{1,0:T(8,128)(2,1)} %reshape.89.refs_2_, bf16[96,208]{1,0:T(8,128)(2,1)} %reshape.90.refs_3_, ...), custom_call_target="tpu_custom_call" | custom-call | flops 1811939328 | bytes 4194304 | tf_op jit(solution)/shard_map/pallas_call | solution.py:73
  72.8 1.9 %collective-permute-start.6 = (bf16[2,3,256,256]{3,2,1,0:T(8,128)(2,1)}, bf16[2,3,256,256]{3,2,1,0:T(8,128)(2,1)S(1)}, u32[]{:S(2)}, u32[]{:S(2)}) collective-permute-start(bf16[2,3,256,256]{3,2,1,0:T(8,128)(2,1)} %get-tuple-element.16), channel_id=1, source_target_pairs={{0,1},{1,2},{2,3},{4,5},{5,6},{6,7},{8,9},{9,10},{10,11},{12,13},{... | collective-permute-start | bytes 2359304 | tf_op jit(solution)/shard_map/ppermute | solution.py:21
  77.2 10.0 %shard_map.76 = (bf16[2,3,256,256]{3,2,1,0:T(8,128)(2,1)}, bf16[2,3,256,256]{3,2,1,0:T(8,128)(2,1)}) custom-call(bf16[13,256,256]{2,1,0:T(8,128)(2,1)} %get-tuple-element.38.refs_0_, bf16[13,256,256]{2,1,0:T(8,128)(2,1)} %get-tuple-element.37.refs_1_, bf16[192,208]{1,0:T(8,128)(2,1)} %reshape.91.refs_2_, bf16[96,208]{1,0:T(8,128)(2,1)} %reshape.92.refs_3_, ...), custom_call_target="tpu_custom_call" | custom-call | flops 1811939328 | bytes 4194304 | tf_op jit(solution)/shard_map/pallas_call | solution.py:73
  89.1 11.4 %shard_map.74 = (bf16[2,4,256,256]{3,2,1,0:T(8,128)(2,1)}, bf16[2,4,256,256]{3,2,1,0:T(8,128)(2,1)}) custom-call(bf16[13,256,256]{2,1,0:T(8,128)(2,1)} %get-tuple-element.38.refs_0_, bf16[13,256,256]{2,1,0:T(8,128)(2,1)} %get-tuple-element.37.refs_1_, bf16[256,208]{1,0:T(8,128)(2,1)} %reshape.95.refs_2_, bf16[128,208]{1,0:T(8,128)(2,1)} %reshape.96.refs_3_, ...), custom_call_target="tpu_custom_call" | custom-call | flops 2415919104 | bytes 4194304 | tf_op jit(solution)/shard_map/pallas_call | solution.py:73
  100.5 2.0 %collective-permute-start.3 = (bf16[2,4,256,256]{3,2,1,0:T(8,128)(2,1)}, bf16[2,4,256,256]{3,2,1,0:T(8,128)(2,1)S(1)}, u32[]{:S(2)}, u32[]{:S(2)}) collective-permute-start(bf16[2,4,256,256]{3,2,1,0:T(8,128)(2,1)} %get-tuple-element.14), channel_id=1, source_target_pairs={{0,1},{1,2},{2,3},{4,5},{5,6},{6,7},{8,9},{9,10},{10,11},{12,13},{... | collective-permute-start | bytes 3145736 | tf_op jit(solution)/shard_map/ppermute | solution.py:21
  102.6 9.9 %shard_map.77 = (bf16[2,3,256,256]{3,2,1,0:T(8,128)(2,1)}, bf16[2,3,256,256]{3,2,1,0:T(8,128)(2,1)}) custom-call(bf16[13,256,256]{2,1,0:T(8,128)(2,1)} %get-tuple-element.38.refs_0_, bf16[13,256,256]{2,1,0:T(8,128)(2,1)} %get-tuple-element.37.refs_1_, bf16[192,208]{1,0:T(8,128)(2,1)} %reshape.93.refs_2_, bf16[96,208]{1,0:T(8,128)(2,1)} %reshape.94.refs_3_, ...), custom_call_target="tpu_custom_call" | custom-call | flops 1811939328 | bytes 4194304 | tf_op jit(solution)/shard_map/pallas_call | solution.py:73
  114.7 5.0 %collective-permute-start.7 = (bf16[3,256,256]{2,1,0:T(8,128)(2,1)S(1)}, bf16[3,256,256]{2,1,0:T(8,128)(2,1)S(1)}, u32[]{:S(2)}, u32[]{:S(2)}) collective-permute-start(bf16[3,256,256]{2,1,0:T(8,128)(2,1)S(1)} %fusion.10), channel_id=1, source_target_pairs={{0,4},{1,5},{2,6},{3,7},{8,12},{9,13},{10,14},{11,15},{16,20},{17,... | collective-permute-start | bytes 1179656 | tf_op jit(solution)/shard_map/ppermute | solution.py:16
  121.2 2.4 %collective-permute-done.12 = bf16[2,3,256,256]{3,2,1,0:T(8,128)(2,1)S(1)} collective-permute-done((bf16[2,3,256,256]{3,2,1,0:T(8,128)(2,1)}, bf16[2,3,256,256]{3,2,1,0:T(8,128)(2,1)S(1)}, u32[]{:S(2)}, u32[]{:S(2)}) %collective-permute-start.12) | collective-permute-done | bytes 786464 | tf_op jit(solution)/shard_map/ppermute | solution.py:21
  123.9 5.1 %collective-permute-start.13 = (bf16[3,256,256]{2,1,0:T(8,128)(2,1)S(1)}, bf16[3,256,256]{2,1,0:T(8,128)(2,1)S(1)}, u32[]{:S(2)}, u32[]{:S(2)}) collective-permute-start(bf16[3,256,256]{2,1,0:T(8,128)(2,1)S(1)} %fusion.12), channel_id=1, source_target_pairs={{0,4},{1,5},{2,6},{3,7},{8,12},{9,13},{10,14},{11,15},{16,20},{17,... | collective-permute-start | bytes 1179656 | tf_op jit(solution)/shard_map/ppermute | solution.py:16
  130.8 3.2 %collective-permute-start.8 = (bf16[3,256,256]{2,1,0:T(8,128)(2,1)S(1)}, bf16[3,256,256]{2,1,0:T(8,128)(2,1)S(1)}, u32[]{:S(2)}, u32[]{:S(2)}) collective-permute-start(bf16[3,256,256]{2,1,0:T(8,128)(2,1)S(1)} %fusion.8), channel_id=1, source_target_pairs={{0,8},{8,16},{16,24},{1,9},{9,17},{17,25},{2,10},{10,18},{18,26},{... | collective-permute-start | bytes 1179656 | tf_op jit(solution)/shard_map/ppermute | solution.py:16
  134.0 2.0 %collective-permute-done.10 = bf16[3,256,256]{2,1,0:T(8,128)(2,1)S(1)} collective-permute-done((bf16[3,256,256]{2,1,0:T(8,128)(2,1)S(1)}, bf16[3,256,256]{2,1,0:T(8,128)(2,1)S(1)}, u32[]{:S(2)}, u32[]{:S(2)}) %collective-permute-start.10) | collective-permute-done | bytes 393248 | tf_op jit(solution)/shard_map/ppermute | solution.py:16
  136.1 3.2 %collective-permute-start.11 = (bf16[3,256,256]{2,1,0:T(8,128)(2,1)S(1)}, bf16[3,256,256]{2,1,0:T(8,128)(2,1)S(1)}, u32[]{:S(2)}, u32[]{:S(2)}) collective-permute-start(bf16[3,256,256]{2,1,0:T(8,128)(2,1)S(1)} %fusion.6), channel_id=1, source_target_pairs={{0,8},{8,16},{16,24},{1,9},{9,17},{17,25},{2,10},{10,18},{18,26},{... | collective-permute-start | bytes 1179656 | tf_op jit(solution)/shard_map/ppermute | solution.py:16
  139.3 16.3 %collective-permute-done.4 = bf16[4,256,256]{2,1,0:T(8,128)(2,1)S(1)} collective-permute-done((bf16[4,256,256]{2,1,0:T(8,128)(2,1)S(1)}, bf16[4,256,256]{2,1,0:T(8,128)(2,1)S(1)}, u32[]{:S(2)}, u32[]{:S(2)}) %collective-permute-start.4) | collective-permute-done | bytes 524320 | tf_op jit(solution)/shard_map/ppermute | solution.py:16
  155.8 3.2 %collective-permute-start.5 = (bf16[4,256,256]{2,1,0:T(8,128)(2,1)S(1)}, bf16[4,256,256]{2,1,0:T(8,128)(2,1)S(1)}, u32[]{:S(2)}, u32[]{:S(2)}) collective-permute-start(bf16[4,256,256]{2,1,0:T(8,128)(2,1)S(1)} %fusion.1), channel_id=1, source_target_pairs={{0,8},{8,16},{16,24},{1,9},{9,17},{17,25},{2,10},{10,18},{18,26},{... | collective-permute-start | bytes 1572872 | tf_op jit(solution)/shard_map/ppermute | solution.py:16
  159.1 3.2 %collective-permute-start.14 = (bf16[3,256,256]{2,1,0:T(8,128)(2,1)S(1)}, bf16[3,256,256]{2,1,0:T(8,128)(2,1)S(1)}, u32[]{:S(2)}, u32[]{:S(2)}) collective-permute-start(bf16[3,256,256]{2,1,0:T(8,128)(2,1)S(1)} %fusion.4), channel_id=1, source_target_pairs={{0,8},{8,16},{16,24},{1,9},{9,17},{17,25},{2,10},{10,18},{18,26},{... | collective-permute-start | bytes 1179656 | tf_op jit(solution)/shard_map/ppermute | solution.py:16
  162.4 14.9 %collective-permute-done.14 = bf16[3,256,256]{2,1,0:T(8,128)(2,1)S(1)} collective-permute-done((bf16[3,256,256]{2,1,0:T(8,128)(2,1)S(1)}, bf16[3,256,256]{2,1,0:T(8,128)(2,1)S(1)}, u32[]{:S(2)}, u32[]{:S(2)}) %collective-permute-start.14) | collective-permute-done | bytes 393248 | tf_op jit(solution)/shard_map/ppermute | solution.py:16
  (96 shorter events, 39.3 us)
Async XLA Ops:
  5.8 11.1 %copy-start.15 = (bf16[2,4,13,13]{3,1,2,0:T(4,128)(2,1)S(1)}, bf16[2,4,13,13]{3,1,2,0:T(4,128)(2,1)}, u32[]{:S(2)}) copy-start(bf16[2,4,13,13]{3,1,2,0:T(4,128)(2,1)} %param.9) | copy-start | bytes 8116
  9.1 29.8 %collective-permute-start.1 = (bf16[2,256,256]{2,1,0:T(8,128)(2,1)}, bf16[2,256,256]{2,1,0:T(8,128)(2,1)}, u32[]{:S(2)}, u32[]{:S(2)}) collective-permute-start(bf16[2,256,256]{2,1,0:T(8,128)(2,1)} %get-tuple-element.44), channel_id=1, source_target_pairs={{0,1},{1,2},{2,3},{4,5},{5,6},{6,7},{8,9},{9,10},{10,11},{12,13},{... | collective-permute-start | bytes 786440 | tf_op jit(solution)/shard_map/ppermute | solution.py:21
  13.6 29.0 %collective-permute-start = (bf16[13,256,256]{2,1,0:T(8,128)(2,1)}, bf16[13,256,256]{2,1,0:T(8,128)(2,1)}, u32[]{:S(2)}, u32[]{:S(2)}) collective-permute-start(bf16[13,256,256]{2,1,0:T(8,128)(2,1)} %bitcast.refs_0_), channel_id=1, source_target_pairs={{0,1},{1,2},{2,3},{4,5},{5,6},{6,7},{8,9},{9,10},{10,11},{12,13},{... | collective-permute-start | bytes 5111816 | tf_op jit(solution)/shard_map/ppermute | solution.py:21
  15.5 25.2 %collective-permute-start.2 = (bf16[2,256,256]{2,1,0:T(8,128)(2,1)}, bf16[2,256,256]{2,1,0:T(8,128)(2,1)}, u32[]{:S(2)}, u32[]{:S(2)}) collective-permute-start(bf16[2,256,256]{2,1,0:T(8,128)(2,1)} %get-tuple-element.43), channel_id=1, source_target_pairs={{4,0},{5,1},{6,2},{7,3},{12,8},{13,9},{14,10},{15,11},{20,16},{21,... | collective-permute-start | bytes 786440 | tf_op jit(solution)/shard_map/ppermute | solution.py:115
  29.8 6.9 %copy-start.3 = (bf16[12,16,13,16]{3,2,1,0:T(8,128)(2,1)S(1)}, bf16[12,16,13,16]{3,2,1,0:T(8,128)(2,1)}, u32[]{:S(2)}) copy-start(bf16[12,16,13,16]{3,2,1,0:T(8,128)(2,1)} %get-tuple-element.53) | copy-start | bytes 239620
  31.3 6.6 %copy-start.7 = (bf16[6,16,13,16]{3,2,1,0:T(8,128)(2,1)S(1)}, bf16[6,16,13,16]{3,2,1,0:T(8,128)(2,1)}, u32[]{:S(2)}) copy-start(bf16[6,16,13,16]{3,2,1,0:T(8,128)(2,1)} %get-tuple-element.55) | copy-start | bytes 119812
  31.3 7.5 %copy-start.1 = (bf16[2,4,256,256]{3,2,1,0:T(8,128)(2,1)S(1)}, bf16[2,4,256,256]{3,2,1,0:T(8,128)(2,1)}, u32[]{:S(2)}) copy-start(bf16[2,4,256,256]{3,2,1,0:T(8,128)(2,1)} %copy-done) | copy-start | bytes 3145732
  62.8 11.9 %copy-start.5 = (bf16[3,16,13,16]{3,2,1,0:T(8,128)(2,1)S(1)}, bf16[3,16,13,16]{3,2,1,0:T(8,128)(2,1)}, u32[]{:S(2)}) copy-start(bf16[3,16,13,16]{3,2,1,0:T(8,128)(2,1)} %get-tuple-element.27) | copy-start | bytes 59908
  62.8 11.9 %copy-start.6 = (bf16[3,16,13,16]{3,2,1,0:T(8,128)(2,1)S(1)}, bf16[3,16,13,16]{3,2,1,0:T(8,128)(2,1)}, u32[]{:S(2)}) copy-start(bf16[3,16,13,16]{3,2,1,0:T(8,128)(2,1)} %get-tuple-element.29) | copy-start | bytes 59908
  62.8 11.9 %copy-start.10 = (bf16[3,16,13,16]{3,2,1,0:T(8,128)(2,1)S(1)}, bf16[3,16,13,16]{3,2,1,0:T(8,128)(2,1)}, u32[]{:S(2)}) copy-start(bf16[3,16,13,16]{3,2,1,0:T(8,128)(2,1)} %get-tuple-element.26) | copy-start | bytes 59908
  62.8 11.9 %copy-start.11 = (bf16[3,16,13,16]{3,2,1,0:T(8,128)(2,1)S(1)}, bf16[3,16,13,16]{3,2,1,0:T(8,128)(2,1)}, u32[]{:S(2)}) copy-start(bf16[3,16,13,16]{3,2,1,0:T(8,128)(2,1)} %get-tuple-element.28) | copy-start | bytes 59908
  72.8 41.6 %collective-permute-start.6 = (bf16[2,3,256,256]{3,2,1,0:T(8,128)(2,1)}, bf16[2,3,256,256]{3,2,1,0:T(8,128)(2,1)S(1)}, u32[]{:S(2)}, u32[]{:S(2)}) collective-permute-start(bf16[2,3,256,256]{3,2,1,0:T(8,128)(2,1)} %get-tuple-element.16), channel_id=1, source_target_pairs={{0,1},{1,2},{2,3},{4,5},{5,6},{6,7},{8,9},{9,10},{10,11},{12,13},{... | collective-permute-start | bytes 2359304 | tf_op jit(solution)/shard_map/ppermute | solution.py:21
  87.2 32.5 %collective-permute-start.9 = (bf16[2,3,256,256]{3,2,1,0:T(8,128)(2,1)}, bf16[2,3,256,256]{3,2,1,0:T(8,128)(2,1)S(1)}, u32[]{:S(2)}, u32[]{:S(2)}) collective-permute-start(bf16[2,3,256,256]{3,2,1,0:T(8,128)(2,1)} %get-tuple-element.18), channel_id=1, source_target_pairs={{0,1},{1,2},{2,3},{4,5},{5,6},{6,7},{8,9},{9,10},{10,11},{12,13},{... | collective-permute-start | bytes 2359304 | tf_op jit(solution)/shard_map/ppermute | solution.py:21
  100.5 13.9 %copy-start.12 = (bf16[2,3,256,256]{3,2,1,0:T(8,128)(2,1)S(1)}, bf16[2,3,256,256]{3,2,1,0:T(8,128)(2,1)}, u32[]{:S(2)}) copy-start(bf16[2,3,256,256]{3,2,1,0:T(8,128)(2,1)} %get-tuple-element.15) | copy-start | bytes 2359300
  100.5 28.5 %collective-permute-start.3 = (bf16[2,4,256,256]{3,2,1,0:T(8,128)(2,1)}, bf16[2,4,256,256]{3,2,1,0:T(8,128)(2,1)S(1)}, u32[]{:S(2)}, u32[]{:S(2)}) collective-permute-start(bf16[2,4,256,256]{3,2,1,0:T(8,128)(2,1)} %get-tuple-element.14), channel_id=1, source_target_pairs={{0,1},{1,2},{2,3},{4,5},{5,6},{6,7},{8,9},{9,10},{10,11},{12,13},{... | collective-permute-start | bytes 3145736 | tf_op jit(solution)/shard_map/ppermute | solution.py:21
  112.5 11.1 %collective-permute-start.12 = (bf16[2,3,256,256]{3,2,1,0:T(8,128)(2,1)}, bf16[2,3,256,256]{3,2,1,0:T(8,128)(2,1)S(1)}, u32[]{:S(2)}, u32[]{:S(2)}) collective-permute-start(bf16[2,3,256,256]{3,2,1,0:T(8,128)(2,1)} %get-tuple-element.20), channel_id=1, source_target_pairs={{0,1},{1,2},{2,3},{4,5},{5,6},{6,7},{8,9},{9,10},{10,11},{12,13},{... | collective-permute-start | bytes 2359304 | tf_op jit(solution)/shard_map/ppermute | solution.py:21
  114.7 16.0 %collective-permute-start.7 = (bf16[3,256,256]{2,1,0:T(8,128)(2,1)S(1)}, bf16[3,256,256]{2,1,0:T(8,128)(2,1)S(1)}, u32[]{:S(2)}, u32[]{:S(2)}) collective-permute-start(bf16[3,256,256]{2,1,0:T(8,128)(2,1)S(1)} %fusion.10), channel_id=1, source_target_pairs={{0,4},{1,5},{2,6},{3,7},{8,12},{9,13},{10,14},{11,15},{16,20},{17,... | collective-permute-start | bytes 1179656 | tf_op jit(solution)/shard_map/ppermute | solution.py:16
  119.9 16.1 %collective-permute-start.10 = (bf16[3,256,256]{2,1,0:T(8,128)(2,1)S(1)}, bf16[3,256,256]{2,1,0:T(8,128)(2,1)S(1)}, u32[]{:S(2)}, u32[]{:S(2)}) collective-permute-start(bf16[3,256,256]{2,1,0:T(8,128)(2,1)S(1)} %fusion.11), channel_id=1, source_target_pairs={{0,4},{1,5},{2,6},{3,7},{8,12},{9,13},{10,14},{11,15},{16,20},{17,... | collective-permute-start | bytes 1179656 | tf_op jit(solution)/shard_map/ppermute | solution.py:16
  123.9 35.2 %collective-permute-start.13 = (bf16[3,256,256]{2,1,0:T(8,128)(2,1)S(1)}, bf16[3,256,256]{2,1,0:T(8,128)(2,1)S(1)}, u32[]{:S(2)}, u32[]{:S(2)}) collective-permute-start(bf16[3,256,256]{2,1,0:T(8,128)(2,1)S(1)} %fusion.12), channel_id=1, source_target_pairs={{0,4},{1,5},{2,6},{3,7},{8,12},{9,13},{10,14},{11,15},{16,20},{17,... | collective-permute-start | bytes 1179656 | tf_op jit(solution)/shard_map/ppermute | solution.py:16
  129.3 26.3 %collective-permute-start.4 = (bf16[4,256,256]{2,1,0:T(8,128)(2,1)S(1)}, bf16[4,256,256]{2,1,0:T(8,128)(2,1)S(1)}, u32[]{:S(2)}, u32[]{:S(2)}) collective-permute-start(bf16[4,256,256]{2,1,0:T(8,128)(2,1)S(1)} %fusion.9), channel_id=1, source_target_pairs={{0,4},{1,5},{2,6},{3,7},{8,12},{9,13},{10,14},{11,15},{16,20},{17,... | collective-permute-start | bytes 1572872 | tf_op jit(solution)/shard_map/ppermute | solution.py:16
  130.8 31.6 %collective-permute-start.8 = (bf16[3,256,256]{2,1,0:T(8,128)(2,1)S(1)}, bf16[3,256,256]{2,1,0:T(8,128)(2,1)S(1)}, u32[]{:S(2)}, u32[]{:S(2)}) collective-permute-start(bf16[3,256,256]{2,1,0:T(8,128)(2,1)S(1)} %fusion.8), channel_id=1, source_target_pairs={{0,8},{8,16},{16,24},{1,9},{9,17},{17,25},{2,10},{10,18},{18,26},{... | collective-permute-start | bytes 1179656 | tf_op jit(solution)/shard_map/ppermute | solution.py:16
  136.1 26.3 %collective-permute-start.11 = (bf16[3,256,256]{2,1,0:T(8,128)(2,1)S(1)}, bf16[3,256,256]{2,1,0:T(8,128)(2,1)S(1)}, u32[]{:S(2)}, u32[]{:S(2)}) collective-permute-start(bf16[3,256,256]{2,1,0:T(8,128)(2,1)S(1)} %fusion.6), channel_id=1, source_target_pairs={{0,8},{8,16},{16,24},{1,9},{9,17},{17,25},{2,10},{10,18},{18,26},{... | collective-permute-start | bytes 1179656 | tf_op jit(solution)/shard_map/ppermute | solution.py:16
  155.8 21.4 %collective-permute-start.5 = (bf16[4,256,256]{2,1,0:T(8,128)(2,1)S(1)}, bf16[4,256,256]{2,1,0:T(8,128)(2,1)S(1)}, u32[]{:S(2)}, u32[]{:S(2)}) collective-permute-start(bf16[4,256,256]{2,1,0:T(8,128)(2,1)S(1)} %fusion.1), channel_id=1, source_target_pairs={{0,8},{8,16},{16,24},{1,9},{9,17},{17,25},{2,10},{10,18},{18,26},{... | collective-permute-start | bytes 1572872 | tf_op jit(solution)/shard_map/ppermute | solution.py:16
  159.1 18.1 %collective-permute-start.14 = (bf16[3,256,256]{2,1,0:T(8,128)(2,1)S(1)}, bf16[3,256,256]{2,1,0:T(8,128)(2,1)S(1)}, u32[]{:S(2)}, u32[]{:S(2)}) collective-permute-start(bf16[3,256,256]{2,1,0:T(8,128)(2,1)S(1)} %fusion.4), channel_id=1, source_target_pairs={{0,8},{8,16},{16,24},{1,9},{9,17},{17,25},{2,10},{10,18},{18,26},{... | collective-permute-start | bytes 1179656 | tf_op jit(solution)/shard_map/ppermute | solution.py:16
  (7 other events, 27.8 us)

commit v2 on v1

v2 whole, which is shorter than its diff:
```python
import jax
import jax.numpy as jnp
from jax import lax
from jax.experimental import pallas as pl
from jax.experimental.pallas import tpu as pltpu
from jax.sharding import PartitionSpec as P

ND = 4
ROWS = 16
PARTS = 2
UNROLL = True
VMEM_BYTES = 56 * 2**20


def from_behind(shard, axis, by):
    count = lax.axis_size(axis)
    pairs = [(i, i + by) for i in range(count) if 0 <= i + by < count]
    return lax.ppermute(shard, axis, pairs)


def shift_column(shard):
    count = lax.axis_size("sec")
    return lax.ppermute(shard, "sec", [(q, q + 1) for q in range(count - 1) if q % ND < ND - 1])


def mask_kernel(site_ref, mask_ref, dims_ref, *out_refs):
    cap = site_ref.shape[-1]
    total = dims_ref.shape[0]
    q = lax.axis_index("sec")
    rows = lax.broadcasted_iota(jnp.int32, (cap, cap), 0)
    columns = lax.broadcasted_iota(jnp.int32, (cap, cap), 1)
    own = rows < dims_ref[q]
    for out_ref, (site, states) in zip(out_refs, TAKEN):
        for place, s in enumerate(states):
            target = q + (0, ND, 1, ND + 1)[s]
            allowed = (mask_ref[site, 0, s] > 0) & (target < total)
            if s >= 2:
                allowed = allowed & (q % ND < ND - 1)
            width = jnp.where(allowed, dims_ref[jnp.minimum(target, total - 1)], 0)
            out_ref[place] = jnp.where(own & (columns < width), site_ref[site, 0, s], 0).astype(jnp.bfloat16)


TAKEN = ((0, (2, 3)), (1, (0, 2)), (0, (0, 1)), (1, (0, 1, 2, 3)))


def mask_blocks(site_block_tensors, block_mask, sector_dims):
    cap = site_block_tensors.shape[-1]
    return pl.pallas_call(
        mask_kernel,
        out_shape=[jax.ShapeDtypeStruct((len(states), cap, cap), jnp.bfloat16) for _, states in TAKEN],
        in_specs=[
            pl.BlockSpec(memory_space=pltpu.VMEM),
            pl.BlockSpec(memory_space=pltpu.SMEM),
            pl.BlockSpec(memory_space=pltpu.SMEM),
        ],
        out_specs=[pl.BlockSpec(memory_space=pltpu.VMEM)] * len(TAKEN),
        compiler_params=pltpu.CompilerParams(vmem_limit_bytes=VMEM_BYTES),
        cost_estimate=pl.CostEstimate(flops=10**6, bytes_accessed=2 * 2**20, transcendentals=0),
    )(site_block_tensors, block_mask, sector_dims)


def build_mixers(mpo_ref, site, plan, mixer_refs):
    channels = mpo_ref.shape[-1]
    span = channels * ROWS
    spread = (
        lax.broadcasted_iota(jnp.int32, (span, channels), 0) // ROWS
        == lax.broadcasted_iota(jnp.int32, (span, channels), 1)
    ).astype(jnp.bfloat16)
    same_row = (
        lax.broadcasted_iota(jnp.int32, (span, span), 0) % ROWS
        == lax.broadcasted_iota(jnp.int32, (span, span), 1) % ROWS
    )
    contract_last = (((1,), (1,)), ((), ()))
    for states, mixer_ref in zip(plan, mixer_refs):
        for place, (state, _, _) in enumerate(states):
            tall = lax.dot_general(spread, mpo_ref[site, state], contract_last, preferred_element_type=jnp.float32)
            wide = lax.dot_general(
                tall.astype(jnp.bfloat16), spread, contract_last, preferred_element_type=jnp.float32
            )
            mixer_ref[place * span:(place + 1) * span, :] = jnp.where(same_row, wide, 0.0).astype(jnp.bfloat16)


def product_kernel(site, plan, cuts, based, block_counts, *refs):
    sources = len(plan)
    outputs = 1 + max(out for states in plan for _, _, out in states)
    parts = len(cuts) - 1
    refs = list(refs)
    env_refs = [refs.pop(0) for _ in plan]
    base_refs = [refs.pop(0) for _ in range(outputs if based else 0)]
    mpo_ref = refs.pop(0)
    block_refs = [refs.pop(0) for _ in block_counts]
    out_refs = [[refs.pop(0) for _ in range(parts)] for _ in range(outputs)]
    mixed_refs = [refs.pop(0) for _ in plan]
    mixer_refs = [refs.pop(0) for _ in plan]
    flipped_ref = refs.pop(0)
    blocks = [(ref, k) for ref, count in zip(block_refs, block_counts) for k in range(count)]
    channels, cap, _ = env_refs[0].shape
    build_mixers(mpo_ref, site, plan, mixer_refs)
    for k, (ref, place) in enumerate(blocks):
        flipped_ref[k] = ref[place].T
    for env_ref, mixer_ref, mixed_ref in zip(env_refs, mixer_refs, mixed_refs):
        count = mixed_ref.shape[0]

        def mix(g, _):
            rows = pl.ds(pl.multiple_of(g * ROWS, ROWS), ROWS)
            piece = env_ref[:, rows, :].reshape(channels * ROWS, cap)
            mixed = jnp.dot(mixer_ref[...], piece, preferred_element_type=jnp.float32)
            mixed_ref[:, rows, :] = mixed.astype(jnp.bfloat16).reshape(count, ROWS, cap)
            return 0

        lax.fori_loop(0, cap // ROWS, mix, 0, unroll=4)
    for part, (low, high) in enumerate(zip(cuts[:-1], cuts[1:])):

        def channel(v, _):
            totals = [None] * outputs
            if based:
                totals = [ref[low + v].astype(jnp.float32) for ref in base_refs]
            for source, states in enumerate(plan):
                for place, (_, block, out) in enumerate(states):
                    ref, k = blocks[block]
                    blended = jnp.dot(
                        mixed_refs[source][place * channels + low + v], ref[k], preferred_element_type=jnp.float32
                    ).astype(jnp.bfloat16)
                    one = jnp.dot(flipped_ref[block], blended, preferred_element_type=jnp.float32)
                    totals[out] = one if totals[out] is None else totals[out] + one
            for out, total in enumerate(totals):
                out_refs[out][part][v] = total.astype(jnp.bfloat16)
            return 0

        lax.fori_loop(0, high - low, channel, 0, unroll=UNROLL)


def products(site, plan, cuts, envs, base, mpo, blocks):
    channels, cap, _ = envs[0].shape
    outputs = 1 + max(out for states in plan for _, _, out in states)
    work = sum(len(states) for states in plan)
    counts = [block.shape[0] for block in blocks]
    span = channels * ROWS
    operands = (*envs, *base, mpo, *blocks)
    results = pl.pallas_call(
        lambda *refs: product_kernel(site, plan, cuts, bool(base), counts, *refs),
        out_shape=[
            jax.ShapeDtypeStruct((high - low, cap, cap), jnp.bfloat16)
            for _ in range(outputs) for low, high in zip(cuts[:-1], cuts[1:])
        ],
        in_specs=[pl.BlockSpec(memory_space=pltpu.VMEM)] * len(operands),
        out_specs=[pl.BlockSpec(memory_space=pltpu.VMEM)] * (outputs * (len(cuts) - 1)),
        scratch_shapes=[pltpu.VMEM((len(states) * channels, cap, cap), jnp.bfloat16) for states in plan]
        + [pltpu.VMEM((len(states) * span, span), jnp.bfloat16) for states in plan]
        + [pltpu.VMEM((sum(counts), cap, cap), jnp.bfloat16)],
        compiler_params=pltpu.CompilerParams(vmem_limit_bytes=VMEM_BYTES),
        cost_estimate=pl.CostEstimate(
            flops=6 * work * channels * cap**3, bytes_accessed=4 * 2**20, transcendentals=0
        ),
    )(*operands)
    parts = len(cuts) - 1
    return [results[k * parts:(k + 1) * parts] for k in range(outputs)]


def masked_blocks(site_block_tensors, block_mask, sector_dims):
    capacity = site_block_tensors.shape[-1]
    sector_total = lax.axis_size("sec")
    sector_id = lax.axis_index("sec")
    offsets = jnp.array([0, ND, 1, ND + 1])
    down_step = jnp.array([0, 0, 1, 1])
    targets = sector_id + offsets
    allowed = (targets < sector_total) & ((down_step == 0) | (sector_id % ND < ND - 1))
    sectors = jnp.arange(sector_total)
    own_dims = jnp.sum(jnp.where(sectors == sector_id, sector_dims, 0))
    target_dims = jnp.sum(
        jnp.where(sectors[None, :] == targets[:, None], sector_dims[None, :], 0), axis=1
    )
    target_dims = jnp.where(allowed, target_dims, 0)
    line = jnp.arange(capacity)
    row_live = line < own_dims
    col_live = line[None, :] < target_dims[:, None]
    present = (block_mask[:, 0] * allowed.astype(jnp.int32)).astype(jnp.bfloat16)
    live = row_live[None, :, None] & col_live[:, None, :]
    return jnp.where(live[None], site_block_tensors[:, 0] * present[:, :, None, None], 0)


def two_rows(boundary_env, site_block_tensors, mpo_tensors, block_mask, sector_dims):
    env = boundary_env[0, 0]
    channels = env.shape[0]
    near_env = shift_column(env)
    up_blocks, column_blocks, first_blocks, last_blocks = mask_blocks(site_block_tensors, block_mask, sector_dims)
    near_blocks = shift_column(up_blocks)
    below = lax.ppermute(column_blocks, "sec", [(ND + j, j) for j in range(ND)])
    whole = (0, channels)
    (own,), (own_below,) = products(
        0, (((0, 0, 0), (1, 1, 1)),), whole, (env,), (), mpo_tensors, (first_blocks,)
    )
    (middle,), (middle_below,) = products(
        0, (((2, 0, 0), (3, 1, 1)),), whole, (near_env,), (own, own_below), mpo_tensors, (near_blocks,)
    )
    cuts = tuple(-(-channels * k // PARTS) for k in range(PARTS + 1))
    up, up_below, stay, stay_below = products(
        1, (((0, 0, 2), (1, 1, 3), (2, 2, 0), (3, 3, 1)), ((0, 4, 3), (2, 5, 1))), cuts,
        (middle, middle_below), (), mpo_tensors, (last_blocks, below),
    )
    handed = []
    for part in range(len(cuts) - 1):
        arrived_below = shift_column(up_below[part])
        arrived = shift_column(up[part])
        total_below = (stay_below[part].astype(jnp.float32) + arrived_below.astype(jnp.float32)).astype(jnp.bfloat16)
        from_up = from_behind(total_below, "sec", ND)
        total = stay[part].astype(jnp.float32) + arrived.astype(jnp.float32)
        total = (total + from_up.astype(jnp.float32)).astype(jnp.bfloat16)
        handed.append(from_behind(total, "seg", 1))
    return jnp.concatenate(handed)[None, None]


def contract(left_environ_tensor, block_list, weight_factors):
    merged_mixture = jnp.einsum(
        "umi,ue->emi", left_environ_tensor, weight_factors, preferred_element_type=jnp.float32
    ).astype(jnp.bfloat16)
    combined_mixture = jnp.einsum(
        "gip,pq->giq", merged_mixture, block_list, preferred_element_type=jnp.float32
    ).astype(jnp.bfloat16)
    return jnp.einsum(
        "ba,vbc->vac", block_list, combined_mixture, preferred_element_type=jnp.float32
    ).astype(jnp.bfloat16)


def any_rows(boundary_env, site_block_tensors, mpo_tensors, block_mask, sector_dims):
    blocks = masked_blocks(site_block_tensors, block_mask, sector_dims)
    env = boundary_env[0, 0]
    for n in range(blocks.shape[0]):
        parts = [contract(env, blocks[n, s], mpo_tensors[n, s]) for s in range(4)]
        total = parts[0].astype(jnp.float32) + from_behind(parts[1], "sec", ND).astype(jnp.float32)
        total = total + from_behind(parts[2], "sec", 1).astype(jnp.float32)
        total = total + from_behind(parts[3], "sec", ND + 1).astype(jnp.float32)
        env = total.astype(jnp.bfloat16)
    return from_behind(env, "seg", 1)[None, None]


def solution(mesh):
    in_specs = (
        P("seg", "sec", None, None, None),
        P("seg", "sec", None, None, None),
        P("seg", None, None, None),
        P("seg", "sec", None),
        P(),
    )
    out_specs = P("seg", "sec", None, None, None)
    body = two_rows if mesh.shape["sec"] == 2 * ND else any_rows
    return jax.shard_map(body, mesh=mesh, in_specs=in_specs, out_specs=out_specs, check_vma=False)
```

time: 182 us -> 130 us (0.71); the launches traced: 179 us -> 129 us
  local copies, waits for them, and re-layouts: 24.1 us -> 3.34 us
  Pallas kernels: 57.4 us -> 38.1 us
  other arithmetic: 19.9 us -> 3.71 us
  waiting for transfers between devices: 35.6 us -> 50.9 us
  starting transfers between devices: 41.1 us -> 32.6 us
    pallas_call x5 -> x4, Pallas kernels: 57.4 us -> 38.1 us  [the longest x3 35.6 us: products(): pl.pallas_call(lambda *refs: product_kernel(site, plan, cuts, bool(base),...]
    ppermute x6, waiting for transfers between devices: 2.41 us -> 20.7 us  [shift_column(): lax.ppermute(shard, 'sec', [(q, q + 1) for q in range(count - 1) if q % N...]
    reshape x10 -> x0, local copies, waits for them, and re-layouts: 15.3 us -> none  [mixer(): jnp.concatenate([wide[n][s, low:high] for s in states]).reshape(-1, span)]
    ppermute x8 -> x4, starting transfers between devices: 25.6 us -> 12.1 us  [from_behind(): return lax.ppermute(shard, axis, pairs)]
    concatenate x9 -> x0, other arithmetic: 9.57 us -> none  [the longest x7 5.88 us: mixer(): jnp.concatenate([wide[n][s, low:high] for s in states]).reshape(-1, span)]
    squeeze x6 -> x0, local copies, waits for them, and re-layouts: 7.42 us -> none  [the longest x1 4.08 us: two_rows(): middle[1]]
    ppermute x6, starting transfers between devices: 14.2 us -> 19.2 us  [shift_column(): lax.ppermute(shard, 'sec', [(q, q + 1) for q in range(count - 1) if q % N...]
    ppermute x8 -> x4, waiting for transfers between devices: 33.2 us -> 30.2 us  [from_behind(): return lax.ppermute(shard, axis, pairs)]
  transfers between devices with their start and end apart: 15 -> 11, of which waited for: 4 -> 6; matrix products, arithmetic and copies ran while one was open for 16% -> 3% of each run, Pallas kernels for 18% -> 14%
where the time goes in v2:
time: 130 us; the launch traced here: 129 us
  waiting for transfers between devices  50.9 us (39%)
  Pallas kernels  38.1 us (29%)
  starting transfers between devices  32.6 us (25%)
  other arithmetic  3.71 us (3%)
  local copies, waits for them, and re-layouts  3.34 us (3%)
    pallas_call x3, Pallas kernels, products(): pl.pallas_call(lambda *refs: product_kernel(site, plan, cuts, bool(base),...  35.6 us
    ppermute x4, waiting for transfers between devices, from_behind(): return lax.ppermute(shard, axis, pairs)  30.2 us
    ppermute x6, waiting for transfers between devices, shift_column(): lax.ppermute(shard, 'sec', [(q, q + 1) for q in range(count - 1) if q % N...  20.7 us
    ppermute x6, starting transfers between devices, shift_column(): lax.ppermute(shard, 'sec', [(q, q + 1) for q in range(count - 1) if q % N...  19.2 us
    ppermute x4, starting transfers between devices, from_behind(): return lax.ppermute(shard, axis, pairs)  12.1 us
    unnamed x15, local copies, waits for them, and re-layouts  3.34 us
  transfers between devices with their start and end apart: 11, of which 6 were waited for; matrix products, arithmetic and copies ran while one was open for 3% of the time, Pallas kernels for 14%

profile of v2, /device:TPU:1, one launch (start us, length us, event | category | flops | bytes accessed | tf_op | source)
XLA Modules:
  0.0 128.8 jit_solution(4363847680457471163)
XLA Ops:
  0.0 4.5 %collective-permute-start = (bf16[13,256,256]{2,1,0:T(8,128)(2,1)}, bf16[13,256,256]{2,1,0:T(8,128)(2,1)S(1)}, u32[]{:S(2)}, u32[]{:S(2)}) collective-permute-start(bf16[13,256,256]{2,1,0:T(8,128)(2,1)} %bitcast.3), channel_id=1, source_target_pairs={{0,1},{1,2},{2,3},{4,5},{5,6},{6,7},{8,9},{9,10},{10,11},{12,13},{... | collective-permute-start | bytes 5111816 | tf_op jit(solution)/shard_map/ppermute | solution.py:23
  4.5 2.6 %shard_map.55 = (bf16[2,256,256]{2,1,0:T(8,128)(2,1)}, bf16[2,256,256]{2,1,0:T(8,128)(2,1)}, bf16[2,256,256]{2,1,0:T(8,128)(2,1)}, bf16[4,256,256]{2,1,0:T(8,128)(2,1)}) custom-call(bf16[2,1,4,256,256]{4,3,2,1,0:T(8,128)(2,1)} %site_ref.1, s32[2,1,4]{2,1,0:T(1,128)} %mask_ref.1, s32[8]{0:T(128)} %dims_ref.1), custom_call_target="tpu_custom_call" | custom-call | flops 1000000 | bytes 2097152 | tf_op jit(solution)/shard_map/pallas_call | solution.py:48
  7.1 1.9 %collective-permute-start.1 = (bf16[2,256,256]{2,1,0:T(8,128)(2,1)}, bf16[2,256,256]{2,1,0:T(8,128)(2,1)S(1)}, u32[]{:S(2)}, u32[]{:S(2)}) collective-permute-start(bf16[2,256,256]{2,1,0:T(8,128)(2,1)} %get-tuple-element.24), channel_id=1, source_target_pairs={{0,1},{1,2},{2,3},{4,5},{5,6},{6,7},{8,9},{9,10},{10,11},{12,13},{... | collective-permute-start | bytes 786440 | tf_op jit(solution)/shard_map/ppermute | solution.py:23
  9.0 1.3 %collective-permute-start.2 = (bf16[2,256,256]{2,1,0:T(8,128)(2,1)}, bf16[2,256,256]{2,1,0:T(8,128)(2,1)S(1)}, u32[]{:S(2)}, u32[]{:S(2)}) collective-permute-start(bf16[2,256,256]{2,1,0:T(8,128)(2,1)} %get-tuple-element.28), channel_id=1, source_target_pairs={{4,0},{5,1},{6,2},{7,3},{12,8},{13,9},{14,10},{15,11},{20,16},{21,... | collective-permute-start | bytes 786440 | tf_op jit(solution)/shard_map/ppermute | solution.py:188
  10.3 1.4 %copy.6.refs_1_.refs_3_.refs_2_ = bf16[2,4,13,13]{3,2,1,0:T(8,128)(2,1)} copy(bf16[2,4,13,13]{3,1,2,0:T(4,128)(2,1)} %param.7) | data formatting | bytes 5408 | tf_op args[2]
  11.6 7.2 %shard_map.56 = (bf16[13,256,256]{2,1,0:T(8,128)(2,1)}, bf16[13,256,256]{2,1,0:T(8,128)(2,1)}) custom-call(bf16[13,256,256]{2,1,0:T(8,128)(2,1)} %bitcast.4, bf16[2,4,13,13]{3,2,1,0:T(8,128)(2,1)} %copy.6.refs_1_.refs_3_.refs_2_, bf16[2,256,256]{2,1,0:T(8,128)(2,1)} %get-tuple-element.21.refs_2_), custom_call_target="tpu_custom_call" | custom-call | flops 2617245696 | bytes 4194304 | tf_op jit(solution)/shard_map/pallas_call | solution.py:140
  18.8 7.5 %collective-permute-done.1.refs_4_ = bf16[2,256,256]{2,1,0:T(8,128)(2,1)S(1)} collective-permute-done((bf16[2,256,256]{2,1,0:T(8,128)(2,1)}, bf16[2,256,256]{2,1,0:T(8,128)(2,1)S(1)}, u32[]{:S(2)}, u32[]{:S(2)}) %collective-permute-start.1) | collective-permute-done | bytes 262176 | tf_op jit(solution)/shard_map/ppermute | solution.py:23
  27.6 8.2 %shard_map.57 = (bf16[13,256,256]{2,1,0:T(8,128)(2,1)}, bf16[13,256,256]{2,1,0:T(8,128)(2,1)}) custom-call(bf16[13,256,256]{2,1,0:T(8,128)(2,1)} %copy-done.3, bf16[13,256,256]{2,1,0:T(8,128)(2,1)} %get-tuple-element.22.refs_1_, bf16[13,256,256]{2,1,0:T(8,128)(2,1)} %get-tuple-element.23.refs_2_, bf16[2,4,13,13]{3,2,1,0:T(8,128)(2,1)} %copy.6.refs_1_.refs_3_.refs_2_, ...), custom_call_target="tpu_custom_call" | custom-call | flops 2617245696 | bytes 4194304 | tf_op jit(solution)/shard_map/pallas_call | solution.py:140
  36.5 20.2 %shard_map.58 = (bf16[7,256,256]{2,1,0:T(8,128)(2,1)}, bf16[6,256,256]{2,1,0:T(8,128)(2,1)}, bf16[7,256,256]{2,1,0:T(8,128)(2,1)}, bf16[6,256,256]{2,1,0:T(8,128...) custom-call(bf16[13,256,256]{2,1,0:T(8,128)(2,1)} %get-tuple-element, ...), custom_call_target="tpu_custom_call" | custom-call | flops 7851737088 | bytes 4194304 | tf_op jit(solution)/shard_map/pallas_call | solution.py:140
  56.7 4.4 %collective-permute-start.4 = (bf16[7,256,256]{2,1,0:T(8,128)(2,1)}, bf16[7,256,256]{2,1,0:T(8,128)(2,1)S(1)}, u32[]{:S(2)}, u32[]{:S(2)}) collective-permute-start(bf16[7,256,256]{2,1,0:T(8,128)(2,1)} %get-tuple-element.32), channel_id=1, source_target_pairs={{0,1},{1,2},{2,3},{4,5},{5,6},{6,7},{8,9},{9,10},{10,11},{12,13},{... | collective-permute-start | bytes 2752520 | tf_op jit(solution)/shard_map/ppermute | solution.py:23
  61.1 1.9 %collective-permute-start.8 = (bf16[6,256,256]{2,1,0:T(8,128)(2,1)}, bf16[6,256,256]{2,1,0:T(8,128)(2,1)S(1)}, u32[]{:S(2)}, u32[]{:S(2)}) collective-permute-start(bf16[6,256,256]{2,1,0:T(8,128)(2,1)} %get-tuple-element.36), channel_id=1, source_target_pairs={{0,1},{1,2},{2,3},{4,5},{5,6},{6,7},{8,9},{9,10},{10,11},{12,13},{... | collective-permute-start | bytes 2359304 | tf_op jit(solution)/shard_map/ppermute | solution.py:23
  63.1 1.9 %collective-permute-start.3 = (bf16[7,256,256]{2,1,0:T(8,128)(2,1)}, bf16[7,256,256]{2,1,0:T(8,128)(2,1)S(1)}, u32[]{:S(2)}, u32[]{:S(2)}) collective-permute-start(bf16[7,256,256]{2,1,0:T(8,128)(2,1)} %get-tuple-element.30), channel_id=1, source_target_pairs={{0,1},{1,2},{2,3},{4,5},{5,6},{6,7},{8,9},{9,10},{10,11},{12,13},{... | collective-permute-start | bytes 2752520 | tf_op jit(solution)/shard_map/ppermute | solution.py:23
  65.0 6.8 %collective-permute-done.4 = bf16[7,256,256]{2,1,0:T(8,128)(2,1)S(1)} collective-permute-done((bf16[7,256,256]{2,1,0:T(8,128)(2,1)}, bf16[7,256,256]{2,1,0:T(8,128)(2,1)S(1)}, u32[]{:S(2)}, u32[]{:S(2)}) %collective-permute-start.4) | collective-permute-done | bytes 917536 | tf_op jit(solution)/shard_map/ppermute | solution.py:23
  71.8 1.4 %add_convert_fusion.1 = bf16[7,256,256]{2,1,0:T(8,128)(2,1)S(1)} fusion(bf16[7,256,256]{2,1,0:T(8,128)(2,1)S(1)} %collective-permute-done.4, bf16[7,256,256]{2,1,0:T(8,128)(2,1)} %get-tuple-element.31), kind=kLoop, calls=%fused_computation.1 | loop fusion | flops 1835008 | bytes 2752512 | tf_op jit(solution)/shard_map/convert_element_type | solution.py:205
  73.2 3.3 %collective-permute-start.5 = (bf16[7,256,256]{2,1,0:T(8,128)(2,1)S(1)}, bf16[7,256,256]{2,1,0:T(8,128)(2,1)S(1)}, u32[]{:S(2)}, u32[]{:S(2)}) collective-permute-start(bf16[7,256,256]{2,1,0:T(8,128)(2,1)S(1)} %add_convert_fusion.1), channel_id=1, source_target_pairs={{0,4},{1,5},{2,6},{3,7},{8,12},{9,13},{10,14},{11,15},{16,20},{17,... | collective-permute-start | bytes 2752520 | tf_op jit(solution)/shard_map/ppermute | solution.py:18
  76.6 4.6 %collective-permute-start.7 = (bf16[6,256,256]{2,1,0:T(8,128)(2,1)S(1)}, bf16[6,256,256]{2,1,0:T(8,128)(2,1)S(1)}, u32[]{:S(2)}, u32[]{:S(2)}) collective-permute-start(bf16[6,256,256]{2,1,0:T(8,128)(2,1)S(1)} %copy-done.4), channel_id=1, source_target_pairs={{0,1},{1,2},{2,3},{4,5},{5,6},{6,7},{8,9},{9,10},{10,11},{12,13},{... | collective-permute-start | bytes 2359304 | tf_op jit(solution)/shard_map/ppermute | solution.py:23
  81.4 2.3 %collective-permute-start.9 = (bf16[6,256,256]{2,1,0:T(8,128)(2,1)S(1)}, bf16[6,256,256]{2,1,0:T(8,128)(2,1)S(1)}, u32[]{:S(2)}, u32[]{:S(2)}) collective-permute-start(bf16[6,256,256]{2,1,0:T(8,128)(2,1)S(1)} %add_convert_fusion.3), channel_id=1, source_target_pairs={{0,4},{1,5},{2,6},{3,7},{8,12},{9,13},{10,14},{11,15},{16,20},{17,... | collective-permute-start | bytes 2359304 | tf_op jit(solution)/shard_map/ppermute | solution.py:18
  83.7 6.4 %collective-permute-done.3 = bf16[7,256,256]{2,1,0:T(8,128)(2,1)S(1)} collective-permute-done((bf16[7,256,256]{2,1,0:T(8,128)(2,1)}, bf16[7,256,256]{2,1,0:T(8,128)(2,1)S(1)}, u32[]{:S(2)}, u32[]{:S(2)}) %collective-permute-start.3) | collective-permute-done | bytes 917536 | tf_op jit(solution)/shard_map/ppermute | solution.py:23
  90.0 6.7 %collective-permute-done.5 = bf16[7,256,256]{2,1,0:T(8,128)(2,1)S(1)} collective-permute-done((bf16[7,256,256]{2,1,0:T(8,128)(2,1)S(1)}, bf16[7,256,256]{2,1,0:T(8,128)(2,1)S(1)}, u32[]{:S(2)}, u32[]{:S(2)}) %collective-permute-start.5) | collective-permute-done | bytes 917536 | tf_op jit(solution)/shard_map/ppermute | solution.py:18
  97.1 3.3 %collective-permute-start.6 = (bf16[7,256,256]{2,1,0:T(8,128)(2,1)S(1)}, bf16[7,256,256]{2,1,0:T(8,128)(2,1)S(1)}, u32[]{:S(2)}, u32[]{:S(2)}) collective-permute-start(bf16[7,256,256]{2,1,0:T(8,128)(2,1)S(1)} %add_convert_fusion), channel_id=1, source_target_pairs={{0,8},{8,16},{16,24},{1,9},{9,17},{17,25},{2,10},{10,18},{18,26},{... | collective-permute-start | bytes 2752520 | tf_op jit(solution)/shard_map/ppermute | solution.py:18
  100.4 7.4 %collective-permute-done.9 = bf16[6,256,256]{2,1,0:T(8,128)(2,1)S(1)} collective-permute-done((bf16[6,256,256]{2,1,0:T(8,128)(2,1)S(1)}, bf16[6,256,256]{2,1,0:T(8,128)(2,1)S(1)}, u32[]{:S(2)}, u32[]{:S(2)}) %collective-permute-start.9) | collective-permute-done | bytes 786464 | tf_op jit(solution)/shard_map/ppermute | solution.py:18
  108.1 3.2 %collective-permute-start.10 = (bf16[6,256,256]{2,1,0:T(8,128)(2,1)S(1)}, bf16[6,256,256]{2,1,0:T(8,128)(2,1)S(1)}, u32[]{:S(2)}, u32[]{:S(2)}) collective-permute-start(bf16[6,256,256]{2,1,0:T(8,128)(2,1)S(1)} %add_convert_fusion.2), channel_id=1, source_target_pairs={{0,8},{8,16},{16,24},{1,9},{9,17},{17,25},{2,10},{10,18},{18,26},{... | collective-permute-start | bytes 2359304 | tf_op jit(solution)/shard_map/ppermute | solution.py:18
  111.4 16.1 %collective-permute-done.10 = bf16[6,256,256]{2,1,0:T(8,128)(2,1)S(1)} collective-permute-done((bf16[6,256,256]{2,1,0:T(8,128)(2,1)S(1)}, bf16[6,256,256]{2,1,0:T(8,128)(2,1)S(1)}, u32[]{:S(2)}, u32[]{:S(2)}) %collective-permute-start.10) | collective-permute-done | bytes 786464 | tf_op jit(solution)/shard_map/ppermute | solution.py:18
  127.5 1.3 %maximum_bitcast_fusion = bf16[1,1,13,256,256]{4,3,2,1,0:T(8,128)(2,1)} fusion(bf16[6,256,256]{2,1,0:T(8,128)(2,1)S(1)} %collective-permute-done.10, bf16[7,256,256]{2,1,0:T(8,128)(2,1)S(1)} %collective-permute-done.6), kind=kLoop, calls=%fused_computation.2 | loop fusion | flops 851968 | bytes 3407872 | tf_op jit(solution)/shard_map/broadcast_in_dim | solution.py:210
  (22 shorter events, 3.0 us)
Async XLA Ops:
  0.0 26.4 %collective-permute-start = (bf16[13,256,256]{2,1,0:T(8,128)(2,1)}, bf16[13,256,256]{2,1,0:T(8,128)(2,1)S(1)}, u32[]{:S(2)}, u32[]{:S(2)}) collective-permute-start(bf16[13,256,256]{2,1,0:T(8,128)(2,1)} %bitcast.3), channel_id=1, source_target_pairs={{0,1},{1,2},{2,3},{4,5},{5,6},{6,7},{8,9},{9,10},{10,11},{12,13},{... | collective-permute-start | bytes 5111816 | tf_op jit(solution)/shard_map/ppermute | solution.py:23
  7.1 19.3 %collective-permute-start.1 = (bf16[2,256,256]{2,1,0:T(8,128)(2,1)}, bf16[2,256,256]{2,1,0:T(8,128)(2,1)S(1)}, u32[]{:S(2)}, u32[]{:S(2)}) collective-permute-start(bf16[2,256,256]{2,1,0:T(8,128)(2,1)} %get-tuple-element.24), channel_id=1, source_target_pairs={{0,1},{1,2},{2,3},{4,5},{5,6},{6,7},{8,9},{9,10},{10,11},{12,13},{... | collective-permute-start | bytes 786440 | tf_op jit(solution)/shard_map/ppermute | solution.py:23
  9.0 26.8 %collective-permute-start.2 = (bf16[2,256,256]{2,1,0:T(8,128)(2,1)}, bf16[2,256,256]{2,1,0:T(8,128)(2,1)S(1)}, u32[]{:S(2)}, u32[]{:S(2)}) collective-permute-start(bf16[2,256,256]{2,1,0:T(8,128)(2,1)} %get-tuple-element.28), channel_id=1, source_target_pairs={{4,0},{5,1},{6,2},{7,3},{12,8},{13,9},{14,10},{15,11},{20,16},{21,... | collective-permute-start | bytes 786440 | tf_op jit(solution)/shard_map/ppermute | solution.py:188
  26.4 0.7 copy-start.6
  26.4 1.3 copy-start.3
  35.8 0.7 copy-start.5
  56.7 19.8 %copy-start.4 = (bf16[6,256,256]{2,1,0:T(8,128)(2,1)S(1)}, bf16[6,256,256]{2,1,0:T(8,128)(2,1)}, u32[]{:S(2)}) copy-start(bf16[6,256,256]{2,1,0:T(8,128)(2,1)} %get-tuple-element.34) | copy-start | bytes 2359300
  56.7 24.4 %copy-start.2 = (bf16[6,256,256]{2,1,0:T(8,128)(2,1)S(1)}, bf16[6,256,256]{2,1,0:T(8,128)(2,1)}, u32[]{:S(2)}) copy-start(bf16[6,256,256]{2,1,0:T(8,128)(2,1)} %get-tuple-element.35) | copy-start | bytes 2359300
  56.7 15.0 %collective-permute-start.4 = (bf16[7,256,256]{2,1,0:T(8,128)(2,1)}, bf16[7,256,256]{2,1,0:T(8,128)(2,1)S(1)}, u32[]{:S(2)}, u32[]{:S(2)}) collective-permute-start(bf16[7,256,256]{2,1,0:T(8,128)(2,1)} %get-tuple-element.32), channel_id=1, source_target_pairs={{0,1},{1,2},{2,3},{4,5},{5,6},{6,7},{8,9},{9,10},{10,11},{12,13},{... | collective-permute-start | bytes 2752520 | tf_op jit(solution)/shard_map/ppermute | solution.py:23
  61.1 20.0 %collective-permute-start.8 = (bf16[6,256,256]{2,1,0:T(8,128)(2,1)}, bf16[6,256,256]{2,1,0:T(8,128)(2,1)S(1)}, u32[]{:S(2)}, u32[]{:S(2)}) collective-permute-start(bf16[6,256,256]{2,1,0:T(8,128)(2,1)} %get-tuple-element.36), channel_id=1, source_target_pairs={{0,1},{1,2},{2,3},{4,5},{5,6},{6,7},{8,9},{9,10},{10,11},{12,13},{... | collective-permute-start | bytes 2359304 | tf_op jit(solution)/shard_map/ppermute | solution.py:23
  63.1 27.0 %collective-permute-start.3 = (bf16[7,256,256]{2,1,0:T(8,128)(2,1)}, bf16[7,256,256]{2,1,0:T(8,128)(2,1)S(1)}, u32[]{:S(2)}, u32[]{:S(2)}) collective-permute-start(bf16[7,256,256]{2,1,0:T(8,128)(2,1)} %get-tuple-element.30), channel_id=1, source_target_pairs={{0,1},{1,2},{2,3},{4,5},{5,6},{6,7},{8,9},{9,10},{10,11},{12,13},{... | collective-permute-start | bytes 2752520 | tf_op jit(solution)/shard_map/ppermute | solution.py:23
  73.2 23.5 %copy-start = (bf16[7,256,256]{2,1,0:T(8,128)(2,1)S(1)}, bf16[7,256,256]{2,1,0:T(8,128)(2,1)}, u32[]{:S(2)}) copy-start(bf16[7,256,256]{2,1,0:T(8,128)(2,1)} %get-tuple-element.29) | copy-start | bytes 2752516
  73.2 23.5 %collective-permute-start.5 = (bf16[7,256,256]{2,1,0:T(8,128)(2,1)S(1)}, bf16[7,256,256]{2,1,0:T(8,128)(2,1)S(1)}, u32[]{:S(2)}, u32[]{:S(2)}) collective-permute-start(bf16[7,256,256]{2,1,0:T(8,128)(2,1)S(1)} %add_convert_fusion.1), channel_id=1, source_target_pairs={{0,4},{1,5},{2,6},{3,7},{8,12},{9,13},{10,14},{11,15},{16,20},{17,... | collective-permute-start | bytes 2752520 | tf_op jit(solution)/shard_map/ppermute | solution.py:18
  76.6 23.8 %collective-permute-start.7 = (bf16[6,256,256]{2,1,0:T(8,128)(2,1)S(1)}, bf16[6,256,256]{2,1,0:T(8,128)(2,1)S(1)}, u32[]{:S(2)}, u32[]{:S(2)}) collective-permute-start(bf16[6,256,256]{2,1,0:T(8,128)(2,1)S(1)} %copy-done.4), channel_id=1, source_target_pairs={{0,1},{1,2},{2,3},{4,5},{5,6},{6,7},{8,9},{9,10},{10,11},{12,13},{... | collective-permute-start | bytes 2359304 | tf_op jit(solution)/shard_map/ppermute | solution.py:23
  81.4 26.4 %collective-permute-start.9 = (bf16[6,256,256]{2,1,0:T(8,128)(2,1)S(1)}, bf16[6,256,256]{2,1,0:T(8,128)(2,1)S(1)}, u32[]{:S(2)}, u32[]{:S(2)}) collective-permute-start(bf16[6,256,256]{2,1,0:T(8,128)(2,1)S(1)} %add_convert_fusion.3), channel_id=1, source_target_pairs={{0,4},{1,5},{2,6},{3,7},{8,12},{9,13},{10,14},{11,15},{16,20},{17,... | collective-permute-start | bytes 2359304 | tf_op jit(solution)/shard_map/ppermute | solution.py:18
  96.7 11.0 %copy-start.1 = (bf16[6,256,256]{2,1,0:T(8,128)(2,1)S(1)}, bf16[6,256,256]{2,1,0:T(8,128)(2,1)}, u32[]{:S(2)}) copy-start(bf16[6,256,256]{2,1,0:T(8,128)(2,1)} %get-tuple-element.33) | copy-start | bytes 2359300
  97.1 30.4 %collective-permute-start.6 = (bf16[7,256,256]{2,1,0:T(8,128)(2,1)S(1)}, bf16[7,256,256]{2,1,0:T(8,128)(2,1)S(1)}, u32[]{:S(2)}, u32[]{:S(2)}) collective-permute-start(bf16[7,256,256]{2,1,0:T(8,128)(2,1)S(1)} %add_convert_fusion), channel_id=1, source_target_pairs={{0,8},{8,16},{16,24},{1,9},{9,17},{17,25},{2,10},{10,18},{18,26},{... | collective-permute-start | bytes 2752520 | tf_op jit(solution)/shard_map/ppermute | solution.py:18
  108.1 19.4 %collective-permute-start.10 = (bf16[6,256,256]{2,1,0:T(8,128)(2,1)S(1)}, bf16[6,256,256]{2,1,0:T(8,128)(2,1)S(1)}, u32[]{:S(2)}, u32[]{:S(2)}) collective-permute-start(bf16[6,256,256]{2,1,0:T(8,128)(2,1)S(1)} %add_convert_fusion.2), channel_id=1, source_target_pairs={{0,8},{8,16},{16,24},{1,9},{9,17},{17,25},{2,10},{10,18},{18,26},{... | collective-permute-start | bytes 2359304 | tf_op jit(solution)/shard_map/ppermute | solution.py:18

commit v3 on v1

v3 whole, which is shorter than its diff:
```python
import jax
import jax.numpy as jnp
from jax import lax
from jax.experimental import pallas as pl
from jax.experimental.pallas import tpu as pltpu
from jax.sharding import PartitionSpec as P

ND = 4
ROWS = 16
PARTS = 4
LAG = 2
VMEM_BYTES = 56 * 2**20


def from_behind(shard, axis, by):
    count = lax.axis_size(axis)
    pairs = [(i, i + by) for i in range(count) if 0 <= i + by < count]
    return lax.ppermute(shard, axis, pairs)


def shift_column(shard):
    count = lax.axis_size("sec")
    return lax.ppermute(shard, "sec", [(q, q + 1) for q in range(count - 1) if q % ND < ND - 1])


TAKEN = ((0, (2, 3)), (1, (0, 2)), (0, (0, 1)), (1, (0, 1, 2, 3)))


def prepare_kernel(site_ref, mask_ref, dims_ref, mpo_ref, mixer_ref, *out_refs):
    cap = site_ref.shape[-1]
    total = dims_ref.shape[0]
    q = lax.axis_index("sec")
    rows = lax.broadcasted_iota(jnp.int32, (cap, cap), 0)
    columns = lax.broadcasted_iota(jnp.int32, (cap, cap), 1)
    own = rows < dims_ref[q]
    for out_ref, (site, states) in zip(out_refs, TAKEN):
        for place, s in enumerate(states):
            target = q + (0, ND, 1, ND + 1)[s]
            allowed = (mask_ref[site, 0, s] > 0) & (target < total)
            if s >= 2:
                allowed = allowed & (q % ND < ND - 1)
            width = jnp.where(allowed, dims_ref[jnp.minimum(target, total - 1)], 0)
            out_ref[place] = jnp.where(own & (columns < width), site_ref[site, 0, s], 0).astype(jnp.bfloat16)
    sites, states, channels, _ = mpo_ref.shape
    span = channels * ROWS
    spread = (
        lax.broadcasted_iota(jnp.int32, (span, channels), 0) // ROWS
        == lax.broadcasted_iota(jnp.int32, (span, channels), 1)
    ).astype(jnp.bfloat16)
    same_row = (
        lax.broadcasted_iota(jnp.int32, (span, span), 0) % ROWS
        == lax.broadcasted_iota(jnp.int32, (span, span), 1) % ROWS
    )
    contract_last = (((1,), (1,)), ((), ()))
    for site in range(sites):
        for s in range(states):
            tall = lax.dot_general(spread, mpo_ref[site, s], contract_last, preferred_element_type=jnp.float32)
            wide = lax.dot_general(
                tall.astype(jnp.bfloat16), spread, contract_last, preferred_element_type=jnp.float32
            )
            mixer_ref[site, s] = jnp.where(same_row, wide, 0.0).astype(jnp.bfloat16)


def prepare(site_block_tensors, block_mask, sector_dims, mpo_tensors):
    cap = site_block_tensors.shape[-1]
    span = mpo_tensors.shape[-1] * ROWS
    vmem, smem = pl.BlockSpec(memory_space=pltpu.VMEM), pl.BlockSpec(memory_space=pltpu.SMEM)
    return pl.pallas_call(
        prepare_kernel,
        out_shape=[jax.ShapeDtypeStruct((*mpo_tensors.shape[:2], span, span), jnp.bfloat16)]
        + [jax.ShapeDtypeStruct((len(states), cap, cap), jnp.bfloat16) for _, states in TAKEN],
        in_specs=[vmem, smem, smem, vmem],
        out_specs=[vmem] * (1 + len(TAKEN)),
        compiler_params=pltpu.CompilerParams(vmem_limit_bytes=VMEM_BYTES),
        cost_estimate=pl.CostEstimate(flops=10**6, bytes_accessed=2 * 2**20, transcendentals=0),
    )(site_block_tensors, block_mask, sector_dims, mpo_tensors)


def mix(mixer_ref, site, states, env_ref, mixed_ref):
    channels, cap, _ = env_ref.shape
    for g in range(0, cap, ROWS):
        piece = env_ref[:, g:g + ROWS, :].reshape(channels * ROWS, cap)
        for k, state in enumerate(states):
            mixed = jnp.dot(mixer_ref[site, state], piece, preferred_element_type=jnp.float32)
            mixed_ref[k, :, g:g + ROWS, :] = mixed.astype(jnp.bfloat16).reshape(channels, ROWS, cap)


def add_products(terms, v, total=None):
    for mixed_ref, block, flipped in terms:
        blended = jnp.dot(mixed_ref[v], block[...], preferred_element_type=jnp.float32).astype(jnp.bfloat16)
        one = jnp.dot(flipped[...], blended, preferred_element_type=jnp.float32)
        total = one if total is None else total + one
    return total.astype(jnp.bfloat16)


def own_kernel(env_ref, mixer_ref, block_ref, own_ref, below_ref, mixed_ref, flipped_ref):
    for k in range(2):
        flipped_ref[k] = block_ref[k].T
    mix(mixer_ref, 0, (0, 1), env_ref, mixed_ref)
    for k, out_ref in enumerate((own_ref, below_ref)):
        for v in range(env_ref.shape[0]):
            out_ref[v] = add_products([(mixed_ref.at[k], block_ref.at[k], flipped_ref.at[k])], v)


def up_kernel(
    near_ref, own_ref, own_below_ref, mixer_ref, near_block_ref, last_ref, column_ref,
    middle_ref, middle_below_ref, *refs,
):
    up_refs, (mixed_ref, mixed_below_ref, flipped_ref) = refs[:-3], refs[-3:]
    channels = near_ref.shape[0]
    for k, block in enumerate((near_block_ref.at[0], near_block_ref.at[1], last_ref.at[2], last_ref.at[3], column_ref.at[1])):
        flipped_ref[k] = block[...].T
    mix(mixer_ref, 0, (2, 3), near_ref, mixed_ref)
    for k, (out_ref, base_ref) in enumerate(((middle_ref, own_ref), (middle_below_ref, own_below_ref))):
        for v in range(channels):
            term = (mixed_ref.at[k], near_block_ref.at[k], flipped_ref.at[k])
            out_ref[v] = add_products([term], v, base_ref[v].astype(jnp.float32))
    mix(mixer_ref, 1, (2, 3), middle_ref, mixed_ref)
    mix(mixer_ref, 1, (2,), middle_below_ref, mixed_below_ref)
    same = [(mixed_ref.at[0], last_ref.at[2], flipped_ref.at[2])]
    down = [
        (mixed_ref.at[1], last_ref.at[3], flipped_ref.at[3]),
        (mixed_below_ref.at[0], column_ref.at[1], flipped_ref.at[4]),
    ]
    v = 0
    for out_ref in up_refs:
        width = out_ref.shape[0] // 2
        for place in range(width):
            out_ref[place] = add_products(down, v + place)
        for place in range(width):
            out_ref[width + place] = add_products(same, v + place)
        v += width


def stay_kernel(middle_ref, middle_below_ref, mixer_ref, last_ref, column_ref, *refs):
    out_refs, (mixed_ref, mixed_below_ref, flipped_ref) = refs[:-3], refs[-3:]
    for k, block in enumerate((last_ref.at[0], last_ref.at[1], column_ref.at[0])):
        flipped_ref[k] = block[...].T
    mix(mixer_ref, 1, (0, 1), middle_ref, mixed_ref)
    mix(mixer_ref, 1, (0,), middle_below_ref, mixed_below_ref)
    same = [(mixed_ref.at[0], last_ref.at[0], flipped_ref.at[0])]
    down = [
        (mixed_ref.at[1], last_ref.at[1], flipped_ref.at[1]),
        (mixed_below_ref.at[0], column_ref.at[0], flipped_ref.at[2]),
    ]
    v = 0
    for out_ref in out_refs:
        width = out_ref.shape[0] // 2
        for place in range(width):
            out_ref[place] = add_products(down, v + place)
        for place in range(width):
            out_ref[width + place] = add_products(same, v + place)
        v += width


def call(kernel, operands, widths, mixed, flipped, work):
    channels, cap, _ = operands[0].shape
    return pl.pallas_call(
        kernel,
        out_shape=[jax.ShapeDtypeStruct((width, cap, cap), jnp.bfloat16) for width in widths],
        in_specs=[pl.BlockSpec(memory_space=pltpu.VMEM)] * len(operands),
        out_specs=[pl.BlockSpec(memory_space=pltpu.VMEM)] * len(widths),
        scratch_shapes=[pltpu.VMEM((n, channels, cap, cap), jnp.bfloat16) for n in mixed]
        + [pltpu.VMEM((flipped, cap, cap), jnp.bfloat16)],
        compiler_params=pltpu.CompilerParams(vmem_limit_bytes=VMEM_BYTES),
        cost_estimate=pl.CostEstimate(
            flops=6 * work * channels * cap**3, bytes_accessed=4 * 2**20, transcendentals=0
        ),
    )(*operands)


def masked_blocks(site_block_tensors, block_mask, sector_dims):
    capacity = site_block_tensors.shape[-1]
    sector_total = lax.axis_size("sec")
    sector_id = lax.axis_index("sec")
    offsets = jnp.array([0, ND, 1, ND + 1])
    down_step = jnp.array([0, 0, 1, 1])
    targets = sector_id + offsets
    allowed = (targets < sector_total) & ((down_step == 0) | (sector_id % ND < ND - 1))
    sectors = jnp.arange(sector_total)
    own_dims = jnp.sum(jnp.where(sectors == sector_id, sector_dims, 0))
    target_dims = jnp.sum(
        jnp.where(sectors[None, :] == targets[:, None], sector_dims[None, :], 0), axis=1
    )
    target_dims = jnp.where(allowed, target_dims, 0)
    line = jnp.arange(capacity)
    row_live = line < own_dims
    col_live = line[None, :] < target_dims[:, None]
    present = (block_mask[:, 0] * allowed.astype(jnp.int32)).astype(jnp.bfloat16)
    live = row_live[None, :, None] & col_live[:, None, :]
    return jnp.where(live[None], site_block_tensors[:, 0] * present[:, :, None, None], 0)


def after(value, *others):
    return lax.optimization_barrier((value, *others))[0]


def cut(count, parts):
    edges = [-(-count * k // parts) for k in range(parts + 1)]
    return list(zip(edges[:-1], edges[1:]))


def wide_add(*terms):
    total = terms[0].astype(jnp.float32)
    for term in terms[1:]:
        total = total + term.astype(jnp.float32)
    return total.astype(jnp.bfloat16)


def two_rows(boundary_env, site_block_tensors, mpo_tensors, block_mask, sector_dims):
    env = boundary_env[0, 0]
    channels = env.shape[0]
    near_env = shift_column(env)
    mixers, up_blocks, column_blocks, first_blocks, last_blocks = prepare(
        site_block_tensors, block_mask, sector_dims, mpo_tensors
    )
    near_blocks = shift_column(up_blocks)
    column = lax.ppermute(column_blocks, "sec", [(ND + j, j) for j in range(ND)])
    own, own_below = call(own_kernel, (env, mixers, first_blocks), (channels,) * 2, (2,), 2, 2)
    pairs = [2 * (high - low) for low, high in cut(channels, PARTS)]
    middle, middle_below, *up = call(
        up_kernel, (near_env, own, own_below, mixers, near_blocks, last_blocks, column),
        (channels, channels, *pairs), (2, 1), 5, 5,
    )
    arrived = [shift_column(x) for x in up]
    stay = call(stay_kernel, (middle, middle_below, mixers, last_blocks, column), pairs, (2, 1), 3, 3)
    below, handed, last = [], [], None
    for step in range(PARTS + LAG):
        if step < PARTS:
            width = pairs[step] // 2
            there = arrived[step] if last is None else after(arrived[step], last)
            last = wide_add(stay[step][:width], there[:width])
            below.append(from_behind(last, "sec", ND))
        if step >= LAG:
            part = step - LAG
            width = pairs[part] // 2
            last = wide_add(stay[part][width:], arrived[part][width:], after(below[part], last))
            handed.append(from_behind(last, "seg", 1))
    return jnp.concatenate(handed)[None, None]


def contract(left_environ_tensor, block_list, weight_factors):
    merged_mixture = jnp.einsum(
        "umi,ue->emi", left_environ_tensor, weight_factors, preferred_element_type=jnp.float32
    ).astype(jnp.bfloat16)
    combined_mixture = jnp.einsum(
        "gip,pq->giq", merged_mixture, block_list, preferred_element_type=jnp.float32
    ).astype(jnp.bfloat16)
    return jnp.einsum(
        "ba,vbc->vac", block_list, combined_mixture, preferred_element_type=jnp.float32
    ).astype(jnp.bfloat16)


def any_rows(boundary_env, site_block_tensors, mpo_tensors, block_mask, sector_dims):
    blocks = masked_blocks(site_block_tensors, block_mask, sector_dims)
    env = boundary_env[0, 0]
    for n in range(blocks.shape[0]):
        parts = [contract(env, blocks[n, s], mpo_tensors[n, s]) for s in range(4)]
        total = parts[0].astype(jnp.float32) + from_behind(parts[1], "sec", ND).astype(jnp.float32)
        total = total + from_behind(parts[2], "sec", 1).astype(jnp.float32)
        total = total + from_behind(parts[3], "sec", ND + 1).astype(jnp.float32)
        env = total.astype(jnp.bfloat16)
    return from_behind(env, "seg", 1)[None, None]


def solution(mesh):
    in_specs = (
        P("seg", "sec", None, None, None),
        P("seg", "sec", None, None, None),
        P("seg", None, None, None),
        P("seg", "sec", None),
        P(),
    )
    out_specs = P("seg", "sec", None, None, None)
    body = two_rows if mesh.shape["sec"] == 2 * ND else any_rows
    return jax.shard_map(body, mesh=mesh, in_specs=in_specs, out_specs=out_specs, check_vma=False)
```

time: 182 us -> 117 us (0.64); the launches traced: 179 us -> 117 us
  Pallas kernels: 57.4 us -> 30.1 us
  local copies, waits for them, and re-layouts: 24.1 us -> 2.73 us
  other arithmetic: 19.9 us -> 3.64 us
  starting transfers between devices: 41.1 us -> 44.9 us
    pallas_call x5 -> x4, Pallas kernels: 57.4 us -> 30.1 us  [the longest x3 26.7 us: call(): pl.pallas_call(kernel, out_shape=[jax.ShapeDtypeStruct((width, cap, cap),...]
    reshape x10 -> x0, local copies, waits for them, and re-layouts: 15.3 us -> none  [mixer(): jnp.concatenate([wide[n][s, low:high] for s in states]).reshape(-1, span)]
    ppermute x8, waiting for transfers between devices: 33.2 us -> 20.6 us  [from_behind(): return lax.ppermute(shard, axis, pairs)]
    ppermute x6, waiting for transfers between devices: 2.41 us -> 14.6 us  [shift_column(): lax.ppermute(shard, 'sec', [(q, q + 1) for q in range(count - 1) if q % N...]
    concatenate x9 -> x0, other arithmetic: 9.57 us -> none  [the longest x7 5.88 us: mixer(): jnp.concatenate([wide[n][s, low:high] for s in states]).reshape(-1, span)]
    squeeze x6 -> x0, local copies, waits for them, and re-layouts: 7.42 us -> none  [the longest x1 4.08 us: two_rows(): middle[1]]
    ppermute x6, starting transfers between devices: 14.2 us -> 18.5 us  [shift_column(): lax.ppermute(shard, 'sec', [(q, q + 1) for q in range(count - 1) if q % N...]
    select_n x2 -> x0, other arithmetic: 2.13 us -> none  [the longest x1 1.46 us: masked_blocks(): jnp.where(live[None], site_block_tensors[:, 0] * present[:, :, None, None...]
  transfers between devices with their start and end apart: 15 -> 15, of which waited for: 4 -> 7; matrix products, arithmetic and copies ran while one was open for 16% -> 3% of each run, Pallas kernels for 18% -> 15%
where the time goes in v3:
time: 117 us
  starting transfers between devices  44.9 us (38%)
  waiting for transfers between devices  35.2 us (30%)
  Pallas kernels  30.1 us (26%)
  other arithmetic  3.64 us (3%)
  local copies, waits for them, and re-layouts  2.73 us (2%)
    pallas_call x3, Pallas kernels, call(): pl.pallas_call(kernel, out_shape=[jax.ShapeDtypeStruct((width, cap, cap),...  26.7 us
    ppermute x8, starting transfers between devices, from_behind(): return lax.ppermute(shard, axis, pairs)  25.1 us
    ppermute x8, waiting for transfers between devices, from_behind(): return lax.ppermute(shard, axis, pairs)  20.6 us
    ppermute x6, starting transfers between devices, shift_column(): lax.ppermute(shard, 'sec', [(q, q + 1) for q in range(count - 1) if q % N...  18.5 us
    ppermute x6, waiting for transfers between devices, shift_column(): lax.ppermute(shard, 'sec', [(q, q + 1) for q in range(count - 1) if q % N...  14.6 us
    pallas_call x1, Pallas kernels, prepare(): pl.pallas_call(prepare_kernel, out_shape=[jax.ShapeDtypeStruct((*mpo_tens...  3.38 us
    unnamed x17, local copies, waits for them, and re-layouts  2.73 us
  transfers between devices with their start and end apart: 15, of which 7 were waited for; matrix products, arithmetic and copies ran while one was open for 3% of the time, Pallas kernels for 15%

profile of v3, /device:TPU:1, one launch (start us, length us, event | category | flops | bytes accessed | tf_op | source)
XLA Modules:
  0.0 116.8 jit_solution(2114374045009766595)
XLA Ops:
  0.0 4.5 %collective-permute-start = (bf16[13,256,256]{2,1,0:T(8,128)(2,1)}, bf16[13,256,256]{2,1,0:T(8,128)(2,1)S(1)}, u32[]{:S(2)}, u32[]{:S(2)}) collective-permute-start(bf16[13,256,256]{2,1,0:T(8,128)(2,1)} %bitcast.3), channel_id=1, source_target_pairs={{0,1},{1,2},{2,3},{4,5},{5,6},{6,7},{8,9},{9,10},{10,11},{12,13},{... | collective-permute-start | bytes 5111816 | tf_op jit(solution)/shard_map/ppermute | solution.py:23
  5.9 3.4 %shard_map.55 = (bf16[2,4,208,208]{3,2,1,0:T(8,128)(2,1)}, bf16[2,256,256]{2,1,0:T(8,128)(2,1)}, bf16[2,256,256]{2,1,0:T(8,128)(2,1)}, bf16[2,256,256]{2,1,0:T(8,128)(2,1)}, bf16[4,256,256]{2,1,0:T(8,128)(2,1)}) custom-call(bf16[2,1,4,256,256]{4,3,2,1,0:T(8,128)(2,1)} %site_ref.1, s32[2,1,4]{2,1,0:T(1,128)} %mask_ref.1, s32[8]{0:T(128)} %dims_ref.1, ...), custom_call_target="tpu_custom_call" | custom-call | flops 1000000 | bytes 2097152 | tf_op jit(solution)/shard_map/pallas_call | solution.py:68
  9.3 1.9 %collective-permute-start.1 = (bf16[2,256,256]{2,1,0:T(8,128)(2,1)}, bf16[2,256,256]{2,1,0:T(8,128)(2,1)S(1)}, u32[]{:S(2)}, u32[]{:S(2)}) collective-permute-start(bf16[2,256,256]{2,1,0:T(8,128)(2,1)} %get-tuple-element.33), channel_id=1, source_target_pairs={{0,1},{1,2},{2,3},{4,5},{5,6},{6,7},{8,9},{9,10},{10,11},{12,13},{... | collective-permute-start | bytes 786440 | tf_op jit(solution)/shard_map/ppermute | solution.py:23
  12.5 5.9 %shard_map.56 = (bf16[13,256,256]{2,1,0:T(8,128)(2,1)}, bf16[13,256,256]{2,1,0:T(8,128)(2,1)}) custom-call(bf16[13,256,256]{2,1,0:T(8,128)(2,1)} %bitcast.4, bf16[2,4,208,208]{3,2,1,0:T(8,128)(2,1)} %get-tuple-element.29.mixer_ref, bf16[2,256,256]{2,1,0:T(8,128)(2,1)} %get-tuple-element.30.block_ref), custom_call_target="tpu_custom_call" | custom-call | flops 2617245696 | bytes 4194304 | tf_op jit(solution)/shard_map/pallas_call | solution.py:158
  18.4 8.0 %collective-permute-done.1.near_block_ref = bf16[2,256,256]{2,1,0:T(8,128)(2,1)S(1)} collective-permute-done((bf16[2,256,256]{2,1,0:T(8,128)(2,1)}, bf16[2,256,256]{2,1,0:T(8,128)(2,1)S(1)}, u32[]{:S(2)}, u32[]{:S(2)}) %collective-permute-start.1) | collective-permute-done | bytes 262176 | tf_op jit(solution)/shard_map/ppermute | solution.py:23
  27.7 12.1 %shard_map.57 = (bf16[13,256,256]{2,1,0:T(8,128)(2,1)}, bf16[13,256,256]{2,1,0:T(8,128)(2,1)}, bf16[8,256,256]{2,1,0:T(8,128)(2,1)}, bf16[6,256,256]{2,1,0:T(8,1...) custom-call(bf16[13,256,256]{2,1,0:T(8,128)(2,1)} %copy-done.4, ...), custom_call_target="tpu_custom_call" | custom-call | flops 6543114240 | bytes 4194304 | tf_op jit(solution)/shard_map/pallas_call | solution.py:158
  39.8 4.3 %collective-permute-start.3 = (bf16[8,256,256]{2,1,0:T(8,128)(2,1)}, bf16[8,256,256]{2,1,0:T(8,128)(2,1)S(1)}, u32[]{:S(2)}, u32[]{:S(2)}) collective-permute-start(bf16[8,256,256]{2,1,0:T(8,128)(2,1)} %get-tuple-element.39), channel_id=1, source_target_pairs={{0,1},{1,2},{2,3},{4,5},{5,6},{6,7},{8,9},{9,10},{10,11},{12,13},{... | collective-permute-start | bytes 3145736 | tf_op jit(solution)/shard_map/ppermute | solution.py:23
  44.1 1.9 %collective-permute-start.6 = (bf16[6,256,256]{2,1,0:T(8,128)(2,1)}, bf16[6,256,256]{2,1,0:T(8,128)(2,1)S(1)}, u32[]{:S(2)}, u32[]{:S(2)}) collective-permute-start(bf16[6,256,256]{2,1,0:T(8,128)(2,1)} %get-tuple-element.43), channel_id=1, source_target_pairs={{0,1},{1,2},{2,3},{4,5},{5,6},{6,7},{8,9},{9,10},{10,11},{12,13},{... | collective-permute-start | bytes 2359304 | tf_op jit(solution)/shard_map/ppermute | solution.py:23
  46.0 2.1 %collective-permute-start.5 = (bf16[6,256,256]{2,1,0:T(8,128)(2,1)}, bf16[6,256,256]{2,1,0:T(8,128)(2,1)S(1)}, u32[]{:S(2)}, u32[]{:S(2)}) collective-permute-start(bf16[6,256,256]{2,1,0:T(8,128)(2,1)} %get-tuple-element.41), channel_id=1, source_target_pairs={{0,1},{1,2},{2,3},{4,5},{5,6},{6,7},{8,9},{9,10},{10,11},{12,13},{... | collective-permute-start | bytes 2359304 | tf_op jit(solution)/shard_map/ppermute | solution.py:23
  48.1 8.7 %shard_map.58 = (bf16[8,256,256]{2,1,0:T(8,128)(2,1)}, bf16[6,256,256]{2,1,0:T(8,128)(2,1)}, bf16[6,256,256]{2,1,0:T(8,128)(2,1)}, bf16[6,256,256]{2,1,0:T(8,128)(2,1)}) custom-call(bf16[13,256,256]{2,1,0:T(8,128)(2,1)} %get-tuple-element.36.middle_ref, bf16[13,256,256]{2,1,0:T(8,128)(2,1)} %get-tuple-element.37.middle_below_ref, ...), custom_call_target="tpu_custom_call" | custom-call | flops 3925868544 | bytes 4194304 | tf_op jit(solution)/shard_map/pallas_call | solution.py:158
  58.2 3.2 %collective-permute-start.4 = (bf16[4,256,256]{2,1,0:T(8,128)(2,1)S(1)}, bf16[4,256,256]{2,1,0:T(8,128)(2,1)S(1)}, u32[]{:S(2)}, u32[]{:S(2)}) collective-permute-start(bf16[4,256,256]{2,1,0:T(8,128)(2,1)S(1)} %add_convert_fusion.1), channel_id=1, source_target_pairs={{0,4},{1,5},{2,6},{3,7},{8,12},{9,13},{10,14},{11,15},{16,20},{17,... | collective-permute-start | bytes 1572872 | tf_op jit(solution)/shard_map/ppermute | solution.py:18
  61.4 3.8 %collective-permute-start.9 = (bf16[6,256,256]{2,1,0:T(8,128)(2,1)S(1)}, bf16[6,256,256]{2,1,0:T(8,128)(2,1)S(1)}, u32[]{:S(2)}, u32[]{:S(2)}) collective-permute-start(bf16[6,256,256]{2,1,0:T(8,128)(2,1)S(1)} %copy-done.5), channel_id=1, source_target_pairs={{0,1},{1,2},{2,3},{4,5},{5,6},{6,7},{8,9},{9,10},{10,11},{12,13},{... | collective-permute-start | bytes 2359304 | tf_op jit(solution)/shard_map/ppermute | solution.py:23
  65.3 2.7 %collective-permute-start.8 = (bf16[3,256,256]{2,1,0:T(8,128)(2,1)S(1)}, bf16[3,256,256]{2,1,0:T(8,128)(2,1)S(1)}, u32[]{:S(2)}, u32[]{:S(2)}) collective-permute-start(bf16[3,256,256]{2,1,0:T(8,128)(2,1)S(1)} %add_convert_fusion.7), channel_id=1, source_target_pairs={{0,4},{1,5},{2,6},{3,7},{8,12},{9,13},{10,14},{11,15},{16,20},{17,... | collective-permute-start | bytes 1179656 | tf_op jit(solution)/shard_map/ppermute | solution.py:18
  68.0 5.0 %collective-permute-done.5 = bf16[6,256,256]{2,1,0:T(8,128)(2,1)S(1)} collective-permute-done((bf16[6,256,256]{2,1,0:T(8,128)(2,1)}, bf16[6,256,256]{2,1,0:T(8,128)(2,1)S(1)}, u32[]{:S(2)}, u32[]{:S(2)}) %collective-permute-start.5) | collective-permute-done | bytes 786464 | tf_op jit(solution)/shard_map/ppermute | solution.py:23
  73.1 3.2 %collective-permute-start.11 = (bf16[3,256,256]{2,1,0:T(8,128)(2,1)S(1)}, bf16[3,256,256]{2,1,0:T(8,128)(2,1)S(1)}, u32[]{:S(2)}, u32[]{:S(2)}) collective-permute-start(bf16[3,256,256]{2,1,0:T(8,128)(2,1)S(1)} %add_convert_fusion.6), channel_id=1, source_target_pairs={{0,4},{1,5},{2,6},{3,7},{8,12},{9,13},{10,14},{11,15},{16,20},{17,... | collective-permute-start | bytes 1179656 | tf_op jit(solution)/shard_map/ppermute | solution.py:18
  76.5 3.2 %collective-permute-start.7 = (bf16[4,256,256]{2,1,0:T(8,128)(2,1)S(1)}, bf16[4,256,256]{2,1,0:T(8,128)(2,1)S(1)}, u32[]{:S(2)}, u32[]{:S(2)}) collective-permute-start(bf16[4,256,256]{2,1,0:T(8,128)(2,1)S(1)} %add_convert_fusion), channel_id=1, source_target_pairs={{0,8},{8,16},{16,24},{1,9},{9,17},{17,25},{2,10},{10,18},{18,26},{... | collective-permute-start | bytes 1572872 | tf_op jit(solution)/shard_map/ppermute | solution.py:18
  79.7 1.6 %collective-permute-done.9 = bf16[6,256,256]{2,1,0:T(8,128)(2,1)S(1)} collective-permute-done((bf16[6,256,256]{2,1,0:T(8,128)(2,1)S(1)}, bf16[6,256,256]{2,1,0:T(8,128)(2,1)S(1)}, u32[]{:S(2)}, u32[]{:S(2)}) %collective-permute-start.9) | collective-permute-done | bytes 786464 | tf_op jit(solution)/shard_map/ppermute | solution.py:23
  81.4 3.2 %collective-permute-start.13 = (bf16[3,256,256]{2,1,0:T(8,128)(2,1)S(1)}, bf16[3,256,256]{2,1,0:T(8,128)(2,1)S(1)}, u32[]{:S(2)}, u32[]{:S(2)}) collective-permute-start(bf16[3,256,256]{2,1,0:T(8,128)(2,1)S(1)} %add_convert_fusion.5), channel_id=1, source_target_pairs={{0,4},{1,5},{2,6},{3,7},{8,12},{9,13},{10,14},{11,15},{16,20},{17,... | collective-permute-start | bytes 1179656 | tf_op jit(solution)/shard_map/ppermute | solution.py:18
  84.7 3.2 %collective-permute-start.10 = (bf16[3,256,256]{2,1,0:T(8,128)(2,1)S(1)}, bf16[3,256,256]{2,1,0:T(8,128)(2,1)S(1)}, u32[]{:S(2)}, u32[]{:S(2)}) collective-permute-start(bf16[3,256,256]{2,1,0:T(8,128)(2,1)S(1)} %add_convert_fusion.4), channel_id=1, source_target_pairs={{0,8},{8,16},{16,24},{1,9},{9,17},{17,25},{2,10},{10,18},{18,26},{... | collective-permute-start | bytes 1179656 | tf_op jit(solution)/shard_map/ppermute | solution.py:18
  89.0 3.2 %collective-permute-start.12 = (bf16[3,256,256]{2,1,0:T(8,128)(2,1)S(1)}, bf16[3,256,256]{2,1,0:T(8,128)(2,1)S(1)}, u32[]{:S(2)}, u32[]{:S(2)}) collective-permute-start(bf16[3,256,256]{2,1,0:T(8,128)(2,1)S(1)} %add_convert_fusion.3), channel_id=1, source_target_pairs={{0,8},{8,16},{16,24},{1,9},{9,17},{17,25},{2,10},{10,18},{18,26},{... | collective-permute-start | bytes 1179656 | tf_op jit(solution)/shard_map/ppermute | solution.py:18
  92.3 5.0 %collective-permute-done.13 = bf16[3,256,256]{2,1,0:T(8,128)(2,1)S(1)} collective-permute-done((bf16[3,256,256]{2,1,0:T(8,128)(2,1)S(1)}, bf16[3,256,256]{2,1,0:T(8,128)(2,1)S(1)}, u32[]{:S(2)}, u32[]{:S(2)}) %collective-permute-start.13) | collective-permute-done | bytes 393248 | tf_op jit(solution)/shard_map/ppermute | solution.py:18
  97.5 3.2 %collective-permute-start.14 = (bf16[3,256,256]{2,1,0:T(8,128)(2,1)S(1)}, bf16[3,256,256]{2,1,0:T(8,128)(2,1)S(1)}, u32[]{:S(2)}, u32[]{:S(2)}) collective-permute-start(bf16[3,256,256]{2,1,0:T(8,128)(2,1)S(1)} %add_convert_fusion.2), channel_id=1, source_target_pairs={{0,8},{8,16},{16,24},{1,9},{9,17},{17,25},{2,10},{10,18},{18,26},{... | collective-permute-start | bytes 1179656 | tf_op jit(solution)/shard_map/ppermute | solution.py:18
  100.7 7.6 %collective-permute-done.12 = bf16[3,256,256]{2,1,0:T(8,128)(2,1)S(1)} collective-permute-done((bf16[3,256,256]{2,1,0:T(8,128)(2,1)S(1)}, bf16[3,256,256]{2,1,0:T(8,128)(2,1)S(1)}, u32[]{:S(2)}, u32[]{:S(2)}) %collective-permute-start.12) | collective-permute-done | bytes 393248 | tf_op jit(solution)/shard_map/ppermute | solution.py:18
  108.3 7.0 %collective-permute-done.14 = bf16[3,256,256]{2,1,0:T(8,128)(2,1)S(1)} collective-permute-done((bf16[3,256,256]{2,1,0:T(8,128)(2,1)S(1)}, bf16[3,256,256]{2,1,0:T(8,128)(2,1)S(1)}, u32[]{:S(2)}, u32[]{:S(2)}) %collective-permute-start.14) | collective-permute-done | bytes 393248 | tf_op jit(solution)/shard_map/ppermute | solution.py:18
  (36 shorter events, 8.6 us)
Async XLA Ops:
  0.0 26.4 %collective-permute-start = (bf16[13,256,256]{2,1,0:T(8,128)(2,1)}, bf16[13,256,256]{2,1,0:T(8,128)(2,1)S(1)}, u32[]{:S(2)}, u32[]{:S(2)}) collective-permute-start(bf16[13,256,256]{2,1,0:T(8,128)(2,1)} %bitcast.3), channel_id=1, source_target_pairs={{0,1},{1,2},{2,3},{4,5},{5,6},{6,7},{8,9},{9,10},{10,11},{12,13},{... | collective-permute-start | bytes 5111816 | tf_op jit(solution)/shard_map/ppermute | solution.py:23
  9.3 17.1 %collective-permute-start.1 = (bf16[2,256,256]{2,1,0:T(8,128)(2,1)}, bf16[2,256,256]{2,1,0:T(8,128)(2,1)S(1)}, u32[]{:S(2)}, u32[]{:S(2)}) collective-permute-start(bf16[2,256,256]{2,1,0:T(8,128)(2,1)} %get-tuple-element.33), channel_id=1, source_target_pairs={{0,1},{1,2},{2,3},{4,5},{5,6},{6,7},{8,9},{9,10},{10,11},{12,13},{... | collective-permute-start | bytes 786440 | tf_op jit(solution)/shard_map/ppermute | solution.py:23
  11.2 15.2 %collective-permute-start.2 = (bf16[2,256,256]{2,1,0:T(8,128)(2,1)}, bf16[2,256,256]{2,1,0:T(8,128)(2,1)S(1)}, u32[]{:S(2)}, u32[]{:S(2)}) collective-permute-start(bf16[2,256,256]{2,1,0:T(8,128)(2,1)} %get-tuple-element.35), channel_id=1, source_target_pairs={{4,0},{5,1},{6,2},{7,3},{12,8},{13,9},{14,10},{15,11},{20,16},{21,... | collective-permute-start | bytes 786440 | tf_op jit(solution)/shard_map/ppermute | solution.py:218
  26.4 0.7 copy-start.7
  26.4 0.8 copy-start.6
  26.4 1.3 %copy-start.4 = (bf16[13,256,256]{2,1,0:T(8,128)(2,1)}, bf16[13,256,256]{2,1,0:T(8,128)(2,1)S(1)}, u32[]{:S(2)}) copy-start(bf16[13,256,256]{2,1,0:T(8,128)(2,1)S(1)} %collective-permute-done.near_ref) | copy-start | bytes 5111812
  39.8 17.0 %collective-permute-start.3 = (bf16[8,256,256]{2,1,0:T(8,128)(2,1)}, bf16[8,256,256]{2,1,0:T(8,128)(2,1)S(1)}, u32[]{:S(2)}, u32[]{:S(2)}) collective-permute-start(bf16[8,256,256]{2,1,0:T(8,128)(2,1)} %get-tuple-element.39), channel_id=1, source_target_pairs={{0,1},{1,2},{2,3},{4,5},{5,6},{6,7},{8,9},{9,10},{10,11},{12,13},{... | collective-permute-start | bytes 3145736 | tf_op jit(solution)/shard_map/ppermute | solution.py:23
  44.1 21.1 %collective-permute-start.6 = (bf16[6,256,256]{2,1,0:T(8,128)(2,1)}, bf16[6,256,256]{2,1,0:T(8,128)(2,1)S(1)}, u32[]{:S(2)}, u32[]{:S(2)}) collective-permute-start(bf16[6,256,256]{2,1,0:T(8,128)(2,1)} %get-tuple-element.43), channel_id=1, source_target_pairs={{0,1},{1,2},{2,3},{4,5},{5,6},{6,7},{8,9},{9,10},{10,11},{12,13},{... | collective-permute-start | bytes 2359304 | tf_op jit(solution)/shard_map/ppermute | solution.py:23
  46.0 27.0 %collective-permute-start.5 = (bf16[6,256,256]{2,1,0:T(8,128)(2,1)}, bf16[6,256,256]{2,1,0:T(8,128)(2,1)S(1)}, u32[]{:S(2)}, u32[]{:S(2)}) collective-permute-start(bf16[6,256,256]{2,1,0:T(8,128)(2,1)} %get-tuple-element.41), channel_id=1, source_target_pairs={{0,1},{1,2},{2,3},{4,5},{5,6},{6,7},{8,9},{9,10},{10,11},{12,13},{... | collective-permute-start | bytes 2359304 | tf_op jit(solution)/shard_map/ppermute | solution.py:23
  48.1 13.2 %copy-start.5 = (bf16[6,256,256]{2,1,0:T(8,128)(2,1)S(1)}, bf16[6,256,256]{2,1,0:T(8,128)(2,1)}, u32[]{:S(2)}) copy-start(bf16[6,256,256]{2,1,0:T(8,128)(2,1)} %get-tuple-element.48) | copy-start | bytes 2359300
  56.8 8.3 %copy-start.3 = (bf16[6,256,256]{2,1,0:T(8,128)(2,1)S(1)}, bf16[6,256,256]{2,1,0:T(8,128)(2,1)}, u32[]{:S(2)}) copy-start(bf16[6,256,256]{2,1,0:T(8,128)(2,1)} %get-tuple-element.42) | copy-start | bytes 2359300
  56.9 16.1 %copy-start.2 = (bf16[6,256,256]{2,1,0:T(8,128)(2,1)S(1)}, bf16[6,256,256]{2,1,0:T(8,128)(2,1)}, u32[]{:S(2)}) copy-start(bf16[6,256,256]{2,1,0:T(8,128)(2,1)} %get-tuple-element.40) | copy-start | bytes 2359300
  56.9 19.4 %copy-start = (bf16[8,256,256]{2,1,0:T(8,128)(2,1)S(1)}, bf16[8,256,256]{2,1,0:T(8,128)(2,1)}, u32[]{:S(2)}) copy-start(bf16[8,256,256]{2,1,0:T(8,128)(2,1)} %get-tuple-element.38) | copy-start | bytes 3145732
  58.2 18.1 %collective-permute-start.4 = (bf16[4,256,256]{2,1,0:T(8,128)(2,1)S(1)}, bf16[4,256,256]{2,1,0:T(8,128)(2,1)S(1)}, u32[]{:S(2)}, u32[]{:S(2)}) collective-permute-start(bf16[4,256,256]{2,1,0:T(8,128)(2,1)S(1)} %add_convert_fusion.1), channel_id=1, source_target_pairs={{0,4},{1,5},{2,6},{3,7},{8,12},{9,13},{10,14},{11,15},{16,20},{17,... | collective-permute-start | bytes 1572872 | tf_op jit(solution)/shard_map/ppermute | solution.py:18
  61.4 19.9 %collective-permute-start.9 = (bf16[6,256,256]{2,1,0:T(8,128)(2,1)S(1)}, bf16[6,256,256]{2,1,0:T(8,128)(2,1)S(1)}, u32[]{:S(2)}, u32[]{:S(2)}) collective-permute-start(bf16[6,256,256]{2,1,0:T(8,128)(2,1)S(1)} %copy-done.5), channel_id=1, source_target_pairs={{0,1},{1,2},{2,3},{4,5},{5,6},{6,7},{8,9},{9,10},{10,11},{12,13},{... | collective-permute-start | bytes 2359304 | tf_op jit(solution)/shard_map/ppermute | solution.py:23
  65.3 16.0 %copy-start.1 = (bf16[6,256,256]{2,1,0:T(8,128)(2,1)S(1)}, bf16[6,256,256]{2,1,0:T(8,128)(2,1)}, u32[]{:S(2)}) copy-start(bf16[6,256,256]{2,1,0:T(8,128)(2,1)} %get-tuple-element.47) | copy-start | bytes 2359300
  65.3 19.3 %collective-permute-start.8 = (bf16[3,256,256]{2,1,0:T(8,128)(2,1)S(1)}, bf16[3,256,256]{2,1,0:T(8,128)(2,1)S(1)}, u32[]{:S(2)}, u32[]{:S(2)}) collective-permute-start(bf16[3,256,256]{2,1,0:T(8,128)(2,1)S(1)} %add_convert_fusion.7), channel_id=1, source_target_pairs={{0,4},{1,5},{2,6},{3,7},{8,12},{9,13},{10,14},{11,15},{16,20},{17,... | collective-permute-start | bytes 1179656 | tf_op jit(solution)/shard_map/ppermute | solution.py:18
  73.1 15.8 %collective-permute-start.11 = (bf16[3,256,256]{2,1,0:T(8,128)(2,1)S(1)}, bf16[3,256,256]{2,1,0:T(8,128)(2,1)S(1)}, u32[]{:S(2)}, u32[]{:S(2)}) collective-permute-start(bf16[3,256,256]{2,1,0:T(8,128)(2,1)S(1)} %add_convert_fusion.6), channel_id=1, source_target_pairs={{0,4},{1,5},{2,6},{3,7},{8,12},{9,13},{10,14},{11,15},{16,20},{17,... | collective-permute-start | bytes 1179656 | tf_op jit(solution)/shard_map/ppermute | solution.py:18
  76.5 31.8 %collective-permute-start.7 = (bf16[4,256,256]{2,1,0:T(8,128)(2,1)S(1)}, bf16[4,256,256]{2,1,0:T(8,128)(2,1)S(1)}, u32[]{:S(2)}, u32[]{:S(2)}) collective-permute-start(bf16[4,256,256]{2,1,0:T(8,128)(2,1)S(1)} %add_convert_fusion), channel_id=1, source_target_pairs={{0,8},{8,16},{16,24},{1,9},{9,17},{17,25},{2,10},{10,18},{18,26},{... | collective-permute-start | bytes 1572872 | tf_op jit(solution)/shard_map/ppermute | solution.py:18
  81.4 15.9 %collective-permute-start.13 = (bf16[3,256,256]{2,1,0:T(8,128)(2,1)S(1)}, bf16[3,256,256]{2,1,0:T(8,128)(2,1)S(1)}, u32[]{:S(2)}, u32[]{:S(2)}) collective-permute-start(bf16[3,256,256]{2,1,0:T(8,128)(2,1)S(1)} %add_convert_fusion.5), channel_id=1, source_target_pairs={{0,4},{1,5},{2,6},{3,7},{8,12},{9,13},{10,14},{11,15},{16,20},{17,... | collective-permute-start | bytes 1179656 | tf_op jit(solution)/shard_map/ppermute | solution.py:18
  84.7 23.6 %collective-permute-start.10 = (bf16[3,256,256]{2,1,0:T(8,128)(2,1)S(1)}, bf16[3,256,256]{2,1,0:T(8,128)(2,1)S(1)}, u32[]{:S(2)}, u32[]{:S(2)}) collective-permute-start(bf16[3,256,256]{2,1,0:T(8,128)(2,1)S(1)} %add_convert_fusion.4), channel_id=1, source_target_pairs={{0,8},{8,16},{16,24},{1,9},{9,17},{17,25},{2,10},{10,18},{18,26},{... | collective-permute-start | bytes 1179656 | tf_op jit(solution)/shard_map/ppermute | solution.py:18
  89.0 19.3 %collective-permute-start.12 = (bf16[3,256,256]{2,1,0:T(8,128)(2,1)S(1)}, bf16[3,256,256]{2,1,0:T(8,128)(2,1)S(1)}, u32[]{:S(2)}, u32[]{:S(2)}) collective-permute-start(bf16[3,256,256]{2,1,0:T(8,128)(2,1)S(1)} %add_convert_fusion.3), channel_id=1, source_target_pairs={{0,8},{8,16},{16,24},{1,9},{9,17},{17,25},{2,10},{10,18},{18,26},{... | collective-permute-start | bytes 1179656 | tf_op jit(solution)/shard_map/ppermute | solution.py:18
  97.5 17.9 %collective-permute-start.14 = (bf16[3,256,256]{2,1,0:T(8,128)(2,1)S(1)}, bf16[3,256,256]{2,1,0:T(8,128)(2,1)S(1)}, u32[]{:S(2)}, u32[]{:S(2)}) collective-permute-start(bf16[3,256,256]{2,1,0:T(8,128)(2,1)S(1)} %add_convert_fusion.2), channel_id=1, source_target_pairs={{0,8},{8,16},{16,24},{1,9},{9,17},{17,25},{2,10},{10,18},{18,26},{... | collective-permute-start | bytes 1179656 | tf_op jit(solution)/shard_map/ppermute | solution.py:18

commit v4 on v3

--- a/solution.py
+++ b/solution.py
@@ -9,7 +9,7 @@
 ROWS = 16
 PARTS = 4
 LAG = 2
-VMEM_BYTES = 56 * 2**20
+VMEM_BYTES = 24 * 2**20
 
 
 def from_behind(shard, axis, by):

time: 117 us -> 108 us (0.923)
  Pallas kernels: 30.1 us -> 18.1 us
  local copies, waits for them, and re-layouts: 2.73 us -> 4.76 us
  starting transfers between devices: 44.9 us -> 46.4 us
    pallas_call x3, Pallas kernels: 26.7 us -> 16.6 us  [call(): pl.pallas_call(kernel, out_shape=[jax.ShapeDtypeStruct((width, cap, cap),...]
    ppermute x8, waiting for transfers between devices: 20.6 us -> 16.2 us  [from_behind(): return lax.ppermute(shard, axis, pairs)]
    ppermute x6, waiting for transfers between devices: 14.6 us -> 18.8 us  [shift_column(): lax.ppermute(shard, 'sec', [(q, q + 1) for q in range(count - 1) if q % N...]
    unnamed x17 -> x9, local copies, waits for them, and re-layouts: 2.73 us -> 4.76 us
    pallas_call x1, Pallas kernels: 3.38 us -> 1.53 us  [prepare(): pl.pallas_call(prepare_kernel, out_shape=[jax.ShapeDtypeStruct((*mpo_tens...]
  transfers between devices with their start and end apart: 15 -> 15, of which waited for: 7 -> 8; matrix products, arithmetic and copies ran while one was open for 3% -> 2% of each run, Pallas kernels for 15% -> 9%
where the time goes in v4:
time: 108 us; the launch traced here: 107 us
  starting transfers between devices  46.4 us (43%)
  waiting for transfers between devices  35 us (32%)
  Pallas kernels  18.1 us (17%)
  local copies, waits for them, and re-layouts  4.76 us (4%)
  other arithmetic  2.48 us (2%)
    ppermute x8, starting transfers between devices, from_behind(): return lax.ppermute(shard, axis, pairs)  25.6 us
    ppermute x6, starting transfers between devices, shift_column(): lax.ppermute(shard, 'sec', [(q, q + 1) for q in range(count - 1) if q % N...  19.5 us
    ppermute x6, waiting for transfers between devices, shift_column(): lax.ppermute(shard, 'sec', [(q, q + 1) for q in range(count - 1) if q % N...  18.8 us
    pallas_call x3, Pallas kernels, call(): pl.pallas_call(kernel, out_shape=[jax.ShapeDtypeStruct((width, cap, cap),...  16.6 us
    ppermute x8, waiting for transfers between devices, from_behind(): return lax.ppermute(shard, axis, pairs)  16.2 us
    unnamed x9, local copies, waits for them, and re-layouts  4.76 us
  transfers between devices with their start and end apart: 15, of which 8 were waited for; matrix products, arithmetic and copies ran while one was open for 2% of the time, Pallas kernels for 9%

profile of v4, /device:TPU:1, one launch (start us, length us, event | category | flops | bytes accessed | tf_op | source)
XLA Modules:
  0.0 107.0 jit_solution(16468777610837891502)
XLA Ops:
  0.0 4.5 %collective-permute-start = (bf16[13,256,256]{2,1,0:T(8,128)(2,1)}, bf16[13,256,256]{2,1,0:T(8,128)(2,1)S(1)}, u32[]{:S(2)}, u32[]{:S(2)}) collective-permute-start(bf16[13,256,256]{2,1,0:T(8,128)(2,1)} %bitcast.3), channel_id=1, source_target_pairs={{0,1},{1,2},{2,3},{4,5},{5,6},{6,7},{8,9},{9,10},{10,11},{12,13},{... | collective-permute-start | bytes 5111816 | tf_op jit(solution)/shard_map/ppermute | solution.py:23
  9.4 1.9 %collective-permute-start.1 = (bf16[2,256,256]{2,1,0:T(8,128)(2,1)S(1)}, bf16[2,256,256]{2,1,0:T(8,128)(2,1)S(1)}, u32[]{:S(2)}, u32[]{:S(2)}) collective-permute-start(bf16[2,256,256]{2,1,0:T(8,128)(2,1)S(1)} %get-tuple-element.33), channel_id=1, source_target_pairs={{0,1},{1,2},{2,3},{4,5},{5,6},{6,7},{8,9},{9,10},{10,11},{12,13},{... | collective-permute-start | bytes 786440 | tf_op jit(solution)/shard_map/ppermute | solution.py:23
  14.0 3.0 %shard_map.56 = (bf16[13,256,256]{2,1,0:T(8,128)(2,1)S(1)}, bf16[13,256,256]{2,1,0:T(8,128)(2,1)S(1)}) custom-call(bf16[13,256,256]{2,1,0:T(8,128)(2,1)S(1)} %bitcast.4, bf16[2,4,208,208]{3,2,1,0:T(8,128)(2,1)S(1)} %get-tuple-element.29.mixer_ref, bf16[2,256,256]{2,1,0:T(8,128)(2,1)S(1)} %get-tuple-element.30.block_ref), custom_call_target="tpu_custom_call" | custom-call | flops 2617245696 | bytes 4194304 | tf_op jit(solution)/shard_map/pallas_call | solution.py:158
  17.0 9.2 %collective-permute-done.1.near_block_ref = bf16[2,256,256]{2,1,0:T(8,128)(2,1)S(1)} collective-permute-done((bf16[2,256,256]{2,1,0:T(8,128)(2,1)S(1)}, bf16[2,256,256]{2,1,0:T(8,128)(2,1)S(1)}, u32[]{:S(2)}, u32[]{:S(2)}) %collective-permute-start.1) | collective-permute-done | bytes 262176 | tf_op jit(solution)/shard_map/ppermute | solution.py:23
  26.3 8.2 %shard_map.57 = (bf16[13,256,256]{2,1,0:T(8,128)(2,1)S(1)}, bf16[13,256,256]{2,1,0:T(8,128)(2,1)S(1)}, bf16[8,256,256]{2,1,0:T(8,128)(2,1)S(1)}, bf16[6,256,256]...) custom-call(bf16[13,256,256]{2,1,0:T(8,128)(2,1)S(1)} %collective-permute-done.near_ref, ...), custom_call_target="tpu_custom_call" | custom-call | flops 6543114240 | bytes 4194304 | tf_op jit(solution)/shard_map/pallas_call | solution.py:158
  34.5 4.4 %collective-permute-start.3 = (bf16[8,256,256]{2,1,0:T(8,128)(2,1)S(1)}, bf16[8,256,256]{2,1,0:T(8,128)(2,1)S(1)}, u32[]{:S(2)}, u32[]{:S(2)}) collective-permute-start(bf16[8,256,256]{2,1,0:T(8,128)(2,1)S(1)} %get-tuple-element.39), channel_id=1, source_target_pairs={{0,1},{1,2},{2,3},{4,5},{5,6},{6,7},{8,9},{9,10},{10,11},{12,13},{... | collective-permute-start | bytes 3145736 | tf_op jit(solution)/shard_map/ppermute | solution.py:23
  38.9 1.9 %collective-permute-start.6 = (bf16[6,256,256]{2,1,0:T(8,128)(2,1)S(1)}, bf16[6,256,256]{2,1,0:T(8,128)(2,1)S(1)}, u32[]{:S(2)}, u32[]{:S(2)}) collective-permute-start(bf16[6,256,256]{2,1,0:T(8,128)(2,1)S(1)} %get-tuple-element.43), channel_id=1, source_target_pairs={{0,1},{1,2},{2,3},{4,5},{5,6},{6,7},{8,9},{9,10},{10,11},{12,13},{... | collective-permute-start | bytes 2359304 | tf_op jit(solution)/shard_map/ppermute | solution.py:23
  40.8 2.1 %collective-permute-start.5 = (bf16[6,256,256]{2,1,0:T(8,128)(2,1)S(1)}, bf16[6,256,256]{2,1,0:T(8,128)(2,1)S(1)}, u32[]{:S(2)}, u32[]{:S(2)}) collective-permute-start(bf16[6,256,256]{2,1,0:T(8,128)(2,1)S(1)} %get-tuple-element.41), channel_id=1, source_target_pairs={{0,1},{1,2},{2,3},{4,5},{5,6},{6,7},{8,9},{9,10},{10,11},{12,13},{... | collective-permute-start | bytes 2359304 | tf_op jit(solution)/shard_map/ppermute | solution.py:23
  42.9 5.4 %shard_map.58 = (bf16[8,256,256]{2,1,0:T(8,128)(2,1)S(1)}, bf16[6,256,256]{2,1,0:T(8,128)(2,1)S(1)}, bf16[6,256,256]{2,1,0:T(8,128)(2,1)S(1)}, bf16[6,256,256]{2,1,0:T(8,128)(2,1)S(1)}) custom-call(bf16[13,256,256]{2,1,0:T(8,128)(2,1)S(1)} %get-tuple-element.36.middle_ref, bf16[13,256,256]{2,1,0:T(8,128)(2,1)S(1)} %get-tuple-element.37.middle_below_ref, ...), custom_call_target="tpu_custom_call" | custom-call | flops 3925868544 | bytes 4194304 | tf_op jit(solution)/shard_map/pallas_call | solution.py:158
  48.3 2.3 %collective-permute-done.3 = bf16[8,256,256]{2,1,0:T(8,128)(2,1)S(1)} collective-permute-done((bf16[8,256,256]{2,1,0:T(8,128)(2,1)S(1)}, bf16[8,256,256]{2,1,0:T(8,128)(2,1)S(1)}, u32[]{:S(2)}, u32[]{:S(2)}) %collective-permute-start.3) | collective-permute-done | bytes 1048608 | tf_op jit(solution)/shard_map/ppermute | solution.py:23
  50.7 3.2 %collective-permute-start.4 = (bf16[4,256,256]{2,1,0:T(8,128)(2,1)S(1)}, bf16[4,256,256]{2,1,0:T(8,128)(2,1)S(1)}, u32[]{:S(2)}, u32[]{:S(2)}) collective-permute-start(bf16[4,256,256]{2,1,0:T(8,128)(2,1)S(1)} %add_convert_fusion.1), channel_id=1, source_target_pairs={{0,4},{1,5},{2,6},{3,7},{8,12},{9,13},{10,14},{11,15},{16,20},{17,... | collective-permute-start | bytes 1572872 | tf_op jit(solution)/shard_map/ppermute | solution.py:18
  53.9 4.7 %collective-permute-start.9 = (bf16[6,256,256]{2,1,0:T(8,128)(2,1)S(1)}, bf16[6,256,256]{2,1,0:T(8,128)(2,1)S(1)}, u32[]{:S(2)}, u32[]{:S(2)}) collective-permute-start(bf16[6,256,256]{2,1,0:T(8,128)(2,1)S(1)} %get-tuple-element.48), channel_id=1, source_target_pairs={{0,1},{1,2},{2,3},{4,5},{5,6},{6,7},{8,9},{9,10},{10,11},{12,13},{... | collective-permute-start | bytes 2359304 | tf_op jit(solution)/shard_map/ppermute | solution.py:23
  59.1 3.2 %collective-permute-start.8 = (bf16[3,256,256]{2,1,0:T(8,128)(2,1)S(1)}, bf16[3,256,256]{2,1,0:T(8,128)(2,1)S(1)}, u32[]{:S(2)}, u32[]{:S(2)}) collective-permute-start(bf16[3,256,256]{2,1,0:T(8,128)(2,1)S(1)} %add_convert_fusion.7), channel_id=1, source_target_pairs={{0,4},{1,5},{2,6},{3,7},{8,12},{9,13},{10,14},{11,15},{16,20},{17,... | collective-permute-start | bytes 1179656 | tf_op jit(solution)/shard_map/ppermute | solution.py:18
  62.3 5.2 %collective-permute-done.5 = bf16[6,256,256]{2,1,0:T(8,128)(2,1)S(1)} collective-permute-done((bf16[6,256,256]{2,1,0:T(8,128)(2,1)S(1)}, bf16[6,256,256]{2,1,0:T(8,128)(2,1)S(1)}, u32[]{:S(2)}, u32[]{:S(2)}) %collective-permute-start.5) | collective-permute-done | bytes 786464 | tf_op jit(solution)/shard_map/ppermute | solution.py:23
  67.6 3.2 %collective-permute-start.11 = (bf16[3,256,256]{2,1,0:T(8,128)(2,1)S(1)}, bf16[3,256,256]{2,1,0:T(8,128)(2,1)S(1)}, u32[]{:S(2)}, u32[]{:S(2)}) collective-permute-start(bf16[3,256,256]{2,1,0:T(8,128)(2,1)S(1)} %add_convert_fusion.6), channel_id=1, source_target_pairs={{0,4},{1,5},{2,6},{3,7},{8,12},{9,13},{10,14},{11,15},{16,20},{17,... | collective-permute-start | bytes 1179656 | tf_op jit(solution)/shard_map/ppermute | solution.py:18
  71.0 3.2 %collective-permute-start.7 = (bf16[4,256,256]{2,1,0:T(8,128)(2,1)S(1)}, bf16[4,256,256]{2,1,0:T(8,128)(2,1)S(1)}, u32[]{:S(2)}, u32[]{:S(2)}) collective-permute-start(bf16[4,256,256]{2,1,0:T(8,128)(2,1)S(1)} %add_convert_fusion), channel_id=1, source_target_pairs={{0,8},{8,16},{16,24},{1,9},{9,17},{17,25},{2,10},{10,18},{18,26},{... | collective-permute-start | bytes 1572872 | tf_op jit(solution)/shard_map/ppermute | solution.py:18
  74.2 1.7 %collective-permute-done.9 = bf16[6,256,256]{2,1,0:T(8,128)(2,1)S(1)} collective-permute-done((bf16[6,256,256]{2,1,0:T(8,128)(2,1)S(1)}, bf16[6,256,256]{2,1,0:T(8,128)(2,1)S(1)}, u32[]{:S(2)}, u32[]{:S(2)}) %collective-permute-start.9) | collective-permute-done | bytes 786464 | tf_op jit(solution)/shard_map/ppermute | solution.py:23
  76.0 3.2 %collective-permute-start.13 = (bf16[3,256,256]{2,1,0:T(8,128)(2,1)S(1)}, bf16[3,256,256]{2,1,0:T(8,128)(2,1)S(1)}, u32[]{:S(2)}, u32[]{:S(2)}) collective-permute-start(bf16[3,256,256]{2,1,0:T(8,128)(2,1)S(1)} %add_convert_fusion.5), channel_id=1, source_target_pairs={{0,4},{1,5},{2,6},{3,7},{8,12},{9,13},{10,14},{11,15},{16,20},{17,... | collective-permute-start | bytes 1179656 | tf_op jit(solution)/shard_map/ppermute | solution.py:18
  79.3 3.2 %collective-permute-start.10 = (bf16[3,256,256]{2,1,0:T(8,128)(2,1)S(1)}, bf16[3,256,256]{2,1,0:T(8,128)(2,1)S(1)}, u32[]{:S(2)}, u32[]{:S(2)}) collective-permute-start(bf16[3,256,256]{2,1,0:T(8,128)(2,1)S(1)} %add_convert_fusion.4), channel_id=1, source_target_pairs={{0,8},{8,16},{16,24},{1,9},{9,17},{17,25},{2,10},{10,18},{18,26},{... | collective-permute-start | bytes 1179656 | tf_op jit(solution)/shard_map/ppermute | solution.py:18
  82.8 3.2 %collective-permute-start.12 = (bf16[3,256,256]{2,1,0:T(8,128)(2,1)S(1)}, bf16[3,256,256]{2,1,0:T(8,128)(2,1)S(1)}, u32[]{:S(2)}, u32[]{:S(2)}) collective-permute-start(bf16[3,256,256]{2,1,0:T(8,128)(2,1)S(1)} %add_convert_fusion.3), channel_id=1, source_target_pairs={{0,8},{8,16},{16,24},{1,9},{9,17},{17,25},{2,10},{10,18},{18,26},{... | collective-permute-start | bytes 1179656 | tf_op jit(solution)/shard_map/ppermute | solution.py:18
  86.0 3.6 %collective-permute-done.13 = bf16[3,256,256]{2,1,0:T(8,128)(2,1)S(1)} collective-permute-done((bf16[3,256,256]{2,1,0:T(8,128)(2,1)S(1)}, bf16[3,256,256]{2,1,0:T(8,128)(2,1)S(1)}, u32[]{:S(2)}, u32[]{:S(2)}) %collective-permute-start.13) | collective-permute-done | bytes 393248 | tf_op jit(solution)/shard_map/ppermute | solution.py:18
  89.8 3.2 %collective-permute-start.14 = (bf16[3,256,256]{2,1,0:T(8,128)(2,1)S(1)}, bf16[3,256,256]{2,1,0:T(8,128)(2,1)S(1)}, u32[]{:S(2)}, u32[]{:S(2)}) collective-permute-start(bf16[3,256,256]{2,1,0:T(8,128)(2,1)S(1)} %add_convert_fusion.2), channel_id=1, source_target_pairs={{0,8},{8,16},{16,24},{1,9},{9,17},{17,25},{2,10},{10,18},{18,26},{... | collective-permute-start | bytes 1179656 | tf_op jit(solution)/shard_map/ppermute | solution.py:18
  93.0 8.2 %collective-permute-done.12 = bf16[3,256,256]{2,1,0:T(8,128)(2,1)S(1)} collective-permute-done((bf16[3,256,256]{2,1,0:T(8,128)(2,1)S(1)}, bf16[3,256,256]{2,1,0:T(8,128)(2,1)S(1)}, u32[]{:S(2)}, u32[]{:S(2)}) %collective-permute-start.12) | collective-permute-done | bytes 393248 | tf_op jit(solution)/shard_map/ppermute | solution.py:18
  101.2 4.4 %collective-permute-done.14 = bf16[3,256,256]{2,1,0:T(8,128)(2,1)S(1)} collective-permute-done((bf16[3,256,256]{2,1,0:T(8,128)(2,1)S(1)}, bf16[3,256,256]{2,1,0:T(8,128)(2,1)S(1)}, u32[]{:S(2)}, u32[]{:S(2)}) %collective-permute-start.14) | collective-permute-done | bytes 393248 | tf_op jit(solution)/shard_map/ppermute | solution.py:18
  (28 shorter events, 10.5 us)
Async XLA Ops:
  0.0 26.3 %collective-permute-start = (bf16[13,256,256]{2,1,0:T(8,128)(2,1)}, bf16[13,256,256]{2,1,0:T(8,128)(2,1)S(1)}, u32[]{:S(2)}, u32[]{:S(2)}) collective-permute-start(bf16[13,256,256]{2,1,0:T(8,128)(2,1)} %bitcast.3), channel_id=1, source_target_pairs={{0,1},{1,2},{2,3},{4,5},{5,6},{6,7},{8,9},{9,10},{10,11},{12,13},{... | collective-permute-start | bytes 5111816 | tf_op jit(solution)/shard_map/ppermute | solution.py:23
  5.3 1.2 %copy-start = (bf16[2,1,4,256,256]{4,3,2,1,0:T(8,128)(2,1)S(1)}, bf16[2,1,4,256,256]{4,3,2,1,0:T(8,128)(2,1)}, u32[]{:S(2)}) copy-start(bf16[2,1,4,256,256]{4,3,2,1,0:T(8,128)(2,1)} %site_ref.1) | copy-start | bytes 3145732
  6.5 0.7 copy-start.1
  7.2 0.7 copy-start.2
  9.4 16.9 %collective-permute-start.1 = (bf16[2,256,256]{2,1,0:T(8,128)(2,1)S(1)}, bf16[2,256,256]{2,1,0:T(8,128)(2,1)S(1)}, u32[]{:S(2)}, u32[]{:S(2)}) collective-permute-start(bf16[2,256,256]{2,1,0:T(8,128)(2,1)S(1)} %get-tuple-element.33), channel_id=1, source_target_pairs={{0,1},{1,2},{2,3},{4,5},{5,6},{6,7},{8,9},{9,10},{10,11},{12,13},{... | collective-permute-start | bytes 786440 | tf_op jit(solution)/shard_map/ppermute | solution.py:23
  11.3 15.0 %collective-permute-start.2 = (bf16[2,256,256]{2,1,0:T(8,128)(2,1)S(1)}, bf16[2,256,256]{2,1,0:T(8,128)(2,1)S(1)}, u32[]{:S(2)}, u32[]{:S(2)}) collective-permute-start(bf16[2,256,256]{2,1,0:T(8,128)(2,1)S(1)} %get-tuple-element.35), channel_id=1, source_target_pairs={{4,0},{5,1},{6,2},{7,3},{12,8},{13,9},{14,10},{15,11},{20,16},{21,... | collective-permute-start | bytes 786440 | tf_op jit(solution)/shard_map/ppermute | solution.py:218
  12.6 1.5 %copy-start.3 = (bf16[1,1,13,256,256]{4,3,2,1,0:T(8,128)(2,1)S(1)}, bf16[1,1,13,256,256]{4,3,2,1,0:T(8,128)(2,1)}, u32[]{:S(2)}) copy-start(bf16[1,1,13,256,256]{4,3,2,1,0:T(8,128)(2,1)} %param.5) | copy-start | bytes 5111812
  34.5 16.1 %collective-permute-start.3 = (bf16[8,256,256]{2,1,0:T(8,128)(2,1)S(1)}, bf16[8,256,256]{2,1,0:T(8,128)(2,1)S(1)}, u32[]{:S(2)}, u32[]{:S(2)}) collective-permute-start(bf16[8,256,256]{2,1,0:T(8,128)(2,1)S(1)} %get-tuple-element.39), channel_id=1, source_target_pairs={{0,1},{1,2},{2,3},{4,5},{5,6},{6,7},{8,9},{9,10},{10,11},{12,13},{... | collective-permute-start | bytes 3145736 | tf_op jit(solution)/shard_map/ppermute | solution.py:23
  38.9 20.1 %collective-permute-start.6 = (bf16[6,256,256]{2,1,0:T(8,128)(2,1)S(1)}, bf16[6,256,256]{2,1,0:T(8,128)(2,1)S(1)}, u32[]{:S(2)}, u32[]{:S(2)}) collective-permute-start(bf16[6,256,256]{2,1,0:T(8,128)(2,1)S(1)} %get-tuple-element.43), channel_id=1, source_target_pairs={{0,1},{1,2},{2,3},{4,5},{5,6},{6,7},{8,9},{9,10},{10,11},{12,13},{... | collective-permute-start | bytes 2359304 | tf_op jit(solution)/shard_map/ppermute | solution.py:23
  40.8 26.6 %collective-permute-start.5 = (bf16[6,256,256]{2,1,0:T(8,128)(2,1)S(1)}, bf16[6,256,256]{2,1,0:T(8,128)(2,1)S(1)}, u32[]{:S(2)}, u32[]{:S(2)}) collective-permute-start(bf16[6,256,256]{2,1,0:T(8,128)(2,1)S(1)} %get-tuple-element.41), channel_id=1, source_target_pairs={{0,1},{1,2},{2,3},{4,5},{5,6},{6,7},{8,9},{9,10},{10,11},{12,13},{... | collective-permute-start | bytes 2359304 | tf_op jit(solution)/shard_map/ppermute | solution.py:23
  50.7 20.0 %collective-permute-start.4 = (bf16[4,256,256]{2,1,0:T(8,128)(2,1)S(1)}, bf16[4,256,256]{2,1,0:T(8,128)(2,1)S(1)}, u32[]{:S(2)}, u32[]{:S(2)}) collective-permute-start(bf16[4,256,256]{2,1,0:T(8,128)(2,1)S(1)} %add_convert_fusion.1), channel_id=1, source_target_pairs={{0,4},{1,5},{2,6},{3,7},{8,12},{9,13},{10,14},{11,15},{16,20},{17,... | collective-permute-start | bytes 1572872 | tf_op jit(solution)/shard_map/ppermute | solution.py:18
  53.9 22.0 %collective-permute-start.9 = (bf16[6,256,256]{2,1,0:T(8,128)(2,1)S(1)}, bf16[6,256,256]{2,1,0:T(8,128)(2,1)S(1)}, u32[]{:S(2)}, u32[]{:S(2)}) collective-permute-start(bf16[6,256,256]{2,1,0:T(8,128)(2,1)S(1)} %get-tuple-element.48), channel_id=1, source_target_pairs={{0,1},{1,2},{2,3},{4,5},{5,6},{6,7},{8,9},{9,10},{10,11},{12,13},{... | collective-permute-start | bytes 2359304 | tf_op jit(solution)/shard_map/ppermute | solution.py:23
  59.1 20.0 %collective-permute-start.8 = (bf16[3,256,256]{2,1,0:T(8,128)(2,1)S(1)}, bf16[3,256,256]{2,1,0:T(8,128)(2,1)S(1)}, u32[]{:S(2)}, u32[]{:S(2)}) collective-permute-start(bf16[3,256,256]{2,1,0:T(8,128)(2,1)S(1)} %add_convert_fusion.7), channel_id=1, source_target_pairs={{0,4},{1,5},{2,6},{3,7},{8,12},{9,13},{10,14},{11,15},{16,20},{17,... | collective-permute-start | bytes 1179656 | tf_op jit(solution)/shard_map/ppermute | solution.py:18
  67.6 15.0 %collective-permute-start.11 = (bf16[3,256,256]{2,1,0:T(8,128)(2,1)S(1)}, bf16[3,256,256]{2,1,0:T(8,128)(2,1)S(1)}, u32[]{:S(2)}, u32[]{:S(2)}) collective-permute-start(bf16[3,256,256]{2,1,0:T(8,128)(2,1)S(1)} %add_convert_fusion.6), channel_id=1, source_target_pairs={{0,4},{1,5},{2,6},{3,7},{8,12},{9,13},{10,14},{11,15},{16,20},{17,... | collective-permute-start | bytes 1179656 | tf_op jit(solution)/shard_map/ppermute | solution.py:18
  71.0 30.2 %collective-permute-start.7 = (bf16[4,256,256]{2,1,0:T(8,128)(2,1)S(1)}, bf16[4,256,256]{2,1,0:T(8,128)(2,1)S(1)}, u32[]{:S(2)}, u32[]{:S(2)}) collective-permute-start(bf16[4,256,256]{2,1,0:T(8,128)(2,1)S(1)} %add_convert_fusion), channel_id=1, source_target_pairs={{0,8},{8,16},{16,24},{1,9},{9,17},{17,25},{2,10},{10,18},{18,26},{... | collective-permute-start | bytes 1572872 | tf_op jit(solution)/shard_map/ppermute | solution.py:18
  76.0 13.6 %collective-permute-start.13 = (bf16[3,256,256]{2,1,0:T(8,128)(2,1)S(1)}, bf16[3,256,256]{2,1,0:T(8,128)(2,1)S(1)}, u32[]{:S(2)}, u32[]{:S(2)}) collective-permute-start(bf16[3,256,256]{2,1,0:T(8,128)(2,1)S(1)} %add_convert_fusion.5), channel_id=1, source_target_pairs={{0,4},{1,5},{2,6},{3,7},{8,12},{9,13},{10,14},{11,15},{16,20},{17,... | collective-permute-start | bytes 1179656 | tf_op jit(solution)/shard_map/ppermute | solution.py:18
  79.3 21.8 %collective-permute-start.10 = (bf16[3,256,256]{2,1,0:T(8,128)(2,1)S(1)}, bf16[3,256,256]{2,1,0:T(8,128)(2,1)S(1)}, u32[]{:S(2)}, u32[]{:S(2)}) collective-permute-start(bf16[3,256,256]{2,1,0:T(8,128)(2,1)S(1)} %add_convert_fusion.4), channel_id=1, source_target_pairs={{0,8},{8,16},{16,24},{1,9},{9,17},{17,25},{2,10},{10,18},{18,26},{... | collective-permute-start | bytes 1179656 | tf_op jit(solution)/shard_map/ppermute | solution.py:18
  82.8 18.4 %collective-permute-start.12 = (bf16[3,256,256]{2,1,0:T(8,128)(2,1)S(1)}, bf16[3,256,256]{2,1,0:T(8,128)(2,1)S(1)}, u32[]{:S(2)}, u32[]{:S(2)}) collective-permute-start(bf16[3,256,256]{2,1,0:T(8,128)(2,1)S(1)} %add_convert_fusion.3), channel_id=1, source_target_pairs={{0,8},{8,16},{16,24},{1,9},{9,17},{17,25},{2,10},{10,18},{18,26},{... | collective-permute-start | bytes 1179656 | tf_op jit(solution)/shard_map/ppermute | solution.py:18
  89.8 15.8 %collective-permute-start.14 = (bf16[3,256,256]{2,1,0:T(8,128)(2,1)S(1)}, bf16[3,256,256]{2,1,0:T(8,128)(2,1)S(1)}, u32[]{:S(2)}, u32[]{:S(2)}) collective-permute-start(bf16[3,256,256]{2,1,0:T(8,128)(2,1)S(1)} %add_convert_fusion.2), channel_id=1, source_target_pairs={{0,8},{8,16},{16,24},{1,9},{9,17},{17,25},{2,10},{10,18},{18,26},{... | collective-permute-start | bytes 1179656 | tf_op jit(solution)/shard_map/ppermute | solution.py:18

commit v5 on v4

--- a/solution.py
+++ b/solution.py
@@ -1,3 +1,5 @@
+import functools
+
 import jax
 import jax.numpy as jnp
 from jax import lax
@@ -6,21 +8,22 @@
 from jax.sharding import PartitionSpec as P
 
 ND = 4
+CORES = 2
 ROWS = 16
-PARTS = 4
-LAG = 2
-VMEM_BYTES = 24 * 2**20
+EDGES = (0, 5, 9, 13)
+LAG = 1
+BACK = 2
+LONE_STEP = 0
+EARLY_FLOPS = 6
+LATE_FLOPS = 60
+SMALL_FLOPS = 0
+VMEM_BYTES = 28 * 2**20
 
 
 def from_behind(shard, axis, by):
     count = lax.axis_size(axis)
     pairs = [(i, i + by) for i in range(count) if 0 <= i + by < count]
     return lax.ppermute(shard, axis, pairs)
-
-
-def shift_column(shard):
-    count = lax.axis_size("sec")
-    return lax.ppermute(shard, "sec", [(q, q + 1) for q in range(count - 1) if q % ND < ND - 1])
 
 
 TAKEN = ((0, (2, 3)), (1, (0, 2)), (0, (0, 1)), (1, (0, 1, 2, 3)))
@@ -102,71 +105,95 @@
             out_ref[v] = add_products([(mixed_ref.at[k], block_ref.at[k], flipped_ref.at[k])], v)
 
 
+def is_x_receiver():
+    j = lax.axis_index("sec") % ND
+    return (j % CORES == 0) & (j > 0)
+
+
 def up_kernel(
-    near_ref, own_ref, own_below_ref, mixer_ref, near_block_ref, last_ref, column_ref,
-    middle_ref, middle_below_ref, *refs,
+    kept, near_ref, own_ref, own_below_ref, mixer_ref, near_block_ref, last_ref, column_ref, *refs,
 ):
-    up_refs, (mixed_ref, mixed_below_ref, flipped_ref) = refs[:-3], refs[-3:]
+    remain_ref, *up_refs = refs[kept:-4]
+    up_refs = up_refs[max(kept - 1, 0):]
+    middle_ref, mixed_ref, mixed_below_ref, flipped_ref = refs[-4:]
     channels = near_ref.shape[0]
-    for k, block in enumerate((near_block_ref.at[0], near_block_ref.at[1], last_ref.at[2], last_ref.at[3], column_ref.at[1])):
-        flipped_ref[k] = block[...].T
-    mix(mixer_ref, 0, (2, 3), near_ref, mixed_ref)
-    for k, (out_ref, base_ref) in enumerate(((middle_ref, own_ref), (middle_below_ref, own_below_ref))):
-        for v in range(channels):
-            term = (mixed_ref.at[k], near_block_ref.at[k], flipped_ref.at[k])
-            out_ref[v] = add_products([term], v, base_ref[v].astype(jnp.float32))
-    mix(mixer_ref, 1, (2, 3), middle_ref, mixed_ref)
-    mix(mixer_ref, 1, (2,), middle_below_ref, mixed_below_ref)
-    same = [(mixed_ref.at[0], last_ref.at[2], flipped_ref.at[2])]
-    down = [
-        (mixed_ref.at[1], last_ref.at[3], flipped_ref.at[3]),
-        (mixed_below_ref.at[0], column_ref.at[1], flipped_ref.at[4]),
-    ]
-    v = 0
-    for out_ref in up_refs:
-        width = out_ref.shape[0] // 2
-        for place in range(width):
-            out_ref[place] = add_products(down, v + place)
-        for place in range(width):
-            out_ref[width + place] = add_products(same, v + place)
-        v += width
-
-
-def stay_kernel(middle_ref, middle_below_ref, mixer_ref, last_ref, column_ref, *refs):
-    out_refs, (mixed_ref, mixed_below_ref, flipped_ref) = refs[:-3], refs[-3:]
+
+    @pl.when(is_x_receiver() if kept else jnp.logical_not(is_x_receiver()))
+    def _():
+        blocks = (near_block_ref.at[0], near_block_ref.at[1], last_ref.at[2], last_ref.at[3], column_ref.at[1])
+        for k, block in enumerate(blocks):
+            flipped_ref[k] = block[...].T
+        mix(mixer_ref, 0, (2, 3), near_ref, mixed_ref)
+        for k, base_ref in enumerate((own_ref, own_below_ref)):
+            for v in range(channels):
+                term = (mixed_ref.at[k], near_block_ref.at[k], flipped_ref.at[k])
+                middle_ref[k, v] = add_products([term], v, base_ref[v].astype(jnp.float32))
+        mix(mixer_ref, 1, (2, 3), middle_ref.at[0], mixed_ref)
+        mix(mixer_ref, 1, (2,), middle_ref.at[1], mixed_below_ref)
+        same = [(mixed_ref.at[0], last_ref.at[2], flipped_ref.at[2])]
+        down = [
+            (mixed_ref.at[1], last_ref.at[3], flipped_ref.at[3]),
+            (mixed_below_ref.at[0], column_ref.at[1], flipped_ref.at[4]),
+        ]
+        v = 0
+        for out_ref in up_refs:
+            width = out_ref.shape[0] // 2
+            for place in range(width):
+                out_ref[place] = add_products(down, v + place)
+            for place in range(width):
+                out_ref[width + place] = add_products(same, v + place)
+            v += width
+        mix(mixer_ref, 1, (0, 1), middle_ref.at[0], remain_ref.at[pl.ds(0, 2)])
+        mix(mixer_ref, 1, (0,), middle_ref.at[1], remain_ref.at[pl.ds(2, 1)])
+
+
+def lone_kernel(own_ref, own_below_ref, mixer_ref, last_ref, column_ref, below_ref, same_ref, mixed_ref, flipped_ref):
+    @pl.when(lax.axis_index("sec") % ND == 0)
+    def _():
+        mix(mixer_ref, 1, (0, 1), own_ref, mixed_ref.at[pl.ds(0, 2)])
+        mix(mixer_ref, 1, (0,), own_below_ref, mixed_ref.at[pl.ds(2, 1)])
+        remain(mixed_ref, last_ref, column_ref, flipped_ref, below_ref, same_ref, 0, ())
+
+
+def remain_kernel(low, remain_ref, last_ref, column_ref, *refs):
+    arrived_refs, (below_ref, same_ref, flipped_ref) = refs[:-3], refs[-3:]
+
+    @pl.when(lax.axis_index("sec") % ND > 0)
+    def _():
+        arrived = [(ref, 0, below_ref.shape[0]) for ref in arrived_refs]
+        remain(remain_ref, last_ref, column_ref, flipped_ref, below_ref, same_ref, low, arrived)
+
+
+def remain(mixed_ref, last_ref, column_ref, flipped_ref, below_ref, same_ref, low, arrived):
     for k, block in enumerate((last_ref.at[0], last_ref.at[1], column_ref.at[0])):
         flipped_ref[k] = block[...].T
-    mix(mixer_ref, 1, (0, 1), middle_ref, mixed_ref)
-    mix(mixer_ref, 1, (0,), middle_below_ref, mixed_below_ref)
     same = [(mixed_ref.at[0], last_ref.at[0], flipped_ref.at[0])]
     down = [
         (mixed_ref.at[1], last_ref.at[1], flipped_ref.at[1]),
-        (mixed_below_ref.at[0], column_ref.at[0], flipped_ref.at[2]),
+        (mixed_ref.at[2], column_ref.at[0], flipped_ref.at[2]),
     ]
-    v = 0
-    for out_ref in out_refs:
-        width = out_ref.shape[0] // 2
-        for place in range(width):
-            out_ref[place] = add_products(down, v + place)
-        for place in range(width):
-            out_ref[width + place] = add_products(same, v + place)
-        v += width
-
-
-def call(kernel, operands, widths, mixed, flipped, work):
-    channels, cap, _ = operands[0].shape
+    for row, (terms, out_ref) in enumerate(((down, below_ref), (same, same_ref))):
+        for k in range(out_ref.shape[0]):
+            total = None
+            for arrived_ref, *begins in arrived:
+                there = arrived_ref[begins[row] + k].astype(jnp.float32)
+                total = there if total is None else total + there
+            out_ref[k] = add_products(terms, low + k, total)
+
+
+def call(kernel, operands, shapes, scratch, work, aliased=(), flops=6):
+    cap = operands[0].shape[-1]
+    vmem = pl.BlockSpec(memory_space=pltpu.VMEM)
     return pl.pallas_call(
         kernel,
-        out_shape=[jax.ShapeDtypeStruct((width, cap, cap), jnp.bfloat16) for width in widths],
-        in_specs=[pl.BlockSpec(memory_space=pltpu.VMEM)] * len(operands),
-        out_specs=[pl.BlockSpec(memory_space=pltpu.VMEM)] * len(widths),
-        scratch_shapes=[pltpu.VMEM((n, channels, cap, cap), jnp.bfloat16) for n in mixed]
-        + [pltpu.VMEM((flipped, cap, cap), jnp.bfloat16)],
+        out_shape=[jax.ShapeDtypeStruct((*shape, cap, cap), jnp.bfloat16) for shape in shapes],
+        in_specs=[vmem] * (len(operands) + len(aliased)),
+        out_specs=[vmem] * len(shapes),
+        input_output_aliases={len(operands) + k: k for k in range(len(aliased))},
+        scratch_shapes=[pltpu.VMEM((*shape, cap, cap), jnp.bfloat16) for shape in scratch],
         compiler_params=pltpu.CompilerParams(vmem_limit_bytes=VMEM_BYTES),
-        cost_estimate=pl.CostEstimate(
-            flops=6 * work * channels * cap**3, bytes_accessed=4 * 2**20, transcendentals=0
-        ),
-    )(*operands)
+        cost_estimate=pl.CostEstimate(flops=flops * work * cap**3, bytes_accessed=flops * 2**19, transcendentals=0),
+    )(*operands, *aliased)
 
 
 def masked_blocks(site_block_tensors, block_mask, sector_dims):
@@ -195,9 +222,9 @@
     return lax.optimization_barrier((value, *others))[0]
 
 
-def cut(count, parts):
-    edges = [-(-count * k // parts) for k in range(parts + 1)]
-    return list(zip(edges[:-1], edges[1:]))
+def cut(count):
+    edges = [-(-count * k // EDGES[-1]) for k in EDGES]
+    return [high - low for low, high in zip(edges[:-1], edges[1:])]
 
 
 def wide_add(*terms):
@@ -210,33 +237,72 @@
 def two_rows(boundary_env, site_block_tensors, mpo_tensors, block_mask, sector_dims):
     env = boundary_env[0, 0]
     channels = env.shape[0]
-    near_env = shift_column(env)
+    count = lax.axis_size("sec")
+
+    def send(shard, sources, seg, sec):
+        pairs = [
+            (g * count + q, (g + seg) * count + q + sec)
+            for g in range(lax.axis_size("seg") - seg) for q in sources
+        ]
+        return lax.ppermute(shard, ("seg", "sec"), pairs)
+
+    steps = [(q, q + 1) for q in range(count - 1) if q % ND < ND - 1]
+    over_x = [pair for pair in steps if pair[1] % CORES == 0]
+    on_chip = [pair for pair in steps if pair[1] % CORES]
+    late_on_chip = [pair for pair in on_chip if pair[0] % ND]
+    early = [pair for pair in steps if pair not in late_on_chip]
+    env_over_x = lax.ppermute(env, "sec", over_x)
+    env_on_chip = lax.ppermute(env, "sec", on_chip)
     mixers, up_blocks, column_blocks, first_blocks, last_blocks = prepare(
         site_block_tensors, block_mask, sector_dims, mpo_tensors
     )
-    near_blocks = shift_column(up_blocks)
+    blocks_over_x = lax.ppermute(up_blocks, "sec", over_x)
+    blocks_on_chip = lax.ppermute(up_blocks, "sec", on_chip)
     column = lax.ppermute(column_blocks, "sec", [(ND + j, j) for j in range(ND)])
-    own, own_below = call(own_kernel, (env, mixers, first_blocks), (channels,) * 2, (2,), 2, 2)
-    pairs = [2 * (high - low) for low, high in cut(channels, PARTS)]
-    middle, middle_below, *up = call(
-        up_kernel, (near_env, own, own_below, mixers, near_blocks, last_blocks, column),
-        (channels, channels, *pairs), (2, 1), 5, 5,
-    )
-    arrived = [shift_column(x) for x in up]
-    stay = call(stay_kernel, (middle, middle_below, mixers, last_blocks, column), pairs, (2, 1), 3, 3)
-    below, handed, last = [], [], None
-    for step in range(PARTS + LAG):
-        if step < PARTS:
-            width = pairs[step] // 2
-            there = arrived[step] if last is None else after(arrived[step], last)
-            last = wide_add(stay[step][:width], there[:width])
-            below.append(from_behind(last, "sec", ND))
+    whole = (channels,)
+    own, own_below = call(
+        own_kernel, (env, mixers, first_blocks), (whole, whole), ((2, channels), (2,)), 2 * channels
+    )
+    parts = cut(channels)
+    lone_below, lone = call(
+        lone_kernel, (own, own_below, mixers, last_blocks, column), (whole, whole), ((3, channels), (3,)),
+        3 * channels, (), SMALL_FLOPS,
+    )
+    lone_from_up = send(lone_below, [0], 0, ND)
+    lone_upper = send(lone, [0], 1, 0)
+    scratch = ((2, channels), (2, channels), (1, channels), (5,))
+    ups = [(2 * width,) for width in parts]
+    remaining, *up = call(
+        functools.partial(up_kernel, 0),
+        (env_on_chip, after(own, lone), own_below, mixers, blocks_on_chip, last_blocks, column),
+        ((3, channels), *ups), scratch, 5 * channels, (), EARLY_FLOPS,
+    )
+    remaining, *late = call(
+        functools.partial(up_kernel, len(parts)),
+        (env_over_x, own, own_below, mixers, blocks_over_x, last_blocks, column),
+        ((3, channels), *ups[1:], *ups), scratch, 5 * channels, (remaining, *up[1:]), LATE_FLOPS,
+    )
+    arrived = [lax.ppermute(x, "sec", early) for x in (up[0], *late[:len(parts) - 1])]
+    late = [lax.ppermute(x, "sec", late_on_chip) for x in late[len(parts) - 1:]]
+    rest = [q for q in range(count) if q % ND]
+    below, same, handed, last, lone_lower = [], [], [], None, None
+    for step in range(len(parts) + LAG):
+        if step < len(parts):
+            low, width = sum(parts[:step]), parts[step]
+            there = after(arrived[step], *((lone_from_up, lone_upper) if last is None else (last,)))
+            last, here = call(
+                functools.partial(remain_kernel, low), (remaining, last_blocks, column, there, late[step]),
+                ((width,), (width,)), ((3,),), 3 * width, (), SMALL_FLOPS,
+            )
+            same.append(here)
+            below.append(send(last, rest[:ND - 1], 0, ND))
+        if step == LONE_STEP:
+            lone_lower = send(wide_add(lone, after(lone_from_up, last)), [ND], 1, 0)
         if step >= LAG:
             part = step - LAG
-            width = pairs[part] // 2
-            last = wide_add(stay[part][width:], arrived[part][width:], after(below[part], last))
-            handed.append(from_behind(last, "seg", 1))
-    return jnp.concatenate(handed)[None, None]
+            last = wide_add(same[part], after(below[part], last, *handed[:max(part - BACK + 1, 0)]))
+            handed.append(send(last, rest, 1, 0))
+    return (jnp.concatenate(handed) + (lone_upper + lone_lower))[None, None]
 
 
 def contract(left_environ_tensor, block_list, weight_factors):

time: 108 us -> 101 us (0.935)
  the two profiles are of different devices: /device:TPU:1 before, /device:TPU:14 now
where the time goes in v5:
time: 101 us
  waiting for transfers between devices  43 us (43%)
  starting transfers between devices  32.8 us (32%)
  Pallas kernels  17.7 us (18%)
  local copies, waits for them, and re-layouts  4.76 us (5%)
  other arithmetic  2.34 us (2%)
    ppermute x9, waiting for transfers between devices, send(): return lax.ppermute(shard, ('seg', 'sec'), pairs)  22.9 us
    ppermute x9, starting transfers between devices, send(): return lax.ppermute(shard, ('seg', 'sec'), pairs)  16.6 us
    pallas_call x7, Pallas kernels, call(): pl.pallas_call(kernel, out_shape=[jax.ShapeDtypeStruct((*shape, cap, cap)...  16.2 us
    ppermute x3, waiting for transfers between devices, two_rows(): lax.ppermute(x, 'sec', early)  12.7 us
    ppermute x1, waiting for transfers between devices, two_rows(): blocks_over_x = lax.ppermute(up_blocks, 'sec', over_x)  7.36 us
    unnamed x9, local copies, waits for them, and re-layouts  4.76 us
    ppermute x3, starting transfers between devices, two_rows(): late = [lax.ppermute(x, 'sec', late_on_chip) for x in late[len(parts) - 1:]]  4.09 us
    ppermute x3, starting transfers between devices, two_rows(): lax.ppermute(x, 'sec', early)  3.88 us
  transfers between devices with their start and end apart: 20, of which 8 were waited for; matrix products, arithmetic and copies ran while one was open for 2% of the time, Pallas kernels for 18%

profile of v5, /device:TPU:14, one launch (start us, length us, event | category | flops | bytes accessed | tf_op | source)
XLA Modules:
  0.0 100.8 jit_solution(928686835201186864)
XLA Ops:
  0.0 1.8 %collective-permute-start.3 = (bf16[13,256,256]{2,1,0:T(8,128)(2,1)}, bf16[13,256,256]{2,1,0:T(8,128)(2,1)S(1)}, u32[]{:S(2)}, u32[]{:S(2)}) collective-permute-start(bf16[13,256,256]{2,1,0:T(8,128)(2,1)} %bitcast.3), channel_id=1, source_target_pairs={{0,1},{2,3},{4,5},{6,7},{8,9},{10,11},{12,13},{14,15},{16,17},{18,... | collective-permute-start | bytes 5111816 | tf_op jit(solution)/shard_map/ppermute | solution.py:255
  1.8 1.3 %collective-permute-start = (bf16[13,256,256]{2,1,0:T(8,128)(2,1)}, bf16[13,256,256]{2,1,0:T(8,128)(2,1)S(1)}, u32[]{:S(2)}, u32[]{:S(2)}) collective-permute-start(bf16[13,256,256]{2,1,0:T(8,128)(2,1)} %bitcast.4), channel_id=1, source_target_pairs={{1,2},{5,6},{9,10},{13,14},{17,18},{21,22},{25,26},{29,30}} | collective-permute-start | bytes 5111816 | tf_op jit(solution)/shard_map/ppermute | solution.py:254
  6.5 1.5 %shard_map.55 = (bf16[2,4,208,208]{3,2,1,0:T(8,128)(2,1)S(1)}, bf16[2,256,256]{2,1,0:T(8,128)(2,1)S(1)}, bf16[2,256,256]{2,1,0:T(8,128)(2,1)S(1)}, bf16[2,256,25...) custom-call(bf16[2,1,4,256,256]{4,3,2,1,0:T(8,128)(2,1)S(1)} %copy-done, s32[2,1,4]{2,1,0:T(1,128)S(1)} %copy-done.1, ...), custom_call_target="tpu_custom_call" | custom-call | flops 1000000 | bytes 2097152 | tf_op jit(solution)/shard_map/pallas_call | solution.py:71
  8.0 2.4 %collective-permute-start.2 = (bf16[2,256,256]{2,1,0:T(8,128)(2,1)S(1)}, bf16[2,256,256]{2,1,0:T(8,128)(2,1)S(1)}, u32[]{:S(2)}, u32[]{:S(2)}) collective-permute-start(bf16[2,256,256]{2,1,0:T(8,128)(2,1)S(1)} %get-tuple-element.44), channel_id=1, source_target_pairs={{4,0},{5,1},{6,2},{7,3},{12,8},{13,9},{14,10},{15,11},{20,16},{21,... | collective-permute-start | bytes 786440 | tf_op jit(solution)/shard_map/ppermute | solution.py:261
  10.4 1.3 %collective-permute-start.4 = (bf16[2,256,256]{2,1,0:T(8,128)(2,1)S(1)}, bf16[2,256,256]{2,1,0:T(8,128)(2,1)S(1)}, u32[]{:S(2)}, u32[]{:S(2)}) collective-permute-start(bf16[2,256,256]{2,1,0:T(8,128)(2,1)S(1)} %get-tuple-element.42), channel_id=1, source_target_pairs={{0,1},{2,3},{4,5},{6,7},{8,9},{10,11},{12,13},{14,15},{16,17},{18,... | collective-permute-start | bytes 786440 | tf_op jit(solution)/shard_map/ppermute | solution.py:260
  13.1 1.4 %copy-done.3 = bf16[1,1,13,256,256]{4,3,2,1,0:T(8,128)(2,1)S(1)} copy-done((bf16[1,1,13,256,256]{4,3,2,1,0:T(8,128)(2,1)S(1)}, bf16[1,1,13,256,256]{4,3,2,1,0:T(8,128)(2,1)}, u32[]{:S(2)}) %copy-start.3) | copy-done | bytes 1703960
  14.5 3.0 %shard_map.56 = (bf16[13,256,256]{2,1,0:T(8,128)(2,1)S(1)}, bf16[13,256,256]{2,1,0:T(8,128)(2,1)S(1)}) custom-call(bf16[13,256,256]{2,1,0:T(8,128)(2,1)S(1)} %bitcast.5, bf16[2,4,208,208]{3,2,1,0:T(8,128)(2,1)S(1)} %get-tuple-element.38.mixer_ref, bf16[2,256,256]{2,1,0:T(8,128)(2,1)S(1)} %get-tuple-element.39.block_ref), custom_call_target="tpu_custom_call" | custom-call | flops 2617245696 | bytes 3145728 | tf_op jit(solution)/shard_map/pallas_call | solution.py:187
  20.6 7.4 %collective-permute-done.1.near_block_ref = bf16[2,256,256]{2,1,0:T(8,128)(2,1)S(1)} collective-permute-done((bf16[2,256,256]{2,1,0:T(8,128)(2,1)S(1)}, bf16[2,256,256]{2,1,0:T(8,128)(2,1)S(1)}, u32[]{:S(2)}, u32[]{:S(2)}) %collective-permute-start.1) | collective-permute-done | bytes 262176 | tf_op jit(solution)/shard_map/ppermute | solution.py:259
  28.0 9.3 %shard_map.59 = (bf16[3,13,256,256]{3,2,1,0:T(8,128)(2,1)S(1)}, bf16[8,256,256]{2,1,0:T(8,128)(2,1)S(1)}, bf16[8,256,256]{2,1,0:T(8,128)(2,1)S(1)}, bf16[10,256,...) custom-call(bf16[13,256,256]{2,1,0:T(8,128)(2,1)S(1)} %collective-pe, ...), custom_call_target="tpu_custom_call", output_to_operand_aliasing={{0}: (7, {}), {1}: (8, {}), {2}: (9, {})} | custom-call | flops 65431142400 | bytes 31457280 | tf_op jit(solution)/shard_map/pallas_call | solution.py:187
  37.3 1.4 %collective-permute-start.8 = (bf16[10,256,256]{2,1,0:T(8,128)(2,1)S(1)}, bf16[10,256,256]{2,1,0:T(8,128)(2,1)S(1)}, u32[]{:S(2)}, u32[]{:S(2)}) collective-permute-start(bf16[10,256,256]{2,1,0:T(8,128)(2,1)S(1)} %get-tuple-element.54), channel_id=1, source_target_pairs={{2,3},{6,7},{10,11},{14,15},{18,19},{22,23},{26,27},{30,31}} | collective-permute-start | bytes 3932168 | tf_op jit(solution)/shard_map/ppermute | solution.py:286
  40.0 1.4 %collective-permute-start.11 = (bf16[8,256,256]{2,1,0:T(8,128)(2,1)S(1)}, bf16[8,256,256]{2,1,0:T(8,128)(2,1)S(1)}, u32[]{:S(2)}, u32[]{:S(2)}) collective-permute-start(bf16[8,256,256]{2,1,0:T(8,128)(2,1)S(1)} %get-tuple-element.59), channel_id=1, source_target_pairs={{2,3},{6,7},{10,11},{14,15},{18,19},{22,23},{26,27},{30,31}} | collective-permute-start | bytes 3145736 | tf_op jit(solution)/shard_map/ppermute | solution.py:286
  41.3 6.8 %collective-permute-done.5.refs_0_ = bf16[10,256,256]{2,1,0:T(8,128)(2,1)S(1)} collective-permute-done((bf16[10,256,256]{2,1,0:T(8,128)(2,1)S(1)}, bf16[10,256,256]{2,1,0:T(8,128)(2,1)S(1)}, u32[]{:S(2)}, u32[]{:S(2)}) %collective-permute-start.5) | collective-permute-done | bytes 1310752 | tf_op jit(solution)/shard_map/ppermute | solution.py:285
  48.1 1.4 %shard_map.60 = (bf16[5,256,256]{2,1,0:T(8,128)(2,1)S(1)}, bf16[5,256,256]{2,1,0:T(8,128)(2,1)S(1)}) custom-call(bf16[3,13,256,256]{3,2,1,0:T(8,128)(2,1)S(1)} %get-tuple-element.50.remain_ref, bf16[4,256,256]{2,1,0:T(8,128)(2,1)S(1)} %get-tuple-element.43.last_ref, bf16[2,256,256]{2,1,0:T(8,128)(2,1)S(1)} %collective-permute-done.2.column_ref, ...), custom_call_target="tpu_custom_call" | custom-call | tf_op jit(solution)/shard_map/pallas_call | solution.py:187
  52.1 1.4 %collective-permute-start.15 = (bf16[8,256,256]{2,1,0:T(8,128)(2,1)S(1)}, bf16[8,256,256]{2,1,0:T(8,128)(2,1)S(1)}, u32[]{:S(2)}, u32[]{:S(2)}) collective-permute-start(bf16[8,256,256]{2,1,0:T(8,128)(2,1)S(1)} %get-tuple-element.65), channel_id=1, source_target_pairs={{2,3},{6,7},{10,11},{14,15},{18,19},{22,23},{26,27},{30,31}} | collective-permute-start | bytes 3145736 | tf_op jit(solution)/shard_map/ppermute | solution.py:286
  53.5 5.9 %collective-permute-done.10.refs_0_ = bf16[8,256,256]{2,1,0:T(8,128)(2,1)S(1)} collective-permute-done((bf16[8,256,256]{2,1,0:T(8,128)(2,1)S(1)}, bf16[8,256,256]{2,1,0:T(8,128)(2,1)S(1)}, u32[]{:S(2)}, u32[]{:S(2)}) %collective-permute-start.10) | collective-permute-done | bytes 1048608 | tf_op jit(solution)/shard_map/ppermute | solution.py:285
  63.1 6.0 %collective-permute-done.9 = bf16[5,256,256]{2,1,0:T(8,128)(2,1)S(1)} collective-permute-done((bf16[5,256,256]{2,1,0:T(8,128)(2,1)S(1)}, bf16[5,256,256]{2,1,0:T(8,128)(2,1)S(1)}, u32[]{:S(2)}, u32[]{:S(2)}) %collective-permute-start.9) | collective-permute-done | bytes 655392 | tf_op jit(solution)/shard_map/ppermute | solution.py:247
  69.2 3.5 %collective-permute-start.12 = (bf16[5,256,256]{2,1,0:T(8,128)(2,1)S(1)}, bf16[5,256,256]{2,1,0:T(8,128)(2,1)S(1)}, u32[]{:S(2)}, u32[]{:S(2)}) collective-permute-start(bf16[5,256,256]{2,1,0:T(8,128)(2,1)S(1)} %add_convert_fusion.1), channel_id=1, source_target_pairs={{1,9},{2,10},{3,11},{5,13},{6,14},{7,15},{9,17},{10,18},{11,19},{1... | collective-permute-start | bytes 1966088 | tf_op jit(solution)/shard_map/ppermute | solution.py:247
  75.2 3.1 %collective-permute-done.13 = bf16[4,256,256]{2,1,0:T(8,128)(2,1)S(1)} collective-permute-done((bf16[4,256,256]{2,1,0:T(8,128)(2,1)S(1)}, bf16[4,256,256]{2,1,0:T(8,128)(2,1)S(1)}, u32[]{:S(2)}, u32[]{:S(2)}) %collective-permute-start.13) | collective-permute-done | bytes 524320 | tf_op jit(solution)/shard_map/ppermute | solution.py:247
  78.5 3.5 %collective-permute-start.16 = (bf16[4,256,256]{2,1,0:T(8,128)(2,1)S(1)}, bf16[4,256,256]{2,1,0:T(8,128)(2,1)S(1)}, u32[]{:S(2)}, u32[]{:S(2)}) collective-permute-start(bf16[4,256,256]{2,1,0:T(8,128)(2,1)S(1)} %add_convert_fusion.3), channel_id=1, source_target_pairs={{1,9},{2,10},{3,11},{5,13},{6,14},{7,15},{9,17},{10,18},{11,19},{1... | collective-permute-start | bytes 1572872 | tf_op jit(solution)/shard_map/ppermute | solution.py:247
  82.0 3.0 %collective-permute-done.17 = bf16[4,256,256]{2,1,0:T(8,128)(2,1)S(1)} collective-permute-done((bf16[4,256,256]{2,1,0:T(8,128)(2,1)S(1)}, bf16[4,256,256]{2,1,0:T(8,128)(2,1)S(1)}, u32[]{:S(2)}, u32[]{:S(2)}) %collective-permute-start.17) | collective-permute-done | bytes 524320 | tf_op jit(solution)/shard_map/ppermute | solution.py:247
  85.1 3.5 %collective-permute-start.18 = (bf16[4,256,256]{2,1,0:T(8,128)(2,1)S(1)}, bf16[4,256,256]{2,1,0:T(8,128)(2,1)S(1)}, u32[]{:S(2)}, u32[]{:S(2)}) collective-permute-start(bf16[4,256,256]{2,1,0:T(8,128)(2,1)S(1)} %add_convert_fusion.2), channel_id=1, source_target_pairs={{1,9},{2,10},{3,11},{5,13},{6,14},{7,15},{9,17},{10,18},{11,19},{1... | collective-permute-start | bytes 1572872 | tf_op jit(solution)/shard_map/ppermute | solution.py:247
  88.6 5.1 %collective-permute-done.16 = bf16[4,256,256]{2,1,0:T(8,128)(2,1)S(1)} collective-permute-done((bf16[4,256,256]{2,1,0:T(8,128)(2,1)S(1)}, bf16[4,256,256]{2,1,0:T(8,128)(2,1)S(1)}, u32[]{:S(2)}, u32[]{:S(2)}) %collective-permute-start.16) | collective-permute-done | bytes 524320 | tf_op jit(solution)/shard_map/ppermute | solution.py:247
  93.7 5.6 %collective-permute-done.18 = bf16[4,256,256]{2,1,0:T(8,128)(2,1)S(1)} collective-permute-done((bf16[4,256,256]{2,1,0:T(8,128)(2,1)S(1)}, bf16[4,256,256]{2,1,0:T(8,128)(2,1)S(1)}, u32[]{:S(2)}, u32[]{:S(2)}) %collective-permute-start.18) | collective-permute-done | bytes 524320 | tf_op jit(solution)/shard_map/ppermute | solution.py:247
  99.3 1.5 %fusion = bf16[1,1,13,256,256]{4,3,2,1,0:T(8,128)(2,1)} fusion(bf16[4,256,256]{2,1,0:T(8,128)(2,1)S(1)} %collective-permute-done.18, bf16[4,256,256]{2,1,0:T(8,128)(2,1)S(1)} %collective-permute-done.16, bf16[5,256,256]{2,1,0:T(8,128)(2,1)S(1)} %collective-permute-done.12, bf16[13,256,256]{2,1,0:T(8,128)(2,1)S(1)} %collective-permute-done.7, ...), kind=kLoop, calls=%fused_computation.2 | loop fusion | flops 3407872 | bytes 6815744 | tf_op jit(solution)/shard_map/broadcast_in_dim | solution.py:305
  (38 shorter events, 18.1 us)
Async XLA Ops:
  0.0 19.1 %collective-permute-start.3 = (bf16[13,256,256]{2,1,0:T(8,128)(2,1)}, bf16[13,256,256]{2,1,0:T(8,128)(2,1)S(1)}, u32[]{:S(2)}, u32[]{:S(2)}) collective-permute-start(bf16[13,256,256]{2,1,0:T(8,128)(2,1)} %bitcast.3), channel_id=1, source_target_pairs={{0,1},{2,3},{4,5},{6,7},{8,9},{10,11},{12,13},{14,15},{16,17},{18,... | collective-permute-start | bytes 5111816 | tf_op jit(solution)/shard_map/ppermute | solution.py:255
  1.8 26.2 %collective-permute-start = (bf16[13,256,256]{2,1,0:T(8,128)(2,1)}, bf16[13,256,256]{2,1,0:T(8,128)(2,1)S(1)}, u32[]{:S(2)}, u32[]{:S(2)}) collective-permute-start(bf16[13,256,256]{2,1,0:T(8,128)(2,1)} %bitcast.4), channel_id=1, source_target_pairs={{1,2},{5,6},{9,10},{13,14},{17,18},{21,22},{25,26},{29,30}} | collective-permute-start | bytes 5111816 | tf_op jit(solution)/shard_map/ppermute | solution.py:254
  3.9 1.2 %copy-start = (bf16[2,1,4,256,256]{4,3,2,1,0:T(8,128)(2,1)S(1)}, bf16[2,1,4,256,256]{4,3,2,1,0:T(8,128)(2,1)}, u32[]{:S(2)}) copy-start(bf16[2,1,4,256,256]{4,3,2,1,0:T(8,128)(2,1)} %site_ref.1) | copy-start | bytes 3145732
  5.1 0.7 copy-start.1
  5.8 0.7 copy-start.2
  8.0 9.5 %collective-permute-start.2 = (bf16[2,256,256]{2,1,0:T(8,128)(2,1)S(1)}, bf16[2,256,256]{2,1,0:T(8,128)(2,1)S(1)}, u32[]{:S(2)}, u32[]{:S(2)}) collective-permute-start(bf16[2,256,256]{2,1,0:T(8,128)(2,1)S(1)} %get-tuple-element.44), channel_id=1, source_target_pairs={{4,0},{5,1},{6,2},{7,3},{12,8},{13,9},{14,10},{15,11},{20,16},{21,... | collective-permute-start | bytes 786440 | tf_op jit(solution)/shard_map/ppermute | solution.py:261
  10.4 7.9 %collective-permute-start.4 = (bf16[2,256,256]{2,1,0:T(8,128)(2,1)S(1)}, bf16[2,256,256]{2,1,0:T(8,128)(2,1)S(1)}, u32[]{:S(2)}, u32[]{:S(2)}) collective-permute-start(bf16[2,256,256]{2,1,0:T(8,128)(2,1)S(1)} %get-tuple-element.42), channel_id=1, source_target_pairs={{0,1},{2,3},{4,5},{6,7},{8,9},{10,11},{12,13},{14,15},{16,17},{18,... | collective-permute-start | bytes 786440 | tf_op jit(solution)/shard_map/ppermute | solution.py:260
  11.7 16.3 %collective-permute-start.1 = (bf16[2,256,256]{2,1,0:T(8,128)(2,1)S(1)}, bf16[2,256,256]{2,1,0:T(8,128)(2,1)S(1)}, u32[]{:S(2)}, u32[]{:S(2)}) collective-permute-start(bf16[2,256,256]{2,1,0:T(8,128)(2,1)S(1)} %get-tuple-element.42), channel_id=1, source_target_pairs={{1,2},{5,6},{9,10},{13,14},{17,18},{21,22},{25,26},{29,30}} | collective-permute-start | bytes 786440 | tf_op jit(solution)/shard_map/ppermute | solution.py:259
  13.0 1.5 %copy-start.3 = (bf16[1,1,13,256,256]{4,3,2,1,0:T(8,128)(2,1)S(1)}, bf16[1,1,13,256,256]{4,3,2,1,0:T(8,128)(2,1)}, u32[]{:S(2)}) copy-start(bf16[1,1,13,256,256]{4,3,2,1,0:T(8,128)(2,1)} %param.5) | copy-start | bytes 5111812
  17.6 23.8 %collective-permute-start.7 = (bf16[13,256,256]{2,1,0:T(8,128)(2,1)S(1)}, bf16[13,256,256]{2,1,0:T(8,128)(2,1)S(1)}, u32[]{:S(2)}, u32[]{:S(2)}) collective-permute-start(bf16[13,256,256]{2,1,0:T(8,128)(2,1)S(1)} %get-tuple-element.45), channel_id=1, source_target_pairs={{0,8},{8,16},{16,24}} | collective-permute-start | bytes 5111816 | tf_op jit(solution)/shard_map/ppermute | solution.py:247
  18.3 21.6 %collective-permute-start.6 = (bf16[13,256,256]{2,1,0:T(8,128)(2,1)S(1)}, bf16[13,256,256]{2,1,0:T(8,128)(2,1)S(1)}, u32[]{:S(2)}, u32[]{:S(2)}) collective-permute-start(bf16[13,256,256]{2,1,0:T(8,128)(2,1)S(1)} %get-tuple-element.52), channel_id=1, source_target_pairs={{0,4},{8,12},{16,20},{24,28}} | collective-permute-start | bytes 5111816 | tf_op jit(solution)/shard_map/ppermute | solution.py:247
  19.3 28.8 %collective-permute-start.5 = (bf16[10,256,256]{2,1,0:T(8,128)(2,1)S(1)}, bf16[10,256,256]{2,1,0:T(8,128)(2,1)S(1)}, u32[]{:S(2)}, u32[]{:S(2)}) collective-permute-start(bf16[10,256,256]{2,1,0:T(8,128)(2,1)S(1)} %get-tuple-element.51), channel_id=1, source_target_pairs={{0,1},{1,2},{4,5},{5,6},{8,9},{9,10},{12,13},{13,14},{16,17},{17,1... | collective-permute-start | bytes 3932168 | tf_op jit(solution)/shard_map/ppermute | solution.py:285
  37.3 10.9 %collective-permute-start.8 = (bf16[10,256,256]{2,1,0:T(8,128)(2,1)S(1)}, bf16[10,256,256]{2,1,0:T(8,128)(2,1)S(1)}, u32[]{:S(2)}, u32[]{:S(2)}) collective-permute-start(bf16[10,256,256]{2,1,0:T(8,128)(2,1)S(1)} %get-tuple-element.54), channel_id=1, source_target_pairs={{2,3},{6,7},{10,11},{14,15},{18,19},{22,23},{26,27},{30,31}} | collective-permute-start | bytes 3932168 | tf_op jit(solution)/shard_map/ppermute | solution.py:286
  38.7 20.7 %collective-permute-start.10 = (bf16[8,256,256]{2,1,0:T(8,128)(2,1)S(1)}, bf16[8,256,256]{2,1,0:T(8,128)(2,1)S(1)}, u32[]{:S(2)}, u32[]{:S(2)}) collective-permute-start(bf16[8,256,256]{2,1,0:T(8,128)(2,1)S(1)} %get-tuple-element.57), channel_id=1, source_target_pairs={{0,1},{1,2},{4,5},{5,6},{8,9},{9,10},{12,13},{13,14},{16,17},{17,1... | collective-permute-start | bytes 3145736 | tf_op jit(solution)/shard_map/ppermute | solution.py:285
  40.0 19.4 %collective-permute-start.11 = (bf16[8,256,256]{2,1,0:T(8,128)(2,1)S(1)}, bf16[8,256,256]{2,1,0:T(8,128)(2,1)S(1)}, u32[]{:S(2)}, u32[]{:S(2)}) collective-permute-start(bf16[8,256,256]{2,1,0:T(8,128)(2,1)S(1)} %get-tuple-element.59), channel_id=1, source_target_pairs={{2,3},{6,7},{10,11},{14,15},{18,19},{22,23},{26,27},{30,31}} | collective-permute-start | bytes 3145736 | tf_op jit(solution)/shard_map/ppermute | solution.py:286
  49.5 19.6 %collective-permute-start.9 = (bf16[5,256,256]{2,1,0:T(8,128)(2,1)S(1)}, bf16[5,256,256]{2,1,0:T(8,128)(2,1)S(1)}, u32[]{:S(2)}, u32[]{:S(2)}) collective-permute-start(bf16[5,256,256]{2,1,0:T(8,128)(2,1)S(1)} %get-tuple-element.56), channel_id=1, source_target_pairs={{1,5},{2,6},{3,7},{9,13},{10,14},{11,15},{17,21},{18,22},{19,23},{... | collective-permute-start | bytes 1966088 | tf_op jit(solution)/shard_map/ppermute | solution.py:247
  50.8 21.9 %collective-permute-start.14 = (bf16[8,256,256]{2,1,0:T(8,128)(2,1)S(1)}, bf16[8,256,256]{2,1,0:T(8,128)(2,1)S(1)}, u32[]{:S(2)}, u32[]{:S(2)}) collective-permute-start(bf16[8,256,256]{2,1,0:T(8,128)(2,1)S(1)} %get-tuple-element.63), channel_id=1, source_target_pairs={{0,1},{1,2},{4,5},{5,6},{8,9},{9,10},{12,13},{13,14},{16,17},{17,1... | collective-permute-start | bytes 3145736 | tf_op jit(solution)/shard_map/ppermute | solution.py:285
  52.1 20.6 %collective-permute-start.15 = (bf16[8,256,256]{2,1,0:T(8,128)(2,1)S(1)}, bf16[8,256,256]{2,1,0:T(8,128)(2,1)S(1)}, u32[]{:S(2)}, u32[]{:S(2)}) collective-permute-start(bf16[8,256,256]{2,1,0:T(8,128)(2,1)S(1)} %get-tuple-element.65), channel_id=1, source_target_pairs={{2,3},{6,7},{10,11},{14,15},{18,19},{22,23},{26,27},{30,31}} | collective-permute-start | bytes 3145736 | tf_op jit(solution)/shard_map/ppermute | solution.py:286
  60.5 17.8 %collective-permute-start.13 = (bf16[4,256,256]{2,1,0:T(8,128)(2,1)S(1)}, bf16[4,256,256]{2,1,0:T(8,128)(2,1)S(1)}, u32[]{:S(2)}, u32[]{:S(2)}) collective-permute-start(bf16[4,256,256]{2,1,0:T(8,128)(2,1)S(1)} %get-tuple-element.60), channel_id=1, source_target_pairs={{1,5},{2,6},{3,7},{9,13},{10,14},{11,15},{17,21},{18,22},{19,23},{... | collective-permute-start | bytes 1572872 | tf_op jit(solution)/shard_map/ppermute | solution.py:247
  62.3 31.4 %collective-permute-start.19 = (bf16[13,256,256]{2,1,0:T(8,128)(2,1)S(1)}, bf16[13,256,256]{2,1,0:T(8,128)(2,1)S(1)}, u32[]{:S(2)}, u32[]{:S(2)}) collective-permute-start(bf16[13,256,256]{2,1,0:T(8,128)(2,1)S(1)} %add_convert_fusion), channel_id=1, source_target_pairs={{4,12},{12,20},{20,28}} | collective-permute-start | bytes 5111816 | tf_op jit(solution)/shard_map/ppermute | solution.py:247
  69.2 15.8 %collective-permute-start.12 = (bf16[5,256,256]{2,1,0:T(8,128)(2,1)S(1)}, bf16[5,256,256]{2,1,0:T(8,128)(2,1)S(1)}, u32[]{:S(2)}, u32[]{:S(2)}) collective-permute-start(bf16[5,256,256]{2,1,0:T(8,128)(2,1)S(1)} %add_convert_fusion.1), channel_id=1, source_target_pairs={{1,9},{2,10},{3,11},{5,13},{6,14},{7,15},{9,17},{10,18},{11,19},{1... | collective-permute-start | bytes 1966088 | tf_op jit(solution)/shard_map/ppermute | solution.py:247
  73.9 11.1 %collective-permute-start.17 = (bf16[4,256,256]{2,1,0:T(8,128)(2,1)S(1)}, bf16[4,256,256]{2,1,0:T(8,128)(2,1)S(1)}, u32[]{:S(2)}, u32[]{:S(2)}) collective-permute-start(bf16[4,256,256]{2,1,0:T(8,128)(2,1)S(1)} %get-tuple-element.66), channel_id=1, source_target_pairs={{1,5},{2,6},{3,7},{9,13},{10,14},{11,15},{17,21},{18,22},{19,23},{... | collective-permute-start | bytes 1572872 | tf_op jit(solution)/shard_map/ppermute | solution.py:247
  78.5 15.3 %collective-permute-start.16 = (bf16[4,256,256]{2,1,0:T(8,128)(2,1)S(1)}, bf16[4,256,256]{2,1,0:T(8,128)(2,1)S(1)}, u32[]{:S(2)}, u32[]{:S(2)}) collective-permute-start(bf16[4,256,256]{2,1,0:T(8,128)(2,1)S(1)} %add_convert_fusion.3), channel_id=1, source_target_pairs={{1,9},{2,10},{3,11},{5,13},{6,14},{7,15},{9,17},{10,18},{11,19},{1... | collective-permute-start | bytes 1572872 | tf_op jit(solution)/shard_map/ppermute | solution.py:247
  85.1 14.2 %collective-permute-start.18 = (bf16[4,256,256]{2,1,0:T(8,128)(2,1)S(1)}, bf16[4,256,256]{2,1,0:T(8,128)(2,1)S(1)}, u32[]{:S(2)}, u32[]{:S(2)}) collective-permute-start(bf16[4,256,256]{2,1,0:T(8,128)(2,1)S(1)} %add_convert_fusion.2), channel_id=1, source_target_pairs={{1,9},{2,10},{3,11},{5,13},{6,14},{7,15},{9,17},{10,18},{11,19},{1... | collective-permute-start | bytes 1572872 | tf_op jit(solution)/shard_map/ppermute | solution.py:247

commit v6 on v5

--- a/solution.py
+++ b/solution.py
@@ -274,12 +274,12 @@
     ups = [(2 * width,) for width in parts]
     remaining, *up = call(
         functools.partial(up_kernel, 0),
-        (env_on_chip, after(own, lone), own_below, mixers, blocks_on_chip, last_blocks, column),
+        (env_on_chip, own, own_below, mixers, blocks_on_chip, last_blocks, column),
         ((3, channels), *ups), scratch, 5 * channels, (), EARLY_FLOPS,
     )
     remaining, *late = call(
         functools.partial(up_kernel, len(parts)),
-        (env_over_x, own, own_below, mixers, blocks_over_x, last_blocks, column),
+        (after(env_over_x, lone), own, own_below, mixers, blocks_over_x, last_blocks, column),
         ((3, channels), *ups[1:], *ups), scratch, 5 * channels, (remaining, *up[1:]), LATE_FLOPS,
     )
     arrived = [lax.ppermute(x, "sec", early) for x in (up[0], *late[:len(parts) - 1])]

time: 101 us -> 101 us (level)
  the two profiles are of different devices: /device:TPU:14 before, /device:TPU:30 now
where the time goes in v6:
time: 101 us
  waiting for transfers between devices  49.6 us (49%)
  starting transfers between devices  26.2 us (26%)
  Pallas kernels  17.7 us (18%)
  local copies, waits for them, and re-layouts  4.76 us (5%)
  other arithmetic  2.34 us (2%)
    ppermute x9, waiting for transfers between devices, send(): return lax.ppermute(shard, ('seg', 'sec'), pairs)  29.4 us
    pallas_call x7, Pallas kernels, call(): pl.pallas_call(kernel, out_shape=[jax.ShapeDtypeStruct((*shape, cap, cap)...  16.2 us
    ppermute x3, waiting for transfers between devices, two_rows(): lax.ppermute(x, 'sec', early)  12.8 us
    ppermute x9, starting transfers between devices, send(): return lax.ppermute(shard, ('seg', 'sec'), pairs)  10.1 us
    ppermute x1, waiting for transfers between devices, two_rows(): env_over_x = lax.ppermute(env, 'sec', over_x)  5.85 us
    unnamed x9, local copies, waits for them, and re-layouts  4.76 us
    ppermute x3, starting transfers between devices, two_rows(): late = [lax.ppermute(x, 'sec', late_on_chip) for x in late[len(parts) - 1:]]  4.09 us
    ppermute x3, starting transfers between devices, two_rows(): lax.ppermute(x, 'sec', early)  3.86 us
  transfers between devices with their start and end apart: 20, of which 10 were waited for; matrix products, arithmetic and copies ran while one was open for 2% of the time, Pallas kernels for 18%

profile of v6, /device:TPU:30, one launch (start us, length us, event | category | flops | bytes accessed | tf_op | source)
XLA Modules:
  0.0 100.8 jit_solution(1485983004111658575)
XLA Ops:
  0.0 1.8 %collective-permute-start.3 = (bf16[13,256,256]{2,1,0:T(8,128)(2,1)}, bf16[13,256,256]{2,1,0:T(8,128)(2,1)S(1)}, u32[]{:S(2)}, u32[]{:S(2)}) collective-permute-start(bf16[13,256,256]{2,1,0:T(8,128)(2,1)} %bitcast.3), channel_id=1, source_target_pairs={{0,1},{2,3},{4,5},{6,7},{8,9},{10,11},{12,13},{14,15},{16,17},{18,... | collective-permute-start | bytes 5111816 | tf_op jit(solution)/shard_map/ppermute | solution.py:255
  1.8 1.3 %collective-permute-start = (bf16[13,256,256]{2,1,0:T(8,128)(2,1)}, bf16[13,256,256]{2,1,0:T(8,128)(2,1)S(1)}, u32[]{:S(2)}, u32[]{:S(2)}) collective-permute-start(bf16[13,256,256]{2,1,0:T(8,128)(2,1)} %bitcast.4), channel_id=1, source_target_pairs={{1,2},{5,6},{9,10},{13,14},{17,18},{21,22},{25,26},{29,30}} | collective-permute-start | bytes 5111816 | tf_op jit(solution)/shard_map/ppermute | solution.py:254
  6.5 1.5 %shard_map.55 = (bf16[2,4,208,208]{3,2,1,0:T(8,128)(2,1)S(1)}, bf16[2,256,256]{2,1,0:T(8,128)(2,1)S(1)}, bf16[2,256,256]{2,1,0:T(8,128)(2,1)S(1)}, bf16[2,256,25...) custom-call(bf16[2,1,4,256,256]{4,3,2,1,0:T(8,128)(2,1)S(1)} %copy-done, s32[2,1,4]{2,1,0:T(1,128)S(1)} %copy-done.1, ...), custom_call_target="tpu_custom_call" | custom-call | flops 1000000 | bytes 2097152 | tf_op jit(solution)/shard_map/pallas_call | solution.py:71
  8.0 2.4 %collective-permute-start.1 = (bf16[2,256,256]{2,1,0:T(8,128)(2,1)S(1)}, bf16[2,256,256]{2,1,0:T(8,128)(2,1)S(1)}, u32[]{:S(2)}, u32[]{:S(2)}) collective-permute-start(bf16[2,256,256]{2,1,0:T(8,128)(2,1)S(1)} %get-tuple-element.43), channel_id=1, source_target_pairs={{4,0},{5,1},{6,2},{7,3},{12,8},{13,9},{14,10},{15,11},{20,16},{21,... | collective-permute-start | bytes 786440 | tf_op jit(solution)/shard_map/ppermute | solution.py:261
  10.4 1.3 %collective-permute-start.4 = (bf16[2,256,256]{2,1,0:T(8,128)(2,1)S(1)}, bf16[2,256,256]{2,1,0:T(8,128)(2,1)S(1)}, u32[]{:S(2)}, u32[]{:S(2)}) collective-permute-start(bf16[2,256,256]{2,1,0:T(8,128)(2,1)S(1)} %get-tuple-element.46), channel_id=1, source_target_pairs={{0,1},{2,3},{4,5},{6,7},{8,9},{10,11},{12,13},{14,15},{16,17},{18,... | collective-permute-start | bytes 786440 | tf_op jit(solution)/shard_map/ppermute | solution.py:260
  11.7 1.3 %collective-permute-start.2 = (bf16[2,256,256]{2,1,0:T(8,128)(2,1)S(1)}, bf16[2,256,256]{2,1,0:T(8,128)(2,1)S(1)}, u32[]{:S(2)}, u32[]{:S(2)}) collective-permute-start(bf16[2,256,256]{2,1,0:T(8,128)(2,1)S(1)} %get-tuple-element.46), channel_id=1, source_target_pairs={{1,2},{5,6},{9,10},{13,14},{17,18},{21,22},{25,26},{29,30}} | collective-permute-start | bytes 786440 | tf_op jit(solution)/shard_map/ppermute | solution.py:259
  13.1 1.4 %copy-done.3 = bf16[1,1,13,256,256]{4,3,2,1,0:T(8,128)(2,1)S(1)} copy-done((bf16[1,1,13,256,256]{4,3,2,1,0:T(8,128)(2,1)S(1)}, bf16[1,1,13,256,256]{4,3,2,1,0:T(8,128)(2,1)}, u32[]{:S(2)}) %copy-start.3) | copy-done | bytes 1703960
  14.5 3.0 %shard_map.56 = (bf16[13,256,256]{2,1,0:T(8,128)(2,1)S(1)}, bf16[13,256,256]{2,1,0:T(8,128)(2,1)S(1)}) custom-call(bf16[13,256,256]{2,1,0:T(8,128)(2,1)S(1)} %bitcast.5, bf16[2,4,208,208]{3,2,1,0:T(8,128)(2,1)S(1)} %get-tuple-element.38.mixer_ref, bf16[2,256,256]{2,1,0:T(8,128)(2,1)S(1)} %get-tuple-element.39.block_ref), custom_call_target="tpu_custom_call" | custom-call | flops 2617245696 | bytes 3145728 | tf_op jit(solution)/shard_map/pallas_call | solution.py:187
  19.3 5.9 %collective-permute-done.near_ref = bf16[13,256,256]{2,1,0:T(8,128)(2,1)S(1)} collective-permute-done((bf16[13,256,256]{2,1,0:T(8,128)(2,1)}, bf16[13,256,256]{2,1,0:T(8,128)(2,1)S(1)}, u32[]{:S(2)}, u32[]{:S(2)}) %collective-permute-start) | collective-permute-done | bytes 1703968 | tf_op jit(solution)/shard_map/ppermute | solution.py:254
  26.5 1.5 %collective-permute-done.2.near_block_ref = bf16[2,256,256]{2,1,0:T(8,128)(2,1)S(1)} collective-permute-done((bf16[2,256,256]{2,1,0:T(8,128)(2,1)S(1)}, bf16[2,256,256]{2,1,0:T(8,128)(2,1)S(1)}, u32[]{:S(2)}, u32[]{:S(2)}) %collective-permute-start.2) | collective-permute-done | bytes 262176 | tf_op jit(solution)/shard_map/ppermute | solution.py:259
  28.0 9.3 %shard_map.59 = (bf16[3,13,256,256]{3,2,1,0:T(8,128)(2,1)S(1)}, bf16[8,256,256]{2,1,0:T(8,128)(2,1)S(1)}, bf16[8,256,256]{2,1,0:T(8,128)(2,1)S(1)}, bf16[10,256,...) custom-call(bf16[13,256,256]{2,1,0:T(8,128)(2,1)S(1)} %collective-pe, ...), custom_call_target="tpu_custom_call", output_to_operand_aliasing={{0}: (7, {}), {1}: (8, {}), {2}: (9, {})} | custom-call | flops 65431142400 | bytes 31457280 | tf_op jit(solution)/shard_map/pallas_call | solution.py:187
  37.3 1.4 %collective-permute-start.8 = (bf16[10,256,256]{2,1,0:T(8,128)(2,1)S(1)}, bf16[10,256,256]{2,1,0:T(8,128)(2,1)S(1)}, u32[]{:S(2)}, u32[]{:S(2)}) collective-permute-start(bf16[10,256,256]{2,1,0:T(8,128)(2,1)S(1)} %get-tuple-element.54), channel_id=1, source_target_pairs={{2,3},{6,7},{10,11},{14,15},{18,19},{22,23},{26,27},{30,31}} | collective-permute-start | bytes 3932168 | tf_op jit(solution)/shard_map/ppermute | solution.py:286
  38.7 1.3 %collective-permute-start.10 = (bf16[8,256,256]{2,1,0:T(8,128)(2,1)S(1)}, bf16[8,256,256]{2,1,0:T(8,128)(2,1)S(1)}, u32[]{:S(2)}, u32[]{:S(2)}) collective-permute-start(bf16[8,256,256]{2,1,0:T(8,128)(2,1)S(1)} %get-tuple-element.57), channel_id=1, source_target_pairs={{0,1},{1,2},{4,5},{5,6},{8,9},{9,10},{12,13},{13,14},{16,17},{17,1... | collective-permute-start | bytes 3145736 | tf_op jit(solution)/shard_map/ppermute | solution.py:285
  40.0 1.4 %collective-permute-start.11 = (bf16[8,256,256]{2,1,0:T(8,128)(2,1)S(1)}, bf16[8,256,256]{2,1,0:T(8,128)(2,1)S(1)}, u32[]{:S(2)}, u32[]{:S(2)}) collective-permute-start(bf16[8,256,256]{2,1,0:T(8,128)(2,1)S(1)} %get-tuple-element.59), channel_id=1, source_target_pairs={{2,3},{6,7},{10,11},{14,15},{18,19},{22,23},{26,27},{30,31}} | collective-permute-start | bytes 3145736 | tf_op jit(solution)/shard_map/ppermute | solution.py:286
  41.3 6.8 %collective-permute-done.5.refs_0_ = bf16[10,256,256]{2,1,0:T(8,128)(2,1)S(1)} collective-permute-done((bf16[10,256,256]{2,1,0:T(8,128)(2,1)S(1)}, bf16[10,256,256]{2,1,0:T(8,128)(2,1)S(1)}, u32[]{:S(2)}, u32[]{:S(2)}) %collective-permute-start.5) | collective-permute-done | bytes 1310752 | tf_op jit(solution)/shard_map/ppermute | solution.py:285
  48.2 1.4 %shard_map.60 = (bf16[5,256,256]{2,1,0:T(8,128)(2,1)S(1)}, bf16[5,256,256]{2,1,0:T(8,128)(2,1)S(1)}) custom-call(bf16[3,13,256,256]{3,2,1,0:T(8,128)(2,1)S(1)} %get-tuple-element.50.remain_ref, bf16[4,256,256]{2,1,0:T(8,128)(2,1)S(1)} %get-tuple-element.42.last_ref, bf16[2,256,256]{2,1,0:T(8,128)(2,1)S(1)} %collective-permute-done.1.column_ref, ...), custom_call_target="tpu_custom_call" | custom-call | tf_op jit(solution)/shard_map/pallas_call | solution.py:187
  52.1 1.4 %collective-permute-start.15 = (bf16[8,256,256]{2,1,0:T(8,128)(2,1)S(1)}, bf16[8,256,256]{2,1,0:T(8,128)(2,1)S(1)}, u32[]{:S(2)}, u32[]{:S(2)}) collective-permute-start(bf16[8,256,256]{2,1,0:T(8,128)(2,1)S(1)} %get-tuple-element.65), channel_id=1, source_target_pairs={{2,3},{6,7},{10,11},{14,15},{18,19},{22,23},{26,27},{30,31}} | collective-permute-start | bytes 3145736 | tf_op jit(solution)/shard_map/ppermute | solution.py:286
  53.5 5.9 %collective-permute-done.10.refs_0_ = bf16[8,256,256]{2,1,0:T(8,128)(2,1)S(1)} collective-permute-done((bf16[8,256,256]{2,1,0:T(8,128)(2,1)S(1)}, bf16[8,256,256]{2,1,0:T(8,128)(2,1)S(1)}, u32[]{:S(2)}, u32[]{:S(2)}) %collective-permute-start.10) | collective-permute-done | bytes 1048608 | tf_op jit(solution)/shard_map/ppermute | solution.py:285
  63.1 6.0 %collective-permute-done.9 = bf16[5,256,256]{2,1,0:T(8,128)(2,1)S(1)} collective-permute-done((bf16[5,256,256]{2,1,0:T(8,128)(2,1)S(1)}, bf16[5,256,256]{2,1,0:T(8,128)(2,1)S(1)}, u32[]{:S(2)}, u32[]{:S(2)}) %collective-permute-start.9) | collective-permute-done | bytes 655392 | tf_op jit(solution)/shard_map/ppermute | solution.py:247
  73.1 5.3 %collective-permute-done.13 = bf16[4,256,256]{2,1,0:T(8,128)(2,1)S(1)} collective-permute-done((bf16[4,256,256]{2,1,0:T(8,128)(2,1)S(1)}, bf16[4,256,256]{2,1,0:T(8,128)(2,1)S(1)}, u32[]{:S(2)}, u32[]{:S(2)}) %collective-permute-start.13) | collective-permute-done | bytes 524320 | tf_op jit(solution)/shard_map/ppermute | solution.py:247
  79.8 4.2 %collective-permute-done.17 = bf16[4,256,256]{2,1,0:T(8,128)(2,1)S(1)} collective-permute-done((bf16[4,256,256]{2,1,0:T(8,128)(2,1)S(1)}, bf16[4,256,256]{2,1,0:T(8,128)(2,1)S(1)}, u32[]{:S(2)}, u32[]{:S(2)}) %collective-permute-start.17) | collective-permute-done | bytes 524320 | tf_op jit(solution)/shard_map/ppermute | solution.py:247
  85.4 8.3 %collective-permute-done.16 = bf16[4,256,256]{2,1,0:T(8,128)(2,1)S(1)} collective-permute-done((bf16[4,256,256]{2,1,0:T(8,128)(2,1)S(1)}, bf16[4,256,256]{2,1,0:T(8,128)(2,1)S(1)}, u32[]{:S(2)}, u32[]{:S(2)}) %collective-permute-start.16) | collective-permute-done | bytes 524320 | tf_op jit(solution)/shard_map/ppermute | solution.py:247
  93.7 5.6 %collective-permute-done.18 = bf16[4,256,256]{2,1,0:T(8,128)(2,1)S(1)} collective-permute-done((bf16[4,256,256]{2,1,0:T(8,128)(2,1)S(1)}, bf16[4,256,256]{2,1,0:T(8,128)(2,1)S(1)}, u32[]{:S(2)}, u32[]{:S(2)}) %collective-permute-start.18) | collective-permute-done | bytes 524320 | tf_op jit(solution)/shard_map/ppermute | solution.py:247
  99.3 1.5 %fusion = bf16[1,1,13,256,256]{4,3,2,1,0:T(8,128)(2,1)} fusion(bf16[4,256,256]{2,1,0:T(8,128)(2,1)S(1)} %collective-permute-done.18, bf16[4,256,256]{2,1,0:T(8,128)(2,1)S(1)} %collective-permute-done.16, bf16[5,256,256]{2,1,0:T(8,128)(2,1)S(1)} %collective-permute-done.12, bf16[13,256,256]{2,1,0:T(8,128)(2,1)S(1)} %collective-permute-done.7, ...), kind=kLoop, calls=%fused_computation.2 | loop fusion | flops 3407872 | bytes 6815744 | tf_op jit(solution)/shard_map/broadcast_in_dim | solution.py:305
  (38 shorter events, 19.5 us)
Async XLA Ops:
  0.0 19.1 %collective-permute-start.3 = (bf16[13,256,256]{2,1,0:T(8,128)(2,1)}, bf16[13,256,256]{2,1,0:T(8,128)(2,1)S(1)}, u32[]{:S(2)}, u32[]{:S(2)}) collective-permute-start(bf16[13,256,256]{2,1,0:T(8,128)(2,1)} %bitcast.3), channel_id=1, source_target_pairs={{0,1},{2,3},{4,5},{6,7},{8,9},{10,11},{12,13},{14,15},{16,17},{18,... | collective-permute-start | bytes 5111816 | tf_op jit(solution)/shard_map/ppermute | solution.py:255
  1.8 23.4 %collective-permute-start = (bf16[13,256,256]{2,1,0:T(8,128)(2,1)}, bf16[13,256,256]{2,1,0:T(8,128)(2,1)S(1)}, u32[]{:S(2)}, u32[]{:S(2)}) collective-permute-start(bf16[13,256,256]{2,1,0:T(8,128)(2,1)} %bitcast.4), channel_id=1, source_target_pairs={{1,2},{5,6},{9,10},{13,14},{17,18},{21,22},{25,26},{29,30}} | collective-permute-start | bytes 5111816 | tf_op jit(solution)/shard_map/ppermute | solution.py:254
  3.9 1.2 %copy-start = (bf16[2,1,4,256,256]{4,3,2,1,0:T(8,128)(2,1)S(1)}, bf16[2,1,4,256,256]{4,3,2,1,0:T(8,128)(2,1)}, u32[]{:S(2)}) copy-start(bf16[2,1,4,256,256]{4,3,2,1,0:T(8,128)(2,1)} %site_ref.1) | copy-start | bytes 3145732
  5.1 0.7 copy-start.1
  5.8 0.7 copy-start.2
  8.0 9.5 %collective-permute-start.1 = (bf16[2,256,256]{2,1,0:T(8,128)(2,1)S(1)}, bf16[2,256,256]{2,1,0:T(8,128)(2,1)S(1)}, u32[]{:S(2)}, u32[]{:S(2)}) collective-permute-start(bf16[2,256,256]{2,1,0:T(8,128)(2,1)S(1)} %get-tuple-element.43), channel_id=1, source_target_pairs={{4,0},{5,1},{6,2},{7,3},{12,8},{13,9},{14,10},{15,11},{20,16},{21,... | collective-permute-start | bytes 786440 | tf_op jit(solution)/shard_map/ppermute | solution.py:261
  10.4 7.9 %collective-permute-start.4 = (bf16[2,256,256]{2,1,0:T(8,128)(2,1)S(1)}, bf16[2,256,256]{2,1,0:T(8,128)(2,1)S(1)}, u32[]{:S(2)}, u32[]{:S(2)}) collective-permute-start(bf16[2,256,256]{2,1,0:T(8,128)(2,1)S(1)} %get-tuple-element.46), channel_id=1, source_target_pairs={{0,1},{2,3},{4,5},{6,7},{8,9},{10,11},{12,13},{14,15},{16,17},{18,... | collective-permute-start | bytes 786440 | tf_op jit(solution)/shard_map/ppermute | solution.py:260
  11.7 16.3 %collective-permute-start.2 = (bf16[2,256,256]{2,1,0:T(8,128)(2,1)S(1)}, bf16[2,256,256]{2,1,0:T(8,128)(2,1)S(1)}, u32[]{:S(2)}, u32[]{:S(2)}) collective-permute-start(bf16[2,256,256]{2,1,0:T(8,128)(2,1)S(1)} %get-tuple-element.46), channel_id=1, source_target_pairs={{1,2},{5,6},{9,10},{13,14},{17,18},{21,22},{25,26},{29,30}} | collective-permute-start | bytes 786440 | tf_op jit(solution)/shard_map/ppermute | solution.py:259
  13.0 1.5 %copy-start.3 = (bf16[1,1,13,256,256]{4,3,2,1,0:T(8,128)(2,1)S(1)}, bf16[1,1,13,256,256]{4,3,2,1,0:T(8,128)(2,1)}, u32[]{:S(2)}) copy-start(bf16[1,1,13,256,256]{4,3,2,1,0:T(8,128)(2,1)} %param.5) | copy-start | bytes 5111812
  17.6 22.4 %collective-permute-start.6 = (bf16[13,256,256]{2,1,0:T(8,128)(2,1)S(1)}, bf16[13,256,256]{2,1,0:T(8,128)(2,1)S(1)}, u32[]{:S(2)}, u32[]{:S(2)}) collective-permute-start(bf16[13,256,256]{2,1,0:T(8,128)(2,1)S(1)} %get-tuple-element.52), channel_id=1, source_target_pairs={{0,4},{8,12},{16,20},{24,28}} | collective-permute-start | bytes 5111816 | tf_op jit(solution)/shard_map/ppermute | solution.py:247
  18.3 23.0 %collective-permute-start.7 = (bf16[13,256,256]{2,1,0:T(8,128)(2,1)S(1)}, bf16[13,256,256]{2,1,0:T(8,128)(2,1)S(1)}, u32[]{:S(2)}, u32[]{:S(2)}) collective-permute-start(bf16[13,256,256]{2,1,0:T(8,128)(2,1)S(1)} %get-tuple-element.44), channel_id=1, source_target_pairs={{0,8},{8,16},{16,24}} | collective-permute-start | bytes 5111816 | tf_op jit(solution)/shard_map/ppermute | solution.py:247
  25.2 23.0 %collective-permute-start.5 = (bf16[10,256,256]{2,1,0:T(8,128)(2,1)S(1)}, bf16[10,256,256]{2,1,0:T(8,128)(2,1)S(1)}, u32[]{:S(2)}, u32[]{:S(2)}) collective-permute-start(bf16[10,256,256]{2,1,0:T(8,128)(2,1)S(1)} %get-tuple-element.51), channel_id=1, source_target_pairs={{0,1},{1,2},{4,5},{5,6},{8,9},{9,10},{12,13},{13,14},{16,17},{17,1... | collective-permute-start | bytes 3932168 | tf_op jit(solution)/shard_map/ppermute | solution.py:285
  37.3 10.9 %collective-permute-start.8 = (bf16[10,256,256]{2,1,0:T(8,128)(2,1)S(1)}, bf16[10,256,256]{2,1,0:T(8,128)(2,1)S(1)}, u32[]{:S(2)}, u32[]{:S(2)}) collective-permute-start(bf16[10,256,256]{2,1,0:T(8,128)(2,1)S(1)} %get-tuple-element.54), channel_id=1, source_target_pairs={{2,3},{6,7},{10,11},{14,15},{18,19},{22,23},{26,27},{30,31}} | collective-permute-start | bytes 3932168 | tf_op jit(solution)/shard_map/ppermute | solution.py:286
  38.7 20.7 %collective-permute-start.10 = (bf16[8,256,256]{2,1,0:T(8,128)(2,1)S(1)}, bf16[8,256,256]{2,1,0:T(8,128)(2,1)S(1)}, u32[]{:S(2)}, u32[]{:S(2)}) collective-permute-start(bf16[8,256,256]{2,1,0:T(8,128)(2,1)S(1)} %get-tuple-element.57), channel_id=1, source_target_pairs={{0,1},{1,2},{4,5},{5,6},{8,9},{9,10},{12,13},{13,14},{16,17},{17,1... | collective-permute-start | bytes 3145736 | tf_op jit(solution)/shard_map/ppermute | solution.py:285
  40.0 19.4 %collective-permute-start.11 = (bf16[8,256,256]{2,1,0:T(8,128)(2,1)S(1)}, bf16[8,256,256]{2,1,0:T(8,128)(2,1)S(1)}, u32[]{:S(2)}, u32[]{:S(2)}) collective-permute-start(bf16[8,256,256]{2,1,0:T(8,128)(2,1)S(1)} %get-tuple-element.59), channel_id=1, source_target_pairs={{2,3},{6,7},{10,11},{14,15},{18,19},{22,23},{26,27},{30,31}} | collective-permute-start | bytes 3145736 | tf_op jit(solution)/shard_map/ppermute | solution.py:286
  49.5 19.6 %collective-permute-start.9 = (bf16[5,256,256]{2,1,0:T(8,128)(2,1)S(1)}, bf16[5,256,256]{2,1,0:T(8,128)(2,1)S(1)}, u32[]{:S(2)}, u32[]{:S(2)}) collective-permute-start(bf16[5,256,256]{2,1,0:T(8,128)(2,1)S(1)} %get-tuple-element.56), channel_id=1, source_target_pairs={{1,5},{2,6},{3,7},{9,13},{10,14},{11,15},{17,21},{18,22},{19,23},{... | collective-permute-start | bytes 1966088 | tf_op jit(solution)/shard_map/ppermute | solution.py:247
  50.8 19.8 %collective-permute-start.14 = (bf16[8,256,256]{2,1,0:T(8,128)(2,1)S(1)}, bf16[8,256,256]{2,1,0:T(8,128)(2,1)S(1)}, u32[]{:S(2)}, u32[]{:S(2)}) collective-permute-start(bf16[8,256,256]{2,1,0:T(8,128)(2,1)S(1)} %get-tuple-element.63), channel_id=1, source_target_pairs={{0,1},{1,2},{4,5},{5,6},{8,9},{9,10},{12,13},{13,14},{16,17},{17,1... | collective-permute-start | bytes 3145736 | tf_op jit(solution)/shard_map/ppermute | solution.py:285
  52.1 18.5 %collective-permute-start.15 = (bf16[8,256,256]{2,1,0:T(8,128)(2,1)S(1)}, bf16[8,256,256]{2,1,0:T(8,128)(2,1)S(1)}, u32[]{:S(2)}, u32[]{:S(2)}) collective-permute-start(bf16[8,256,256]{2,1,0:T(8,128)(2,1)S(1)} %get-tuple-element.65), channel_id=1, source_target_pairs={{2,3},{6,7},{10,11},{14,15},{18,19},{22,23},{26,27},{30,31}} | collective-permute-start | bytes 3145736 | tf_op jit(solution)/shard_map/ppermute | solution.py:286
  60.5 17.8 %collective-permute-start.13 = (bf16[4,256,256]{2,1,0:T(8,128)(2,1)S(1)}, bf16[4,256,256]{2,1,0:T(8,128)(2,1)S(1)}, u32[]{:S(2)}, u32[]{:S(2)}) collective-permute-start(bf16[4,256,256]{2,1,0:T(8,128)(2,1)S(1)} %get-tuple-element.60), channel_id=1, source_target_pairs={{1,5},{2,6},{3,7},{9,13},{10,14},{11,15},{17,21},{18,22},{19,23},{... | collective-permute-start | bytes 1572872 | tf_op jit(solution)/shard_map/ppermute | solution.py:247
  62.3 31.4 %collective-permute-start.19 = (bf16[13,256,256]{2,1,0:T(8,128)(2,1)S(1)}, bf16[13,256,256]{2,1,0:T(8,128)(2,1)S(1)}, u32[]{:S(2)}, u32[]{:S(2)}) collective-permute-start(bf16[13,256,256]{2,1,0:T(8,128)(2,1)S(1)} %add_convert_fusion), channel_id=1, source_target_pairs={{4,12},{12,20},{20,28}} | collective-permute-start | bytes 5111816 | tf_op jit(solution)/shard_map/ppermute | solution.py:247
  69.2 14.7 %collective-permute-start.12 = (bf16[5,256,256]{2,1,0:T(8,128)(2,1)S(1)}, bf16[5,256,256]{2,1,0:T(8,128)(2,1)S(1)}, u32[]{:S(2)}, u32[]{:S(2)}) collective-permute-start(bf16[5,256,256]{2,1,0:T(8,128)(2,1)S(1)} %add_convert_fusion.1), channel_id=1, source_target_pairs={{1,9},{2,10},{3,11},{5,13},{6,14},{7,15},{9,17},{10,18},{11,19},{1... | collective-permute-start | bytes 1966088 | tf_op jit(solution)/shard_map/ppermute | solution.py:247
  71.8 12.2 %collective-permute-start.17 = (bf16[4,256,256]{2,1,0:T(8,128)(2,1)S(1)}, bf16[4,256,256]{2,1,0:T(8,128)(2,1)S(1)}, u32[]{:S(2)}, u32[]{:S(2)}) collective-permute-start(bf16[4,256,256]{2,1,0:T(8,128)(2,1)S(1)} %get-tuple-element.66), channel_id=1, source_target_pairs={{1,5},{2,6},{3,7},{9,13},{10,14},{11,15},{17,21},{18,22},{19,23},{... | collective-permute-start | bytes 1572872 | tf_op jit(solution)/shard_map/ppermute | solution.py:247
  78.5 15.3 %collective-permute-start.16 = (bf16[4,256,256]{2,1,0:T(8,128)(2,1)S(1)}, bf16[4,256,256]{2,1,0:T(8,128)(2,1)S(1)}, u32[]{:S(2)}, u32[]{:S(2)}) collective-permute-start(bf16[4,256,256]{2,1,0:T(8,128)(2,1)S(1)} %add_convert_fusion.3), channel_id=1, source_target_pairs={{1,9},{2,10},{3,11},{5,13},{6,14},{7,15},{9,17},{10,18},{11,19},{1... | collective-permute-start | bytes 1572872 | tf_op jit(solution)/shard_map/ppermute | solution.py:247
  84.1 15.3 %collective-permute-start.18 = (bf16[4,256,256]{2,1,0:T(8,128)(2,1)S(1)}, bf16[4,256,256]{2,1,0:T(8,128)(2,1)S(1)}, u32[]{:S(2)}, u32[]{:S(2)}) collective-permute-start(bf16[4,256,256]{2,1,0:T(8,128)(2,1)S(1)} %add_convert_fusion.2), channel_id=1, source_target_pairs={{1,9},{2,10},{3,11},{5,13},{6,14},{7,15},{9,17},{10,18},{11,19},{1... | collective-permute-start | bytes 1572872 | tf_op jit(solution)/shard_map/ppermute | solution.py:247
